TPU v7x, 32 devices: a whole 2x2x4 slice. The times are simulated.
32 devices in a mesh: sx: 2 (over core), sy: 4 (over z), gz: 4 (over y, x).
Axes of the slice: x: 2, y: 2, z: 4, core: 2. Of those that a mesh axis runs over, the one named last changes fastest.
Arguments:
- field: float32 [8, 512, 4096], P('gz', 'sy', 'sx'), may hold values from 0.1 to 2
- bins: int32 [8, 512, 4096], P('gz', 'sy', 'sx'), may hold values from 0 to 127
- table: bfloat16 [4, 128], replicated, may hold values from 0.02 to 1, as said below
- march_order: int32 [512], P('sy'), may hold values from 0 to 1
Outputs:
- image: float32 [4, 512, 4096], P(None, ('sy', 'gz'), 'sx')
Inputs may be any that keep to these rules, and one draw needn't show every extreme that they name: `table`: rows 0 to 2 lie between 0.05 and 1, row 3 between 0.02 and about 0.12.
All inputs are finite; a program needn't handle non-finite values.
Results may differ from a plain program's by a relative error of at most 0.0003.
Values sent between devices are 32-bit elements; how exact they have to be, the bound alone decides.
No kernel may reach another device: no remote copies, remote signals or barrier semaphores. Data moves between devices by JAX's collectives and lax.ppermute only.
A program may use at most 128 MiB of HBM per device.

v0:
```python
import jax
import jax.numpy as jnp
from jax import lax
from jax.sharding import PartitionSpec as P

light_x = 0.36
light_y = 0.48
light_z = 0.8


def extended(block, sides, width):
    for axis, dim in sides:
        count = lax.axis_size(axis)
        forward = [(i, i + 1) for i in range(count - 1)]
        backward = [(target, source) for source, target in forward]
        low = lax.ppermute(
            lax.slice_in_dim(block, block.shape[dim] - width, None, axis=dim), axis, forward
        )
        high = lax.ppermute(lax.slice_in_dim(block, 0, width, axis=dim), axis, backward)
        block = jnp.concatenate([low, block, high], axis=dim)
    return block


def partner(x, axis, distance):
    return lax.ppermute(x, axis, [(i, i ^ 1 << distance) for i in range(lax.axis_size(axis))])


def classify(padded, bins, table):
    depth, height, width = bins.shape
    centre = padded[1:-1, 1:-1, 1:-1]
    grad_x = 0.5 * (padded[1:-1, 1:-1, 2:] - padded[1:-1, 1:-1, :-2])
    grad_y = 0.5 * (padded[1:-1, 2:, 1:-1] - padded[1:-1, :-2, 1:-1])
    grad_z = 0.5 * (padded[2:, 1:-1, 1:-1] - padded[:-2, 1:-1, 1:-1])
    facing = light_x * grad_x + light_y * grad_y + light_z * grad_z
    length = jnp.sqrt(grad_x * grad_x + grad_y * grad_y + grad_z * grad_z + 1.0)
    shading = 0.3 + 0.7 * jnp.abs(facing) / length
    labels = jnp.arange(table.shape[1], dtype=jnp.int32)
    blocked = bins.reshape(-1, 16, width)

    def lookup(block_bins):
        onehot = (block_bins[None] == labels[:, None, None]).astype(jnp.bfloat16)
        return jnp.einsum("kn,nrw->krw", table, onehot, preferred_element_type=jnp.float32)

    looked = lax.map(lookup, blocked)
    looked = jnp.moveaxis(looked, 1, 0).reshape(4, depth, height, width)
    opacity = 1.0 - jnp.exp(-looked[3] * centre)
    emitted = looked[:3] * (shading * opacity)[None]
    return (emitted, opacity)


def over(front, behind):
    colour = front[:3] + front[3:] * behind[:3]
    trans = front[3:] * behind[3:]
    return jnp.concatenate([colour, trans], 0)


def shards(field, bins, table, march_order):
    depth, height, width = field.shape
    backward = (march_order == 1)[:, None]
    padded = extended(field, (("sx", 2), ("sy", 1), ("gz", 0)), 1)
    emitted, opacity = classify(padded, bins, table)
    colour = jnp.zeros((3, height, width), jnp.float32)
    trans = jnp.ones((height, width), jnp.float32)
    for slice_step in range(depth):
        other_step = depth - 1 - slice_step
        here_colour = jnp.where(backward[None], emitted[:, other_step], emitted[:, slice_step])
        here_alpha = jnp.where(backward, opacity[other_step], opacity[slice_step])
        colour = colour + trans[None] * here_colour
        trans = trans * (1.0 - here_alpha)
    partial_value = jnp.concatenate([colour, trans[None]], 0)
    count = lax.axis_size("gz")
    piece_rows = height // count
    rank = lax.axis_index("gz")
    levels = count.bit_length() - 1
    current = partial_value
    flip_now = march_order
    for bit_level in range(levels):
        halves = current.reshape(4, -1, 2, piece_rows, width)
        flip_halves = flip_now.reshape(-1, 2, piece_rows)
        my_bit = rank >> bit_level & 1
        lower = halves[:, :, 0]
        upper = halves[:, :, 1]
        kept = jnp.where(my_bit == 0, lower, upper)
        sent = jnp.where(my_bit == 0, upper, lower)
        flip_kept = jnp.where(my_bit == 0, flip_halves[:, 0], flip_halves[:, 1])
        arrived = partner(sent, "gz", bit_level)
        in_front = (my_bit == flip_kept)[None, :, :, None]
        front = jnp.where(in_front, kept, arrived)
        behind = jnp.where(in_front, arrived, kept)
        current = over(front, behind).reshape(4, -1, width)
        flip_now = flip_kept.reshape(-1)
    return jnp.concatenate([current[:3], 1.0 - current[3:]], 0)


def solution(mesh):
    placed = (P("gz", "sy", "sx"), P("gz", "sy", "sx"), P(), P("sy"))
    return jax.shard_map(
        shards, mesh=mesh, in_specs=placed, out_specs=P(None, ("sy", "gz"), "sx"), check_vma=False
    )
```

profile of v0, /device:TPU:0, one launch (start us, length us, event | category | flops | bytes accessed | tf_op | source)
XLA Modules:
  0.0 198.6 jit_solution(11094140502153494340)
XLA Ops:
  2.4 3.0 %collective-permute-start.1 = (f32[2,128,1]{2,1,0:T(8,128)S(1)}, f32[2,128,1]{2,1,0:T(8,128)S(1)}, u32[]{:S(2)}, u32[]{:S(2)}) collective-permute-start(f32[2,128,1]{2,1,0:T(8,128)S(1)} %get-tuple-element.70), channel_id=1, source_target_pairs={{0,16},{1,17},{2,18},{3,19},{4,20},{5,21},{6,22},{7,23},{8,24},{9,... | collective-permute-start | bytes 3080 | tf_op jit(solution)/shard_map/ppermute | solution.py:16
  6.4 3.0 %concatenate.40 = f32[2,128,2050]{2,1,0:T(8,128)S(1)} concatenate(f32[2,128,1]{2,1,0:T(8,128)S(1)} %collective-permute-done.1, f32[2,128,2048]{2,1,0:T(8,128)} %param.6, f32[2,128,1]{2,1,0:T(8,128)S(1)} %collective-permute-done), dimensions={2} | concatenate | bytes 4198400 | tf_op jit(solution)/shard_map/concatenate | solution.py:20
  10.7 5.6 %collective-permute-start.3 = (f32[2,1,2050]{2,1,0:T(1,128)S(1)}, f32[2,1,2050]{2,1,0:T(1,128)S(1)}, u32[]{:S(2)}, u32[]{:S(2)}) collective-permute-start(f32[2,1,2050]{2,1,0:T(1,128)S(1)} %get-tuple-element.65), channel_id=1, source_target_pairs={{0,4},{4,8},{8,12},{1,5},{5,9},{9,13},{2,6},{6,10},{10,14},{3,7},{... | collective-permute-start | bytes 49208 | tf_op jit(solution)/shard_map/ppermute | solution.py:16
  22.8 5.5 %collective-permute-start.5 = (f32[1,130,2050]{2,0,1:T(1,128)}, f32[1,130,2050]{2,0,1:T(1,128)}, u32[]{:S(2)}, u32[]{:S(2)}) collective-permute-start(f32[1,130,2050]{2,0,1:T(1,128)} %copy.29), channel_id=1, source_target_pairs={{0,1},{1,2},{2,3},{4,5},{5,6},{6,7},{8,9},{9,10},{10,11},{12,13},{... | collective-permute-start | bytes 3198008 | tf_op jit(solution)/shard_map/ppermute | solution.py:16
  28.3 73.0 %while.11 = (s32[]{:T(128)}, f32[16,4,16,2048]{3,2,0,1:T(8,128)}, s32[16,16,2048]{2,1,0:T(8,128)}, bf16[4,128]{1,0:T(4,128)(2,1)S(1)}, s32[]{:T(128)}) while((s32[]{:T(128)}, f32[16,4,16,2048]{3,2,0,1:T(8,128)}, s32[16,16,2048]{2,1,0:T(8,128)}, bf16[4,128]{1,0:T(4,128)(2,1)S(1)}, s32[]{:T(128)}) %tuple.36), condition=%wide.region_1.2_spmd.clone, body=%wide.region_0.1_spmd.clone.sunk | while | flops 37748736 | bytes 1967681 | solution.py:44
  29.3 2.5 %fusion.24 = f32[1,4,16,2048]{3,1,2,0:T(4,128)S(1)} fusion(s32[16,2048]{1,0:T(8,128)S(1)} %dynamic-slice_bitcast_fusion.2, bf16[4,128]{1,0:T(4,128)(2,1)S(1)} %get-tuple-element.111), kind=kOutput, calls=%fused_computation.4.clone.1 | convolution fusion | flops 37748736 | bytes 656384 | tf_op jit(solution)/shard_map/while/body/eval_jaxpr/kn,nrw->krw/dot_general | solution.py:42
  33.8 2.5 %fusion.24 = f32[1,4,16,2048]{3,1,2,0:T(4,128)S(1)} fusion(s32[16,2048]{1,0:T(8,128)S(1)} %dynamic-slice_bitcast_fusion.2, bf16[4,128]{1,0:T(4,128)(2,1)S(1)} %get-tuple-element.111), kind=kOutput, calls=%fused_computation.4.clone.1 | convolution fusion | flops 37748736 | bytes 656384 | tf_op jit(solution)/shard_map/while/body/eval_jaxpr/kn,nrw->krw/dot_general | solution.py:42
  38.4 2.5 %fusion.24 = f32[1,4,16,2048]{3,1,2,0:T(4,128)S(1)} fusion(s32[16,2048]{1,0:T(8,128)S(1)} %dynamic-slice_bitcast_fusion.2, bf16[4,128]{1,0:T(4,128)(2,1)S(1)} %get-tuple-element.111), kind=kOutput, calls=%fused_computation.4.clone.1 | convolution fusion | flops 37748736 | bytes 656384 | tf_op jit(solution)/shard_map/while/body/eval_jaxpr/kn,nrw->krw/dot_general | solution.py:42
  42.9 2.5 %fusion.24 = f32[1,4,16,2048]{3,1,2,0:T(4,128)S(1)} fusion(s32[16,2048]{1,0:T(8,128)S(1)} %dynamic-slice_bitcast_fusion.2, bf16[4,128]{1,0:T(4,128)(2,1)S(1)} %get-tuple-element.111), kind=kOutput, calls=%fused_computation.4.clone.1 | convolution fusion | flops 37748736 | bytes 656384 | tf_op jit(solution)/shard_map/while/body/eval_jaxpr/kn,nrw->krw/dot_general | solution.py:42
  47.5 2.5 %fusion.24 = f32[1,4,16,2048]{3,1,2,0:T(4,128)S(1)} fusion(s32[16,2048]{1,0:T(8,128)S(1)} %dynamic-slice_bitcast_fusion.2, bf16[4,128]{1,0:T(4,128)(2,1)S(1)} %get-tuple-element.111), kind=kOutput, calls=%fused_computation.4.clone.1 | convolution fusion | flops 37748736 | bytes 656384 | tf_op jit(solution)/shard_map/while/body/eval_jaxpr/kn,nrw->krw/dot_general | solution.py:42
  52.1 2.5 %fusion.24 = f32[1,4,16,2048]{3,1,2,0:T(4,128)S(1)} fusion(s32[16,2048]{1,0:T(8,128)S(1)} %dynamic-slice_bitcast_fusion.2, bf16[4,128]{1,0:T(4,128)(2,1)S(1)} %get-tuple-element.111), kind=kOutput, calls=%fused_computation.4.clone.1 | convolution fusion | flops 37748736 | bytes 656384 | tf_op jit(solution)/shard_map/while/body/eval_jaxpr/kn,nrw->krw/dot_general | solution.py:42
  56.6 2.5 %fusion.24 = f32[1,4,16,2048]{3,1,2,0:T(4,128)S(1)} fusion(s32[16,2048]{1,0:T(8,128)S(1)} %dynamic-slice_bitcast_fusion.2, bf16[4,128]{1,0:T(4,128)(2,1)S(1)} %get-tuple-element.111), kind=kOutput, calls=%fused_computation.4.clone.1 | convolution fusion | flops 37748736 | bytes 656384 | tf_op jit(solution)/shard_map/while/body/eval_jaxpr/kn,nrw->krw/dot_general | solution.py:42
  61.2 2.5 %fusion.24 = f32[1,4,16,2048]{3,1,2,0:T(4,128)S(1)} fusion(s32[16,2048]{1,0:T(8,128)S(1)} %dynamic-slice_bitcast_fusion.2, bf16[4,128]{1,0:T(4,128)(2,1)S(1)} %get-tuple-element.111), kind=kOutput, calls=%fused_computation.4.clone.1 | convolution fusion | flops 37748736 | bytes 656384 | tf_op jit(solution)/shard_map/while/body/eval_jaxpr/kn,nrw->krw/dot_general | solution.py:42
  65.7 2.5 %fusion.24 = f32[1,4,16,2048]{3,1,2,0:T(4,128)S(1)} fusion(s32[16,2048]{1,0:T(8,128)S(1)} %dynamic-slice_bitcast_fusion.2, bf16[4,128]{1,0:T(4,128)(2,1)S(1)} %get-tuple-element.111), kind=kOutput, calls=%fused_computation.4.clone.1 | convolution fusion | flops 37748736 | bytes 656384 | tf_op jit(solution)/shard_map/while/body/eval_jaxpr/kn,nrw->krw/dot_general | solution.py:42
  70.3 2.5 %fusion.24 = f32[1,4,16,2048]{3,1,2,0:T(4,128)S(1)} fusion(s32[16,2048]{1,0:T(8,128)S(1)} %dynamic-slice_bitcast_fusion.2, bf16[4,128]{1,0:T(4,128)(2,1)S(1)} %get-tuple-element.111), kind=kOutput, calls=%fused_computation.4.clone.1 | convolution fusion | flops 37748736 | bytes 656384 | tf_op jit(solution)/shard_map/while/body/eval_jaxpr/kn,nrw->krw/dot_general | solution.py:42
  79.4 2.5 %fusion.24 = f32[1,4,16,2048]{3,1,2,0:T(4,128)S(1)} fusion(s32[16,2048]{1,0:T(8,128)S(1)} %dynamic-slice_bitcast_fusion.2, bf16[4,128]{1,0:T(4,128)(2,1)S(1)} %get-tuple-element.111), kind=kOutput, calls=%fused_computation.4.clone.1 | convolution fusion | flops 37748736 | bytes 656384 | tf_op jit(solution)/shard_map/while/body/eval_jaxpr/kn,nrw->krw/dot_general | solution.py:42
  84.0 2.5 %fusion.24 = f32[1,4,16,2048]{3,1,2,0:T(4,128)S(1)} fusion(s32[16,2048]{1,0:T(8,128)S(1)} %dynamic-slice_bitcast_fusion.2, bf16[4,128]{1,0:T(4,128)(2,1)S(1)} %get-tuple-element.111), kind=kOutput, calls=%fused_computation.4.clone.1 | convolution fusion | flops 37748736 | bytes 656384 | tf_op jit(solution)/shard_map/while/body/eval_jaxpr/kn,nrw->krw/dot_general | solution.py:42
  88.5 2.5 %fusion.24 = f32[1,4,16,2048]{3,1,2,0:T(4,128)S(1)} fusion(s32[16,2048]{1,0:T(8,128)S(1)} %dynamic-slice_bitcast_fusion.2, bf16[4,128]{1,0:T(4,128)(2,1)S(1)} %get-tuple-element.111), kind=kOutput, calls=%fused_computation.4.clone.1 | convolution fusion | flops 37748736 | bytes 656384 | tf_op jit(solution)/shard_map/while/body/eval_jaxpr/kn,nrw->krw/dot_general | solution.py:42
  97.7 2.5 %fusion.24 = f32[1,4,16,2048]{3,1,2,0:T(4,128)S(1)} fusion(s32[16,2048]{1,0:T(8,128)S(1)} %dynamic-slice_bitcast_fusion.2, bf16[4,128]{1,0:T(4,128)(2,1)S(1)} %get-tuple-element.111), kind=kOutput, calls=%fused_computation.4.clone.1 | convolution fusion | flops 37748736 | bytes 656384 | tf_op jit(solution)/shard_map/while/body/eval_jaxpr/kn,nrw->krw/dot_general | solution.py:42
  101.4 6.3 %slice.162 = f32[3,16,16,2048]{3,2,1,0:T(8,128)} slice(f32[4,16,16,2048]{3,2,1,0:T(8,128)} %bitcast.101), slice={[0:3], [0:16], [0:16], [0:2048]} | slice | bytes 12582912 | tf_op jit(solution)/shard_map/slice | solution.py:47
  112.4 6.4 %add_multiply_fusion = (f32[2,128,2048]{2,1,0:T(8,128)S(1)}, f32[2,128,2048]{2,1,0:T(8,128)S(1)}) fusion(f32[2,1,2050]{2,1,0:T(1,128)S(1)} %collective-permute-done.2, f32[2,128,2050]{2,1,0:T(8,128)S(1)} %concatenate.40, f32[2,1,2050]{2,1,0:T(1,128)S(1)} %collective-permute-done.3, f32[1,130,2050]{2,1,0:T(8,128)S(1)} %copy.30, f32[1,130,2050]{2,1,0:T(8,128)S(1)} %copy.28, ...), kind=kLoop, calls=%fused_computation.34 | loop fusion | flops 17825792 | bytes 12654656 | tf_op jit(solution)/shard_map/mul | solution.py:47
  125.7 44.7 %collective-permute-done.6 = f32[4,2,32,2048]{3,2,1,0:T(8,128)} collective-permute-done((f32[4,2,32,2048]{3,2,1,0:T(8,128)}, f32[4,2,32,2048]{3,2,1,0:T(8,128)}, u32[]{:S(2)}, u32[]{:S(2)}) %collective-permute-start.6) | collective-permute-done | bytes 2097184 | tf_op jit(solution)/shard_map/ppermute | solution.py:25
  170.4 2.7 %broadcast_select_fusion.1 = (f32[4,2,32,2048]{3,2,1,0:T(8,128)S(1)}, f32[4,2,32,2048]{3,2,1,0:T(8,128)S(1)}) fusion(f32[4,2,32,2048]{3,2,1,0:T(8,128)} %collective-permute-done.6, pred[2,32]{1,0:T(4,128)(4,1)S(1)} %bitcast.106, pred[]{:T(512)S(6)} %eq.61, f32[1,2,2,32,2048]{4,3,2,1,0:T(8,128)} %bitcast.99, f32[3,2,2,32,2048]{4,3,2,1,0:T(8,128)S(1)} %multiply_add_fusion), kind=kLoop, calls=%fused_computation.44 | loop fusion | flops 3670016 | bytes 10485825 | tf_op jit(solution)/shard_map/jit(_where)/select_n | solution.py:88
  175.8 21.2 %collective-permute-done.7 = f32[4,1,32,2048]{3,2,0,1:T(8,128)S(1)} collective-permute-done((f32[4,1,32,2048]{3,2,0,1:T(8,128)S(1)}, f32[4,1,32,2048]{3,2,0,1:T(8,128)S(1)}, u32[]{:S(2)}, u32[]{:S(2)}) %collective-permute-start.7) | collective-permute-done | bytes 1048608 | tf_op jit(solution)/shard_map/ppermute | solution.py:25
  (91 shorter events, 64.1 us)
Async XLA Ops:
  1.1 4.4 %collective-permute-start = (f32[2,128,1]{2,1,0:T(8,128)S(1)}, f32[2,128,1]{2,1,0:T(8,128)S(1)}, u32[]{:S(2)}, u32[]{:S(2)}) collective-permute-start(f32[2,128,1]{2,1,0:T(8,128)S(1)} %get-tuple-element.69), channel_id=1, source_target_pairs={{16,0},{17,1},{18,2},{19,3},{20,4},{21,5},{22,6},{23,7},{24,8},{25... | collective-permute-start | bytes 3080 | tf_op jit(solution)/shard_map/ppermute | solution.py:19
  2.4 4.0 %collective-permute-start.1 = (f32[2,128,1]{2,1,0:T(8,128)S(1)}, f32[2,128,1]{2,1,0:T(8,128)S(1)}, u32[]{:S(2)}, u32[]{:S(2)}) collective-permute-start(f32[2,128,1]{2,1,0:T(8,128)S(1)} %get-tuple-element.70), channel_id=1, source_target_pairs={{0,16},{1,17},{2,18},{3,19},{4,20},{5,21},{6,22},{7,23},{8,24},{9,... | collective-permute-start | bytes 3080 | tf_op jit(solution)/shard_map/ppermute | solution.py:16
  6.4 3.0 %copy-start.2 = (f32[2,128,1]{2,1,0:T(8,128)}, f32[2,128,1]{2,1,0:T(8,128)S(1)}, u32[]{:S(2)}) copy-start(f32[2,128,1]{2,1,0:T(8,128)S(1)} %collective-permute-done.1) | copy-start | bytes 3076
  9.4 6.9 %collective-permute-start.2 = (f32[2,1,2050]{2,1,0:T(1,128)S(1)}, f32[2,1,2050]{2,1,0:T(1,128)S(1)}, u32[]{:S(2)}, u32[]{:S(2)}) collective-permute-start(f32[2,1,2050]{2,1,0:T(1,128)S(1)} %get-tuple-element.66), channel_id=1, source_target_pairs={{4,0},{8,4},{12,8},{5,1},{9,5},{13,9},{6,2},{10,6},{14,10},{7,3},{... | collective-permute-start | bytes 49208 | tf_op jit(solution)/shard_map/ppermute | solution.py:19
  10.7 7.0 %collective-permute-start.3 = (f32[2,1,2050]{2,1,0:T(1,128)S(1)}, f32[2,1,2050]{2,1,0:T(1,128)S(1)}, u32[]{:S(2)}, u32[]{:S(2)}) collective-permute-start(f32[2,1,2050]{2,1,0:T(1,128)S(1)} %get-tuple-element.65), channel_id=1, source_target_pairs={{0,4},{4,8},{8,12},{1,5},{5,9},{9,13},{2,6},{6,10},{10,14},{3,7},{... | collective-permute-start | bytes 49208 | tf_op jit(solution)/shard_map/ppermute | solution.py:16
  18.1 10.2 %copy-start.5 = (bf16[4,128]{1,0:T(4,128)(2,1)S(1)}, bf16[4,128]{1,0:T(4,128)(2,1)}, u32[]{:S(2)}) copy-start(bf16[4,128]{1,0:T(4,128)(2,1)} %param.8) | copy-start | bytes 3076
  19.3 90.2 %collective-permute-start.4 = (f32[1,130,2050]{2,0,1:T(1,128)S(1)}, f32[1,130,2050]{2,0,1:T(1,128)}, u32[]{:S(2)}, u32[]{:S(2)}) collective-permute-start(f32[1,130,2050]{2,0,1:T(1,128)S(1)} %copy.27), channel_id=1, source_target_pairs={{1,0},{2,1},{3,2},{5,4},{6,5},{7,6},{9,8},{10,9},{11,10},{13,12},{... | collective-permute-start | bytes 3198008 | tf_op jit(solution)/shard_map/ppermute | solution.py:19
  22.8 88.2 %collective-permute-start.5 = (f32[1,130,2050]{2,0,1:T(1,128)}, f32[1,130,2050]{2,0,1:T(1,128)}, u32[]{:S(2)}, u32[]{:S(2)}) collective-permute-start(f32[1,130,2050]{2,0,1:T(1,128)} %copy.29), channel_id=1, source_target_pairs={{0,1},{1,2},{2,3},{4,5},{5,6},{6,7},{8,9},{9,10},{10,11},{12,13},{... | collective-permute-start | bytes 3198008 | tf_op jit(solution)/shard_map/ppermute | solution.py:16
  101.4 6.3 %copy-start.4 = (s32[128]{0:T(128)S(1)}, s32[128]{0:T(128)}, u32[]{:S(2)}) copy-start(s32[128]{0:T(128)} %param.9) | copy-start | bytes 1540
  109.5 2.9 %copy-start = (f32[2,128,2048]{2,1,0:T(8,128)S(1)}, f32[2,128,2048]{2,1,0:T(8,128)}, u32[]{:S(2)}) copy-start(f32[2,128,2048]{2,1,0:T(8,128)} %param.6) | copy-start | bytes 6291460
  109.5 2.9 %copy-start.3 = (f32[2,128,1]{2,1,0:T(8,128)S(1)}, f32[2,128,1]{2,1,0:T(8,128)}, u32[]{:S(2)}) copy-start(f32[2,128,1]{2,1,0:T(8,128)} %copy-done.2) | copy-start | bytes 3076
  112.4 6.5 %slice-start = ((s8[6291456]{0:T(1024)(128)(4,1)}), s8[4194304]{0:T(1024)(128)(4,1)S(1)}, s32[]{:S(2)}) async-start(s8[6291456]{0:T(1024)(128)(4,1)} %bitcast.93), calls=%async_computation | async-start | bytes 8388608
  112.4 6.4 %slice-start.1 = ((s8[6291456]{0:T(1024)(128)(4,1)}), s8[2097152]{0:T(1024)(128)(4,1)S(1)}, s32[]{:S(2)}) async-start(s8[6291456]{0:T(1024)(128)(4,1)} %bitcast.93), calls=%async_computation.1 | async-start | bytes 4194304
  121.0 1.0 copy-start.1
  123.6 46.8 %collective-permute-start.6 = (f32[4,2,32,2048]{3,2,1,0:T(8,128)}, f32[4,2,32,2048]{3,2,1,0:T(8,128)}, u32[]{:S(2)}, u32[]{:S(2)}) collective-permute-start(f32[4,2,32,2048]{3,2,1,0:T(8,128)} %select_bitcast_fusion), channel_id=1, source_target_pairs={{0,1},{1,0},{2,3},{3,2},{4,5},{5,4},{6,7},{7,6},{8,9},{9,8},{10,11... | collective-permute-start | bytes 6291464 | tf_op jit(solution)/shard_map/ppermute | solution.py:25
  173.8 23.1 %collective-permute-start.7 = (f32[4,1,32,2048]{3,2,0,1:T(8,128)S(1)}, f32[4,1,32,2048]{3,2,0,1:T(8,128)S(1)}, u32[]{:S(2)}, u32[]{:S(2)}) collective-permute-start(f32[4,1,32,2048]{3,2,0,1:T(8,128)S(1)} %select_bitcast_fusion.1), channel_id=1, source_target_pairs={{0,2},{1,3},{2,0},{3,1},{4,6},{5,7},{6,4},{7,5},{8,10},{9,11},{10,... | collective-permute-start | bytes 3145736 | tf_op jit(solution)/shard_map/ppermute | solution.py:25
where the time goes:
time: 199 us
  waiting for transfers between devices  68.2 us (34%)
  local copies, waits for them, and re-layouts  49.6 us (25%)
  matrix products  40.8 us (21%)
  starting transfers between devices  22 us (11%)
  other arithmetic  17.5 us (9%)
    ppermute x2, waiting for transfers between devices, partner(): lax.ppermute(x, axis, [(i, i ^ 1 << distance) for i in range(lax.axis_siz...  65.8 us
    dot_general x16, matrix products, lookup(): jnp.einsum('kn,nrw->krw', table, onehot, preferred_element_type=jnp.float32)  40.8 us
    dynamic_update_slice x16, local copies, waits for them, and re-layouts, classify(): looked = lax.map(lookup, blocked)  17.6 us
    eq x16, local copies, waits for them, and re-layouts, lookup(): onehot = (block_bins[None] == labels[:, None, None]).astype(jnp.bfloat16)  14.6 us
    ppermute x3, starting transfers between devices, extended(): lax.ppermute(lax.slice_in_dim(block, block.shape[dim] - width, None, axis...  14.2 us
    mul x2, other arithmetic, classify(): emitted = looked[:3] * (shading * opacity)[None]  7.77 us
    slice x1, local copies, waits for them, and re-layouts, classify(): emitted = looked[:3] * (shading * opacity)[None]  6.29 us
    ppermute x2, starting transfers between devices, partner(): lax.ppermute(x, axis, [(i, i ^ 1 << distance) for i in range(lax.axis_siz...  4 us
  transfers between devices with their start and end apart: 8, of which 4 were waited for; matrix products, arithmetic and copies ran while one was open for 43% of the time, Pallas kernels for 0%

commit v1 on v0

v1 whole, which is shorter than its diff:
```python
import functools

import jax
import jax.numpy as jnp
from jax import lax
from jax.experimental import pallas as pl
from jax.experimental.pallas import tpu as pltpu
from jax.sharding import PartitionSpec as P

light_x = 0.36
light_y = 0.48
light_z = 0.8
LANES = 128
ROWS = 8
WIDE = 512


def partner(x, axis, distance):
    return lax.ppermute(x, axis, [(i, i ^ distance) for i in range(lax.axis_size(axis))])


def shade_kernel(count, depth, place, *refs):
    bricks = refs[:count]
    edges = refs[count : 2 * count]
    beside = refs[2 * count]
    ordered, shading, ext = refs[2 * count + 1 :]
    rows, width = ordered.shape[1:]
    total = count * depth
    rank = place[0]
    side = place[1]
    zero_plane = jnp.zeros((rows, width), jnp.float32)
    ext[0, ROWS : ROWS + rows, LANES : LANES + width] = zero_plane
    ext[total + 1, ROWS : ROWS + rows, LANES : LANES + width] = zero_plane
    for slot in range(count):
        for j in range(depth):
            at = (rank ^ slot) * depth + j
            plane = bricks[slot][j]
            ordered[at] = plane
            ext[at + 1, ROWS : ROWS + rows, LANES : LANES + width] = plane
            ext[at + 1, ROWS - 1 : ROWS, LANES : LANES + width] = edges[slot][j : j + 1, :]
            ext[at + 1, ROWS + rows : ROWS + rows + 1, LANES : LANES + width] = edges[slot][depth + j : depth + j + 1, :]
            column = beside[slot * depth + j]
            ext[at + 1, ROWS : ROWS + rows, :LANES] = jnp.where(side == 1, column, 0.0)
            ext[at + 1, ROWS : ROWS + rows, LANES + width :] = jnp.where(side == 0, column, 0.0)

    def plane_step(at, _):
        for top in range(0, rows, ROWS):
            here = slice(ROWS + top, 2 * ROWS + top)
            for left in range(0, width, WIDE):
                cols = slice(LANES + left, LANES + left + WIDE)
                dx = (
                    ext[at + 1, here, LANES + left + 1 : LANES + left + 1 + WIDE]
                    - ext[at + 1, here, LANES + left - 1 : LANES + left - 1 + WIDE]
                )
                dy = (
                    ext[at + 1, ROWS + top + 1 : 2 * ROWS + top + 1, cols]
                    - ext[at + 1, ROWS + top - 1 : 2 * ROWS + top - 1, cols]
                )
                dz = ext[at + 2, here, cols] - ext[at, here, cols]
                facing = jnp.abs((0.5 * light_x) * dx + (0.5 * light_y) * dy + (0.5 * light_z) * dz)
                square = 0.25 * (dx * dx + dy * dy + dz * dz) + 1.0
                shading[at, top : top + ROWS, left : left + WIDE] = 0.3 + 0.7 * facing * lax.rsqrt(square)
        return 0

    lax.fori_loop(0, total, plane_step, 0)


def blend_kernel(count, depth, place, table, flips, ordered, shading, *refs):
    bricks = refs[:count]
    image = refs[-2]
    sorted_bins = refs[-1]
    total = count * depth
    rows, width = image.shape[1:]
    rank = place[0]
    for slot in range(count):
        for j in range(depth):
            sorted_bins[(rank ^ slot) * depth + j] = bricks[slot][j]
    palette = [table[c] for c in range(4)]
    back = flips[...] == 1

    def look(entries, labels):
        return jnp.take_along_axis(entries, labels, axis=1, mode="promise_in_bounds")

    def tile_step(step, _):
        cols = pl.ds(pl.multiple_of(step * LANES, LANES), LANES)
        labels = [sorted_bins[d, :, cols] for d in range(total)]
        sums = [jnp.zeros((rows, LANES), jnp.float32)]
        for d in range(total):
            sums.append(sums[-1] + look(palette[3], labels[d]) * ordered[d, :, cols])
        whole = sums[-1]
        through = [jnp.exp(-jnp.where(back, whole - s, s)) for s in sums]
        colour = [jnp.zeros((rows, LANES), jnp.float32) for _ in range(3)]
        for d in range(total):
            weight = jnp.abs(through[d] - through[d + 1]) * shading[d, :, cols]
            for c in range(3):
                colour[c] = colour[c] + weight * look(palette[c], labels[d])
        for c in range(3):
            image[c, :, cols] = colour[c]
        image[3, :, cols] = 1.0 - jnp.exp(-whole)
        return 0

    lax.fori_loop(0, width // LANES, tile_step, 0)


def shards(field, bins, table, march_order):
    depth, height, width = field.shape
    count = lax.axis_size("gz")
    rank = lax.axis_index("gz").astype(jnp.int32)
    side = lax.axis_index("sx").astype(jnp.int32)
    place = jnp.stack([rank, side])
    rows = height // count
    total = count * depth
    cuts = [(0, rows)] if rows <= ROWS else [(0, rows - ROWS), (rows - ROWS, ROWS)]

    def piece(array, slot, start, size):
        return lax.dynamic_slice_in_dim(array, (rank ^ slot) * rows + start, size, axis=1)

    def scatter(pieces):
        return [pieces[0]] + [partner(pieces[slot], "gz", slot) for slot in range(1, count)]

    slots = range(count)
    field_bricks = scatter([piece(field, slot, 0, rows) for slot in slots])

    forward = [(i, i + 1) for i in range(lax.axis_size("sy") - 1)]
    backward = [(target, source) for source, target in forward]
    above = lax.ppermute(field[:, height - 1 :], "sy", forward)
    below = lax.ppermute(field[:, :1], "sy", backward)
    tops = jnp.concatenate([above, field[:, rows - 1 : height - 1 : rows]], axis=1)
    bottoms = jnp.concatenate([field[:, rows::rows], below], axis=1)
    edge_rows = jnp.concatenate([tops, bottoms], axis=0)
    edges = scatter(
        [lax.dynamic_index_in_dim(edge_rows, rank ^ slot, axis=1, keepdims=False) for slot in slots]
    )

    bins_bricks = [
        scatter([piece(bins, slot, start, size) for slot in slots]) for start, size in cuts
    ]

    edge_column = (1 - side) * (width - LANES)
    slab = jnp.concatenate(
        [lax.dynamic_slice_in_dim(brick, edge_column, LANES, axis=2) for brick in field_bricks], axis=0
    )
    beside = partner(slab, "sx", 1)

    vmem = pl.BlockSpec(memory_space=pltpu.VMEM)
    smem = pl.BlockSpec(memory_space=pltpu.SMEM)
    planes = jax.ShapeDtypeStruct((total, rows, width), jnp.float32)
    ordered, shading = pl.pallas_call(
        functools.partial(shade_kernel, count, depth),
        out_shape=(planes, planes),
        in_specs=[smem] + [vmem] * (2 * count + 1),
        out_specs=(vmem, vmem),
        scratch_shapes=[pltpu.VMEM((total + 2, rows + 2 * ROWS, width + 2 * LANES), jnp.float32)],
        compiler_params=pltpu.CompilerParams(vmem_limit_bytes=40 * 1024 * 1024),
        cost_estimate=pl.CostEstimate(
            flops=20 * total * rows * width, bytes_accessed=16 * total * rows * width, transcendentals=total * rows * width
        ),
        name="shade",
    )(place, *field_bricks, *edges, beside)

    flips = lax.dynamic_slice_in_dim(march_order, rank * rows, rows, axis=0)
    flips = jnp.broadcast_to(flips[:, None], (rows, LANES))
    palette = jnp.broadcast_to(table.astype(jnp.float32)[:, None, :], (4, ROWS, table.shape[1]))

    image = None
    for (start, size), bricks in zip(cuts, bins_bricks):
        first = start // ROWS
        plane_spec = pl.BlockSpec((total, ROWS, width), lambda i, first=first: (0, first + i, 0))
        in_specs = [
            smem,
            pl.BlockSpec((4, ROWS, table.shape[1]), lambda i: (0, 0, 0)),
            pl.BlockSpec((ROWS, LANES), lambda i, first=first: (first + i, 0)),
            plane_spec,
            plane_spec,
        ] + [pl.BlockSpec((depth, ROWS, width), lambda i: (0, i, 0))] * count
        operands = [place, palette, flips, ordered, shading, *bricks]
        aliases = {}
        if image is not None:
            in_specs.append(pl.BlockSpec(memory_space=pl.ANY))
            aliases = {len(operands): 0}
            operands.append(image)
        image = pl.pallas_call(
            functools.partial(blend_kernel, count, depth),
            grid=(size // ROWS,),
            out_shape=jax.ShapeDtypeStruct((4, rows, width), jnp.float32),
            in_specs=in_specs,
            out_specs=pl.BlockSpec((4, ROWS, width), lambda i, first=first: (0, first + i, 0)),
            scratch_shapes=[pltpu.VMEM((total, ROWS, width), jnp.int32)],
            input_output_aliases=aliases,
            compiler_params=pltpu.CompilerParams(vmem_limit_bytes=40 * 1024 * 1024),
            cost_estimate=pl.CostEstimate(
                flops=20 * total * size * width, bytes_accessed=16 * total * size * width, transcendentals=total * size * width
            ),
            name="blend",
        )(*operands)
    return image


def solution(mesh):
    placed = (P("gz", "sy", "sx"), P("gz", "sy", "sx"), P(), P("sy"))
    return jax.shard_map(
        shards, mesh=mesh, in_specs=placed, out_specs=P(None, ("sy", "gz"), "sx"), check_vma=False
    )
```

time: 199 us -> 79.5 us (0.40)
  waiting for transfers between devices: 68.2 us -> 18 us
  matrix products: 40.8 us -> 0 us
  local copies, waits for them, and re-layouts: 49.6 us -> 13.6 us
  Pallas kernels: 0 us -> 24 us
  other arithmetic: 17.5 us -> 1.79 us
    ppermute x8 -> x15, waiting for transfers between devices: 68.2 us -> 18 us  [the longest x13 18 us: partner(): lax.ppermute(x, axis, [(i, i ^ distance) for i in range(lax.axis_size(axi...]
    dot_general x16 -> x0, matrix products: 40.8 us -> none  [lookup(): jnp.einsum('kn,nrw->krw', table, onehot, preferred_element_type=jnp.float32)]
    pallas_call x0 -> x3, Pallas kernels: none -> 24 us  [the longest x2 12.1 us: shards(): pl.pallas_call(functools.partial(blend_kernel, count, depth), grid=(size...]
    dynamic_update_slice x16 -> x0, local copies, waits for them, and re-layouts: 17.6 us -> none  [classify(): looked = lax.map(lookup, blocked)]
    eq x16 -> x0, local copies, waits for them, and re-layouts: 14.6 us -> none  [lookup(): onehot = (block_bins[None] == labels[:, None, None]).astype(jnp.bfloat16)]
    mul x5 -> x0, other arithmetic: 8.2 us -> none  [the longest x2 7.77 us: classify(): emitted = looked[:3] * (shading * opacity)[None]]
    dynamic_slice x0 -> x9, local copies, waits for them, and re-layouts: none -> 7.75 us  [the longest x3 6.06 us: piece(): lax.dynamic_slice_in_dim(array, (rank ^ slot) * rows + start, size, axis=1)]
    slice x7 -> x3, local copies, waits for them, and re-layouts: 11.3 us -> 5.76 us  [the longest x1 2.1 us: shards(): tops = jnp.concatenate([above, field[:, rows - 1:height - 1:rows]], axis=1)]
  transfers between devices with their start and end apart: 8 -> 15, of which waited for: 4 -> 3; matrix products, arithmetic and copies ran while one was open for 43% -> 16% of each run, Pallas kernels for 0% -> 26%
where the time goes in v1:
time: 79.5 us; the launch traced here: 79 us
  Pallas kernels  24 us (30%)
  starting transfers between devices  21.5 us (27%)
  waiting for transfers between devices  18 us (23%)
  local copies, waits for them, and re-layouts  13.6 us (17%)
  other arithmetic  1.79 us (2%)
    ppermute x13, waiting for transfers between devices, partner(): lax.ppermute(x, axis, [(i, i ^ distance) for i in range(lax.axis_size(axi...  18 us
    ppermute x13, starting transfers between devices, partner(): lax.ppermute(x, axis, [(i, i ^ distance) for i in range(lax.axis_size(axi...  16.3 us
    pallas_call x2, Pallas kernels, shards(): pl.pallas_call(functools.partial(blend_kernel, count, depth), grid=(size...  12.1 us
    pallas_call x1, Pallas kernels, shards(): pl.pallas_call(functools.partial(shade_kernel, count, depth), out_shape=(...  11.9 us
    dynamic_slice x3, local copies, waits for them, and re-layouts, piece(): lax.dynamic_slice_in_dim(array, (rank ^ slot) * rows + start, size, axis=1)  6.06 us
    ppermute x1, starting transfers between devices, shards(): above = lax.ppermute(field[:, height - 1:], 'sy', forward)  3.94 us
    slice x1, local copies, waits for them, and re-layouts, shards(): tops = jnp.concatenate([above, field[:, rows - 1:height - 1:rows]], axis=1)  2.1 us
    slice x1, local copies, waits for them, and re-layouts, shards(): bottoms = jnp.concatenate([field[:, rows::rows], below], axis=1)  2.05 us
  transfers between devices with their start and end apart: 15, of which 3 were waited for; matrix products, arithmetic and copies ran while one was open for 16% of the time, Pallas kernels for 26%

profile of v1, /device:TPU:0, one launch (start us, length us, event | category | flops | bytes accessed | tf_op | source)
XLA Modules:
  0.0 79.0 jit_solution(11888942640941702316)
XLA Ops:
  0.0 2.5 %constant_dynamic-slice_fusion.16 = (f32[2,32,2048]{2,1,0:T(8,128)S(1)}, f32[2,32,2048]{2,1,0:T(8,128)S(1)}, f32[2,32,2048]{2,1,0:T(8,128)}, f32[2,32,2048]{2,1,0:T(8,128)S(1)}) fusion(f32[2,128,2048]{2,1,0:T(8,128)} %param.4, s32[]{:T(128)S(6)} %select_n.55, s32[]{:T(128)S(6)} %select_n.54, s32[]{:T(128)S(6)} %select_n.53, s32[]{:T(128)S(6)} %select_n.52), kind=kLoop, calls=%fused_computation.22 | loop fusion | bytes 4194320 | tf_op jit(solution)/shard_map/dynamic_slice | solution.py:116
  2.5 2.9 %collective-permute-start = (f32[2,32,2048]{2,1,0:T(8,128)}, f32[2,32,2048]{2,1,0:T(8,128)S(1)}, u32[]{:S(2)}, u32[]{:S(2)}) collective-permute-start(f32[2,32,2048]{2,1,0:T(8,128)} %get-tuple-element.21), channel_id=1, source_target_pairs={{0,1},{1,0},{2,3},{3,2},{4,5},{5,4},{6,7},{7,6},{8,9},{9,8},{10,11... | collective-permute-start | bytes 1572872 | tf_op jit(solution)/shard_map/ppermute | solution.py:19
  5.4 1.5 %collective-permute-start.2 = (f32[2,32,2048]{2,1,0:T(8,128)S(1)}, f32[2,32,2048]{2,1,0:T(8,128)S(1)}, u32[]{:S(2)}, u32[]{:S(2)}) collective-permute-start(f32[2,32,2048]{2,1,0:T(8,128)S(1)} %get-tuple-element.19), channel_id=1, source_target_pairs={{0,3},{1,2},{2,1},{3,0},{4,7},{5,6},{6,5},{7,4},{8,11},{9,10},{10,... | collective-permute-start | bytes 1572872 | tf_op jit(solution)/shard_map/ppermute | solution.py:19
  7.0 1.6 %fusion = (f32[2,1,2048]{2,1,0:T(1,128)}, f32[2,1,2048]{2,1,0:T(1,128)}) fusion(f32[2,128,2048]{2,1,0:T(8,128)} %param.4), kind=kLoop, calls=%fused_computation.27 | loop fusion | bytes 65536 | tf_op jit(solution)/shard_map/slice | solution.py:126
  8.6 3.9 %collective-permute-start.3 = (f32[2,1,2048]{2,1,0:T(1,128)}, f32[2,1,2048]{2,1,0:T(1,128)S(1)}, u32[]{:S(2)}, u32[]{:S(2)}) collective-permute-start(f32[2,1,2048]{2,1,0:T(1,128)} %get-tuple-element.17), channel_id=1, source_target_pairs={{0,4},{4,8},{8,12},{1,5},{5,9},{9,13},{2,6},{6,10},{10,14},{3,7},{... | collective-permute-start | bytes 49160 | tf_op jit(solution)/shard_map/ppermute | solution.py:126
  12.5 1.3 %collective-permute-start.4 = (f32[2,1,2048]{2,1,0:T(1,128)}, f32[2,1,2048]{2,1,0:T(1,128)}, u32[]{:S(2)}, u32[]{:S(2)}) collective-permute-start(f32[2,1,2048]{2,1,0:T(1,128)} %get-tuple-element.18), channel_id=1, source_target_pairs={{4,0},{8,4},{12,8},{5,1},{9,5},{13,9},{6,2},{10,6},{14,10},{7,3},{... | collective-permute-start | bytes 49160 | tf_op jit(solution)/shard_map/ppermute | solution.py:127
  13.8 2.4 %constant_dynamic-slice_fusion = (s32[2,24,2048]{2,1,0:T(8,128)}, s32[2,24,2048]{2,1,0:T(8,128)}, s32[2,24,2048]{2,1,0:T(8,128)S(1)}, s32[2,24,2048]{2,1,0:T(8,128)}) fusion(s32[2,128,2048]{2,1,0:T(8,128)} %param.5, s32[]{:T(128)S(6)} %select_n.55, s32[]{:T(128)S(6)} %select_n.53, s32[]{:T(128)S(6)} %select_n.52, s32[]{:T(128)S(6)} %select_n.54), kind=kLoop, calls=%fused_computation.6 | loop fusion | bytes 3145744 | tf_op jit(solution)/shard_map/dynamic_slice | solution.py:116
  16.3 1.5 %constant_dynamic-slice_fusion.11 = f32[2,32,128]{2,1,0:T(8,128)} fusion(f32[2,128,2048]{2,1,0:T(8,128)} %param.4, s32[]{:T(128)S(6)} %select_n.60, s32[]{:T(128)S(6)} %select_n.62), kind=kLoop, calls=%fused_computation.17 | loop fusion | bytes 65544 | tf_op jit(solution)/shard_map/dynamic_slice | solution.py:141
  17.7 2.1 %slice.13 = f32[2,3,2048]{2,1,0:T(4,128)} slice(f32[2,128,2048]{2,1,0:T(8,128)} %param.4), slice={[0:2:1], [31:127:32], [0:2048:1]} | slice | bytes 98304 | tf_op jit(solution)/shard_map/slice | solution.py:128
  19.8 2.1 %slice.14 = f32[2,3,2048]{2,1,0:T(4,128)} slice(f32[2,128,2048]{2,1,0:T(8,128)} %param.4), slice={[0:2:1], [32:128:32], [0:2048:1]} | slice | bytes 98304 | tf_op jit(solution)/shard_map/slice | solution.py:129
  21.9 1.5 %collective-permute-start.12 = (s32[2,24,2048]{2,1,0:T(8,128)}, s32[2,24,2048]{2,1,0:T(8,128)S(1)}, u32[]{:S(2)}, u32[]{:S(2)}) collective-permute-start(s32[2,24,2048]{2,1,0:T(8,128)} %get-tuple-element.10), channel_id=1, source_target_pairs={{0,1},{1,0},{2,3},{3,2},{4,5},{5,4},{6,7},{7,6},{8,9},{9,8},{10,11... | collective-permute-start | bytes 1179656 | tf_op jit(solution)/shard_map/ppermute | solution.py:19
  23.4 1.5 %collective-permute-start.13 = (s32[2,24,2048]{2,1,0:T(8,128)}, s32[2,24,2048]{2,1,0:T(8,128)S(1)}, u32[]{:S(2)}, u32[]{:S(2)}) collective-permute-start(s32[2,24,2048]{2,1,0:T(8,128)} %get-tuple-element.12), channel_id=1, source_target_pairs={{0,2},{1,3},{2,0},{3,1},{4,6},{5,7},{6,4},{7,5},{8,10},{9,11},{10,... | collective-permute-start | bytes 1179656 | tf_op jit(solution)/shard_map/ppermute | solution.py:19
  24.9 1.0 %maximum_maximum_fusion = f32[4,4,2048]{2,1,0:T(4,128)S(1)} fusion(f32[2,1,2048]{2,1,0:T(1,128)} %collective-permute-done.4, f32[2,3,2048]{2,1,0:T(4,128)} %slice.14, f32[2,3,2048]{2,1,0:T(4,128)} %slice.13, f32[2,1,2048]{2,1,0:T(1,128)S(1)} %collective-permute-done.3), kind=kLoop, calls=%fused_computation | loop fusion | flops 98304 | bytes 262144 | tf_op jit(solution)/shard_map/concatenate | solution.py:130
  26.6 4.6 %collective-permute-done.2.refs_3_ = f32[2,32,2048]{2,1,0:T(8,128)S(1)} collective-permute-done((f32[2,32,2048]{2,1,0:T(8,128)S(1)}, f32[2,32,2048]{2,1,0:T(8,128)S(1)}, u32[]{:S(2)}, u32[]{:S(2)}) %collective-permute-start.2) | collective-permute-done | bytes 524320 | tf_op jit(solution)/shard_map/ppermute | solution.py:19
  31.2 1.5 %collective-permute-start.5 = (f32[4,2048]{1,0:T(4,128)S(1)}, f32[4,2048]{1,0:T(4,128)S(1)}, u32[]{:S(2)}, u32[]{:S(2)}) collective-permute-start(f32[4,2048]{1,0:T(4,128)S(1)} %bitcast.17), channel_id=1, source_target_pairs={{0,1},{1,0},{2,3},{3,2},{4,5},{5,4},{6,7},{7,6},{8,9},{9,8},{10,11... | collective-permute-start | bytes 98312 | tf_op jit(solution)/shard_map/ppermute | solution.py:19
  34.0 12.4 %collective-permute-done.5.refs_5_ = f32[4,2048]{1,0:T(4,128)S(1)} collective-permute-done((f32[4,2048]{1,0:T(4,128)S(1)}, f32[4,2048]{1,0:T(4,128)S(1)}, u32[]{:S(2)}, u32[]{:S(2)}) %collective-permute-start.5) | collective-permute-done | bytes 32800 | tf_op jit(solution)/shard_map/ppermute | solution.py:19
  46.4 2.7 %collective-permute-start.7 = (f32[4,2048]{1,0:T(4,128)S(1)}, f32[4,2048]{1,0:T(4,128)S(1)}, u32[]{:S(2)}, u32[]{:S(2)}) collective-permute-start(f32[4,2048]{1,0:T(4,128)S(1)} %bitcast.15), channel_id=1, source_target_pairs={{0,3},{1,2},{2,1},{3,0},{4,7},{5,6},{6,5},{7,4},{8,11},{9,10},{10,... | collective-permute-start | bytes 98312 | tf_op jit(solution)/shard_map/ppermute | solution.py:19
  49.1 1.1 %constant_dynamic-slice_fusion.4 = (s32[2,8,2048]{2,1,0:T(8,128)S(1)}, s32[2,8,2048]{2,1,0:T(8,128)S(1)}, s32[2,8,2048]{2,1,0:T(8,128)S(1)}, s32[2,8,2048]{2,1,0:T(8,128)S(1)}) fusion(s32[2,128,2048]{2,1,0:T(8,128)} %param.5, s32[]{:T(128)S(6)} %select_n.66, s32[]{:T(128)S(6)} %select_n.65, s32[]{:T(128)S(6)} %select_n.64, s32[]{:T(128)S(6)} %select_n.63), kind=kLoop, calls=%fused_computation.10 | loop fusion | bytes 1048592 | tf_op jit(solution)/shard_map/dynamic_slice | solution.py:116
  50.3 1.0 %collective-permute-done.7.refs_7_ = f32[4,2048]{1,0:T(4,128)S(1)} collective-permute-done((f32[4,2048]{1,0:T(4,128)S(1)}, f32[4,2048]{1,0:T(4,128)S(1)}, u32[]{:S(2)}, u32[]{:S(2)}) %collective-permute-start.7) | collective-permute-done | bytes 32800 | tf_op jit(solution)/shard_map/ppermute | solution.py:19
  51.3 1.8 %collective-permute-start.10 = (s32[2,8,2048]{2,1,0:T(8,128)S(1)}, s32[2,8,2048]{2,1,0:T(8,128)S(1)}, u32[]{:S(2)}, u32[]{:S(2)}) collective-permute-start(s32[2,8,2048]{2,1,0:T(8,128)S(1)} %get-tuple-element.14), channel_id=1, source_target_pairs={{0,2},{1,3},{2,0},{3,1},{4,6},{5,7},{6,4},{7,5},{8,10},{9,11},{10,... | collective-permute-start | bytes 393224 | tf_op jit(solution)/shard_map/ppermute | solution.py:19
  53.0 1.4 %collective-permute-start.11 = (s32[2,8,2048]{2,1,0:T(8,128)S(1)}, s32[2,8,2048]{2,1,0:T(8,128)S(1)}, u32[]{:S(2)}, u32[]{:S(2)}) collective-permute-start(s32[2,8,2048]{2,1,0:T(8,128)S(1)} %get-tuple-element.13), channel_id=1, source_target_pairs={{0,3},{1,2},{2,1},{3,0},{4,7},{5,6},{6,5},{7,4},{8,11},{9,10},{10,... | collective-permute-start | bytes 393224 | tf_op jit(solution)/shard_map/ppermute | solution.py:19
  54.9 11.9 %shade.1 = (f32[8,32,2048]{2,1,0:T(8,128)S(1)}, f32[8,32,2048]{2,1,0:T(8,128)S(1)}) custom-call(s32[2]{0:T(128)S(1)} %pad_add_fusion.place, f32[2,32,2048]{2,1,0:T(8,128)S(1)} %get-tuple-element.22.refs_0_, f32[2,32,2048]{2,1,0:T(8,128)S(1)} %collective-permute-done.refs_1_, f32[2,32,2048]{2,1,0:T(8,128)S(1)} %collective-permute-done.1.refs_2_, ...), custom_call_target="tpu_custom_call" | custom-call | flops 10485760 | bytes 8388608 | tf_op jit(solution)/shard_map/shade/pallas_call | solution.py:148
  66.9 8.5 %blend.2.refs_4_ = f32[4,32,2048]{2,1,0:T(8,128)} custom-call(s32[2]{0:T(128)S(1)} %pad_add_fusion.place, f32[4,8,128]{2,1,0:T(8,128)S(1)} %broadcast_in_dim.4.table, s32[32,128]{1,0:T(8,128)S(1)} %broadcast_in_dim.5.flips, f32[8,32,2048]{2,1,0:T(8,128)S(1)} %get-tuple-element.7.ordered, f32[8,32,2048]{2,1,0:T(8,128)S(1)} %get-tuple-element.8.shading, ...), custom_call_target="tpu_custom_call" | custom-call | flops 7864320 | bytes 6291456 | tf_op jit(solution)/shard_map/blend/pallas_call | solution.py:182
  75.4 3.6 %blend.3 = f32[4,32,2048]{2,1,0:T(8,128)} custom-call(s32[2]{0:T(128)S(1)} %pad_add_fusion.place, f32[4,8,128]{2,1,0:T(8,128)S(1)} %broadcast_in_dim.4.table, s32[32,128]{1,0:T(8,128)S(1)} %broadcast_in_dim.5.flips, f32[8,32,2048]{2,1,0:T(8,128)S(1)} %get-tuple-element.7.ordered, ...), custom_call_target="tpu_custom_call", output_to_operand_aliasing={{}: (9, {})} | custom-call | flops 2621440 | bytes 2097152 | tf_op jit(solution)/shard_map/blend/pallas_call | solution.py:182
  (34 shorter events, 2.7 us)
Async XLA Ops:
  2.5 23.6 %collective-permute-start = (f32[2,32,2048]{2,1,0:T(8,128)}, f32[2,32,2048]{2,1,0:T(8,128)S(1)}, u32[]{:S(2)}, u32[]{:S(2)}) collective-permute-start(f32[2,32,2048]{2,1,0:T(8,128)} %get-tuple-element.21), channel_id=1, source_target_pairs={{0,1},{1,0},{2,3},{3,2},{4,5},{5,4},{6,7},{7,6},{8,9},{9,8},{10,11... | collective-permute-start | bytes 1572872 | tf_op jit(solution)/shard_map/ppermute | solution.py:19
  5.4 25.8 %collective-permute-start.2 = (f32[2,32,2048]{2,1,0:T(8,128)S(1)}, f32[2,32,2048]{2,1,0:T(8,128)S(1)}, u32[]{:S(2)}, u32[]{:S(2)}) collective-permute-start(f32[2,32,2048]{2,1,0:T(8,128)S(1)} %get-tuple-element.19), channel_id=1, source_target_pairs={{0,3},{1,2},{2,1},{3,0},{4,7},{5,6},{6,5},{7,4},{8,11},{9,10},{10,... | collective-permute-start | bytes 1572872 | tf_op jit(solution)/shard_map/ppermute | solution.py:19
  6.9 25.8 %collective-permute-start.1 = (f32[2,32,2048]{2,1,0:T(8,128)S(1)}, f32[2,32,2048]{2,1,0:T(8,128)S(1)}, u32[]{:S(2)}, u32[]{:S(2)}) collective-permute-start(f32[2,32,2048]{2,1,0:T(8,128)S(1)} %get-tuple-element.20), channel_id=1, source_target_pairs={{0,2},{1,3},{2,0},{3,1},{4,6},{5,7},{6,4},{7,5},{8,10},{9,11},{10,... | collective-permute-start | bytes 1572872 | tf_op jit(solution)/shard_map/ppermute | solution.py:19
  8.6 13.3 %collective-permute-start.3 = (f32[2,1,2048]{2,1,0:T(1,128)}, f32[2,1,2048]{2,1,0:T(1,128)S(1)}, u32[]{:S(2)}, u32[]{:S(2)}) collective-permute-start(f32[2,1,2048]{2,1,0:T(1,128)} %get-tuple-element.17), channel_id=1, source_target_pairs={{0,4},{4,8},{8,12},{1,5},{5,9},{9,13},{2,6},{6,10},{10,14},{3,7},{... | collective-permute-start | bytes 49160 | tf_op jit(solution)/shard_map/ppermute | solution.py:126
  12.5 10.9 %collective-permute-start.4 = (f32[2,1,2048]{2,1,0:T(1,128)}, f32[2,1,2048]{2,1,0:T(1,128)}, u32[]{:S(2)}, u32[]{:S(2)}) collective-permute-start(f32[2,1,2048]{2,1,0:T(1,128)} %get-tuple-element.18), channel_id=1, source_target_pairs={{4,0},{8,4},{12,8},{5,1},{9,5},{13,9},{6,2},{10,6},{14,10},{7,3},{... | collective-permute-start | bytes 49160 | tf_op jit(solution)/shard_map/ppermute | solution.py:127
  21.9 32.9 %copy-start.1 = (s32[128]{0:T(128)S(1)}, s32[128]{0:T(128)}, u32[]{:S(2)}) copy-start(s32[128]{0:T(128)} %param.7) | copy-start | bytes 1540
  21.9 31.1 %collective-permute-start.12 = (s32[2,24,2048]{2,1,0:T(8,128)}, s32[2,24,2048]{2,1,0:T(8,128)S(1)}, u32[]{:S(2)}, u32[]{:S(2)}) collective-permute-start(s32[2,24,2048]{2,1,0:T(8,128)} %get-tuple-element.10), channel_id=1, source_target_pairs={{0,1},{1,0},{2,3},{3,2},{4,5},{5,4},{6,7},{7,6},{8,9},{9,8},{10,11... | collective-permute-start | bytes 1179656 | tf_op jit(solution)/shard_map/ppermute | solution.py:19
  23.4 43.4 %collective-permute-start.13 = (s32[2,24,2048]{2,1,0:T(8,128)}, s32[2,24,2048]{2,1,0:T(8,128)S(1)}, u32[]{:S(2)}, u32[]{:S(2)}) collective-permute-start(s32[2,24,2048]{2,1,0:T(8,128)} %get-tuple-element.12), channel_id=1, source_target_pairs={{0,2},{1,3},{2,0},{3,1},{4,6},{5,7},{6,4},{7,5},{8,10},{9,11},{10,... | collective-permute-start | bytes 1179656 | tf_op jit(solution)/shard_map/ppermute | solution.py:19
  26.0 40.9 %copy-start = (bf16[4,128]{1,0:T(4,128)(2,1)S(1)}, bf16[4,128]{1,0:T(4,128)(2,1)}, u32[]{:S(2)}) copy-start(bf16[4,128]{1,0:T(4,128)(2,1)} %param.6) | copy-start | bytes 3076
  26.1 40.8 %collective-permute-start.14 = (s32[2,24,2048]{2,1,0:T(8,128)}, s32[2,24,2048]{2,1,0:T(8,128)S(1)}, u32[]{:S(2)}, u32[]{:S(2)}) collective-permute-start(s32[2,24,2048]{2,1,0:T(8,128)} %get-tuple-element.9), channel_id=1, source_target_pairs={{0,3},{1,2},{2,1},{3,0},{4,7},{5,6},{6,5},{7,4},{8,11},{9,10},{10,... | collective-permute-start | bytes 1179656 | tf_op jit(solution)/shard_map/ppermute | solution.py:19
  31.2 15.2 %collective-permute-start.5 = (f32[4,2048]{1,0:T(4,128)S(1)}, f32[4,2048]{1,0:T(4,128)S(1)}, u32[]{:S(2)}, u32[]{:S(2)}) collective-permute-start(f32[4,2048]{1,0:T(4,128)S(1)} %bitcast.17), channel_id=1, source_target_pairs={{0,1},{1,0},{2,3},{3,2},{4,5},{5,4},{6,7},{7,6},{8,9},{9,8},{10,11... | collective-permute-start | bytes 98312 | tf_op jit(solution)/shard_map/ppermute | solution.py:19
  32.7 16.4 %collective-permute-start.6 = (f32[4,2048]{1,0:T(4,128)S(1)}, f32[4,2048]{1,0:T(4,128)S(1)}, u32[]{:S(2)}, u32[]{:S(2)}) collective-permute-start(f32[4,2048]{1,0:T(4,128)S(1)} %bitcast.16), channel_id=1, source_target_pairs={{0,2},{1,3},{2,0},{3,1},{4,6},{5,7},{6,4},{7,5},{8,10},{9,11},{10,... | collective-permute-start | bytes 98312 | tf_op jit(solution)/shard_map/ppermute | solution.py:19
  46.4 4.8 %collective-permute-start.7 = (f32[4,2048]{1,0:T(4,128)S(1)}, f32[4,2048]{1,0:T(4,128)S(1)}, u32[]{:S(2)}, u32[]{:S(2)}) collective-permute-start(f32[4,2048]{1,0:T(4,128)S(1)} %bitcast.15), channel_id=1, source_target_pairs={{0,3},{1,2},{2,1},{3,0},{4,7},{5,6},{6,5},{7,4},{8,11},{9,10},{10,... | collective-permute-start | bytes 98312 | tf_op jit(solution)/shard_map/ppermute | solution.py:19
  49.1 5.3 %collective-permute-start.8 = (f32[8,32,128]{2,1,0:T(8,128)S(1)}, f32[8,32,128]{2,1,0:T(8,128)S(1)}, u32[]{:S(2)}, u32[]{:S(2)}) collective-permute-start(f32[8,32,128]{2,1,0:T(8,128)S(1)} %pad_maximum_fusion), channel_id=1, source_target_pairs={{0,16},{16,0},{1,17},{17,1},{2,18},{18,2},{3,19},{19,3},{4,20},{20... | collective-permute-start | bytes 393224 | tf_op jit(solution)/shard_map/ppermute | solution.py:19
  51.3 24.2 %collective-permute-start.10 = (s32[2,8,2048]{2,1,0:T(8,128)S(1)}, s32[2,8,2048]{2,1,0:T(8,128)S(1)}, u32[]{:S(2)}, u32[]{:S(2)}) collective-permute-start(s32[2,8,2048]{2,1,0:T(8,128)S(1)} %get-tuple-element.14), channel_id=1, source_target_pairs={{0,2},{1,3},{2,0},{3,1},{4,6},{5,7},{6,4},{7,5},{8,10},{9,11},{10,... | collective-permute-start | bytes 393224 | tf_op jit(solution)/shard_map/ppermute | solution.py:19
  53.0 22.4 %collective-permute-start.11 = (s32[2,8,2048]{2,1,0:T(8,128)S(1)}, s32[2,8,2048]{2,1,0:T(8,128)S(1)}, u32[]{:S(2)}, u32[]{:S(2)}) collective-permute-start(s32[2,8,2048]{2,1,0:T(8,128)S(1)} %get-tuple-element.13), channel_id=1, source_target_pairs={{0,3},{1,2},{2,1},{3,0},{4,7},{5,6},{6,5},{7,4},{8,11},{9,10},{10,... | collective-permute-start | bytes 393224 | tf_op jit(solution)/shard_map/ppermute | solution.py:19
  54.5 21.0 %collective-permute-start.9 = (s32[2,8,2048]{2,1,0:T(8,128)S(1)}, s32[2,8,2048]{2,1,0:T(8,128)S(1)}, u32[]{:S(2)}, u32[]{:S(2)}) collective-permute-start(s32[2,8,2048]{2,1,0:T(8,128)S(1)} %get-tuple-element.15), channel_id=1, source_target_pairs={{0,1},{1,0},{2,3},{3,2},{4,5},{5,4},{6,7},{7,6},{8,9},{9,8},{10,11... | collective-permute-start | bytes 393224 | tf_op jit(solution)/shard_map/ppermute | solution.py:19

commit v2 on v1

v2 whole, which is shorter than its diff:
```python
import functools

import jax
import jax.numpy as jnp
from jax import lax
from jax.experimental import pallas as pl
from jax.experimental.pallas import tpu as pltpu
from jax.sharding import PartitionSpec as P

light_x = 0.36
light_y = 0.48
light_z = 0.8
LANES = 128
ROWS = 8
GROUP = 4
COLOUR_UNIT = 2.0**-12
OPACITY_UNIT = 2.0**-13
HALF_WORD = 16
VMEM_LIMIT = 40 * 1024 * 1024

vmem = pl.BlockSpec(memory_space=pltpu.VMEM)
smem = pl.BlockSpec(memory_space=pltpu.SMEM)
anywhere = pl.BlockSpec(memory_space=pl.ANY)


def partner(x, axis, distance):
    return lax.ppermute(x, axis, [(i, i ^ distance) for i in range(lax.axis_size(axis))])


def pack_kernel(count, depth, place, above, below, field, bins, *refs):
    messages = refs[:count]
    high, low, labels, sems = refs[count:]
    height, width = field.shape[1:]
    rows = height // count
    half = width // 2
    rank = place[0]
    copies = []
    for slot in range(count):
        target = rank ^ slot
        top = pl.multiple_of(jnp.maximum(target * rows - ROWS, 0), ROWS)
        bottom = pl.multiple_of(jnp.minimum(target * rows + rows, height - ROWS), ROWS)
        start = pl.multiple_of(target * rows, ROWS)
        moves = [
            pltpu.make_async_copy(field.at[:, pl.ds(top, ROWS)], high.at[slot], sems.at[slot, 0]),
            pltpu.make_async_copy(field.at[:, pl.ds(bottom, ROWS)], low.at[slot], sems.at[slot, 1]),
        ]
        if slot:
            moves.append(pltpu.make_async_copy(bins.at[:, pl.ds(start, ROWS)], labels.at[slot], sems.at[slot, 2]))
        for move in moves:
            move.start()
        copies.append(moves)
    for slot in range(count):
        target = rank ^ slot
        for move in copies[slot]:
            move.wait()
        for j in range(depth):
            upper = jnp.where(target == 0, above[j : j + 1, :], high[slot, j, ROWS - 1 : ROWS, :])
            lower = jnp.where(target == count - 1, below[j : j + 1, :], low[slot, j, 0:1, :])
            for h in range(2):
                cols = slice(h * half, (h + 1) * half)
                at = 2 * depth * h + j
                messages[slot][at : at + 1, :] = upper[:, cols]
                messages[slot][at + depth : at + depth + 1, :] = lower[:, cols]
                if slot:
                    first = 4 * depth + (2 * j + h) * ROWS
                    messages[slot][first : first + ROWS, :] = labels[slot, j, :, cols].astype(jnp.float32)


def shade_kernel(count, depth, place, *refs):
    bricks = refs[:count]
    messages = refs[count : 2 * count]
    beside = refs[2 * count]
    ordered, shading, ext = refs[2 * count + 1 :]
    rows, width = ordered.shape[1:]
    half = width // 2
    total = count * depth
    rank = place[0]
    side = place[1]
    inside = slice(ROWS, ROWS + rows)
    zero_plane = jnp.zeros((rows, width), jnp.float32)
    ext[0, inside, LANES : LANES + width] = zero_plane
    ext[total + 1, inside, LANES : LANES + width] = zero_plane
    for slot in range(count):
        for j in range(depth):
            at = (rank ^ slot) * depth + j
            plane = bricks[slot][j]
            ordered[at] = plane * OPACITY_UNIT
            ext[at + 1, inside, LANES : LANES + width] = plane
            for h in range(2):
                cols = slice(LANES + h * half, LANES + (h + 1) * half)
                row = 2 * depth * h + j
                ext[at + 1, ROWS - 1 : ROWS, cols] = messages[slot][row : row + 1, :]
                ext[at + 1, ROWS + rows : ROWS + rows + 1, cols] = messages[slot][row + depth : row + depth + 1, :]
            column = beside[slot * depth + j]
            ext[at + 1, inside, :LANES] = jnp.where(side == 1, column, 0.0)
            ext[at + 1, inside, LANES + width :] = jnp.where(side == 0, column, 0.0)
    lane = lax.broadcasted_iota(jnp.int32, (ROWS, LANES), 1)
    first = lane == 0
    last = lane == LANES - 1

    def plane_step(at, _):
        for top in range(0, rows, ROWS):
            here = slice(ROWS + top, 2 * ROWS + top)
            tiles = [ext[at + 1, here, left : left + LANES] for left in range(0, width + 2 * LANES, LANES)]
            toward = [pltpu.roll(tile, LANES - 1, 1) for tile in tiles]
            away = [pltpu.roll(tile, 1, 1) for tile in tiles]
            for c in range(1, width // LANES + 1):
                cols = slice(c * LANES, (c + 1) * LANES)
                dx = jnp.where(last, toward[c + 1], toward[c]) - jnp.where(first, away[c - 1], away[c])
                dy = (
                    ext[at + 1, ROWS + top + 1 : 2 * ROWS + top + 1, cols]
                    - ext[at + 1, ROWS + top - 1 : 2 * ROWS + top - 1, cols]
                )
                dz = ext[at + 2, here, cols] - ext[at, here, cols]
                facing = jnp.abs((0.5 * light_x) * dx + (0.5 * light_y) * dy + (0.5 * light_z) * dz)
                square = 0.25 * (dx * dx + dy * dy + dz * dz) + 1.0
                shading[at, top : top + ROWS, (c - 1) * LANES : c * LANES] = (
                    0.3 * COLOUR_UNIT + (0.7 * COLOUR_UNIT) * facing * lax.rsqrt(square)
                )
        return 0

    lax.fori_loop(0, total, plane_step, 0)


def blend_kernel(count, depth, start, packed, place, table, flips, ordered, shading, *refs):
    bricks = refs[:count]
    image, sorted_bins, result, sems = refs[-4:]
    total = count * depth
    rows, width = result.shape[1:]
    half = width // 2
    rank = place[0]
    for slot in range(count):
        for j in range(depth):
            at = (rank ^ slot) * depth + j
            if packed and slot:
                for h in range(2):
                    top = 4 * depth + (2 * j + h) * ROWS
                    values = bricks[slot][top : top + ROWS, :]
                    sorted_bins[at, :, h * half : (h + 1) * half] = values.astype(jnp.int32)
            else:
                sorted_bins[at] = bricks[slot][j]
    entries = [table[c] for c in range(2)]
    wide = GROUP * LANES
    groups = width // wide

    def copy(top, step):
        cols = pl.ds(pl.multiple_of(step * wide, wide), wide)
        return pltpu.make_async_copy(
            result.at[:, top : top + ROWS, cols],
            image.at[:, start + top : start + top + ROWS, cols],
            sems.at[top // ROWS, step],
        )

    def look(values, labels):
        return jnp.take_along_axis(values, labels, axis=1, mode="promise_in_bounds")

    def low_part(words):
        return (words & ((1 << HALF_WORD) - 1)).astype(jnp.float32)

    def high_part(words):
        return (words >> HALF_WORD).astype(jnp.float32)

    for top in range(0, rows, ROWS):
        here = slice(top, top + ROWS)
        span = slice(start + top, start + top + ROWS)
        back = flips[span, :] == 1

        def group_step(step, _):
            for tile in range(GROUP):
                cols = pl.ds(pl.multiple_of((step * GROUP + tile) * LANES, LANES), LANES)
                labels = [sorted_bins[d, here, cols] for d in range(total)]
                second = [look(entries[1], labels[d]) for d in range(total)]
                sums = [jnp.zeros((ROWS, LANES), jnp.float32)]
                for d in range(total):
                    sums.append(sums[-1] + high_part(second[d]) * ordered[d, span, cols])
                whole = sums[-1]
                through = [jnp.exp(-jnp.where(back, whole - s, s)) for s in sums]
                colour = [jnp.zeros((ROWS, LANES), jnp.float32) for _ in range(3)]
                for d in range(total):
                    weight = jnp.abs(through[d] - through[d + 1]) * shading[d, span, cols]
                    first = look(entries[0], labels[d])
                    colour[0] = colour[0] + weight * low_part(first)
                    colour[1] = colour[1] + weight * high_part(first)
                    colour[2] = colour[2] + weight * low_part(second[d])
                for c in range(3):
                    result[c, here, cols] = colour[c]
                result[3, here, cols] = 1.0 - jnp.exp(-whole)
            copy(top, step).start()
            return 0

        lax.fori_loop(0, groups, group_step, 0)

    for top in range(0, rows, ROWS):
        for step in range(groups):
            copy(top, step).wait()


def shards(field, bins, table, march_order):
    depth, height, width = field.shape
    count = lax.axis_size("gz")
    rank = lax.axis_index("gz").astype(jnp.int32)
    side = lax.axis_index("sx").astype(jnp.int32)
    place = jnp.stack([rank, side])
    rows = height // count
    total = count * depth
    cuts = [(0, ROWS)]
    if rows > 2 * ROWS:
        cuts.append((ROWS, rows - 2 * ROWS))
    if rows > ROWS:
        cuts.append((rows - ROWS, ROWS))
    partners = sorted(range(1, count), key=lambda slot: (-slot.bit_count(), slot))

    def piece(array, slot, start, size):
        return lax.dynamic_slice_in_dim(array, (rank ^ slot) * rows + start, size, axis=1)

    def after(array, *others):
        return lax.optimization_barrier((array, *others))[0]

    own_field = piece(field, 0, 0, rows)
    field_bricks = {0: own_field}
    source = field
    for slot in partners:
        cut = piece(source, slot, 0, rows)
        source = after(field, cut)
        field_bricks[slot] = partner(cut, "gz", slot)

    forward = [(i, i + 1) for i in range(lax.axis_size("sy") - 1)]
    backward = [(target, origin) for origin, target in forward]
    above = lax.ppermute(source[:, height - 1], "sy", forward)
    below = lax.ppermute(source[:, 0], "sy", backward)

    half = width // 2
    edge_rows = 4 * depth
    message_rows = edge_rows + 2 * depth * ROWS
    messages = pl.pallas_call(
        functools.partial(pack_kernel, count, depth),
        out_shape=[
            jax.ShapeDtypeStruct((message_rows if slot else edge_rows, half), jnp.float32) for slot in range(count)
        ],
        in_specs=[smem, vmem, vmem, anywhere, anywhere],
        out_specs=[vmem] * count,
        scratch_shapes=[
            pltpu.VMEM((count, depth, ROWS, width), jnp.float32),
            pltpu.VMEM((count, depth, ROWS, width), jnp.float32),
            pltpu.VMEM((count, depth, ROWS, width), jnp.int32),
            pltpu.SemaphoreType.DMA((count, 3)),
        ],
        compiler_params=pltpu.CompilerParams(vmem_limit_bytes=VMEM_LIMIT),
        cost_estimate=pl.CostEstimate(flops=0, bytes_accessed=8 * count * message_rows * half, transcendentals=0),
        name="pack",
    )(place, above, below, field, bins)
    later_bins = after(bins, *messages)
    arrived = {0: messages[0]}
    for slot in partners:
        arrived[slot] = partner(messages[slot], "gz", slot)

    bins_bricks = [[piece(bins, 0, *cuts[0])] + [arrived[slot] for slot in range(1, count)]]
    for start, size in cuts[1:]:
        own = piece(bins, 0, start, size)
        bricks = {0: own}
        cut = [piece(later_bins, slot, start, size) for slot in partners]
        later_bins = after(bins, *cut)
        for slot, sent in zip(partners, cut):
            bricks[slot] = partner(sent, "gz", slot)
        bins_bricks.append([bricks[slot] for slot in range(count)])

    edge_column = (1 - side) * (width - LANES)
    slab = jnp.concatenate(
        [lax.dynamic_slice_in_dim(field_bricks[slot], edge_column, LANES, axis=2) for slot in range(count)], axis=0
    )
    beside = partner(slab, "sx", 1)

    cells = total * rows * width
    planes = jax.ShapeDtypeStruct((total, rows, width), jnp.float32)
    ordered, shading = pl.pallas_call(
        functools.partial(shade_kernel, count, depth),
        out_shape=(planes, planes),
        in_specs=[smem] + [vmem] * (2 * count + 1),
        out_specs=(vmem, vmem),
        scratch_shapes=[pltpu.VMEM((total + 2, rows + 2 * ROWS, width + 2 * LANES), jnp.float32)],
        compiler_params=pltpu.CompilerParams(vmem_limit_bytes=VMEM_LIMIT),
        cost_estimate=pl.CostEstimate(flops=20 * cells, bytes_accessed=16 * cells, transcendentals=cells),
        name="shade",
    )(place, *[field_bricks[slot] for slot in range(count)], *[arrived[slot] for slot in range(count)], beside)

    flips = lax.dynamic_slice_in_dim(march_order, rank * rows, rows, axis=0)
    flips = jnp.broadcast_to(flips[:, None], (rows, LANES))
    colours = (table[:3].astype(jnp.float32) * (1.0 / COLOUR_UNIT)).astype(jnp.int32)
    opacity = (table[3].astype(jnp.float32) * (1.0 / OPACITY_UNIT)).astype(jnp.int32)
    entries = jnp.stack([colours[0] | colours[1] << HALF_WORD, colours[2] | opacity << HALF_WORD])
    entries = jnp.broadcast_to(entries[:, None, :], (2, ROWS, table.shape[1]))

    image = None
    for index, ((start, size), bricks) in enumerate(zip(cuts, bins_bricks)):
        operands = [place, entries, flips, ordered, shading, *bricks]
        in_specs = [smem] + [vmem] * (len(operands) - 1)
        aliases = {}
        if image is not None:
            in_specs.append(anywhere)
            aliases = {len(operands): 0}
            operands.append(image)
        cells = total * size * width
        image = pl.pallas_call(
            functools.partial(blend_kernel, count, depth, start, index == 0),
            out_shape=jax.ShapeDtypeStruct((4, rows, width), jnp.float32),
            in_specs=in_specs,
            out_specs=anywhere,
            scratch_shapes=[
                pltpu.VMEM((total, size, width), jnp.int32),
                pltpu.VMEM((4, size, width), jnp.float32),
                pltpu.SemaphoreType.DMA((size // ROWS, width // (GROUP * LANES))),
            ],
            input_output_aliases=aliases,
            compiler_params=pltpu.CompilerParams(vmem_limit_bytes=VMEM_LIMIT),
            cost_estimate=pl.CostEstimate(flops=20 * cells, bytes_accessed=16 * cells, transcendentals=cells),
            name="blend",
        )(*operands)
    return image


def solution(mesh):
    placed = (P("gz", "sy", "sx"), P("gz", "sy", "sx"), P(), P("sy"))
    return jax.shard_map(
        shards, mesh=mesh, in_specs=placed, out_specs=P(None, ("sy", "gz"), "sx"), check_vma=False
    )
```

time: 79.5 us -> 59.3 us (0.75)
  waiting for transfers between devices: 18 us -> 6.45 us
  Pallas kernels: 24 us -> 13.9 us
  starting transfers between devices: 21.5 us -> 23 us
    ppermute x13, waiting for transfers between devices: 18 us -> 6.45 us  [partner(): lax.ppermute(x, axis, [(i, i ^ distance) for i in range(lax.axis_size(axi...]
    pallas_call x1, Pallas kernels: 11.9 us -> 4.17 us  [shards(): pl.pallas_call(functools.partial(shade_kernel, count, depth), out_shape=(...]
    slice x3 -> x0, local copies, waits for them, and re-layouts: 5.76 us -> none  [the longest x1 2.1 us: shards(): tops = jnp.concatenate([above, field[:, rows - 1:height - 1:rows]], axis=1)]
    pallas_call x2 -> x4, Pallas kernels: 12.1 us -> 9.69 us  [the longest x3 7.81 us: shards(): pl.pallas_call(functools.partial(blend_kernel, count, depth, start, index...]
    unnamed x8 -> x18, local copies, waits for them, and re-layouts: 0.07 us -> 2.23 us
    concatenate x2 -> x1, other arithmetic: 1.72 us -> 0.01 us  [shards(): jnp.concatenate([lax.dynamic_slice_in_dim(field_bricks[slot], edge_column...]
    optimization_barrier x0 -> x1, local copies, waits for them, and re-layouts: none -> 1.62 us  [after(): return lax.optimization_barrier((array, *others))[0]]
    ppermute x13, starting transfers between devices: 16.3 us -> 17.7 us  [partner(): lax.ppermute(x, axis, [(i, i ^ distance) for i in range(lax.axis_size(axi...]
  transfers between devices with their start and end apart: 15 -> 15, of which waited for: 3 -> 3; matrix products, arithmetic and copies ran while one was open for 16% -> 18% of each run, Pallas kernels for 26% -> 20%
where the time goes in v2:
time: 59.3 us; the launch traced here: 58.8 us
  starting transfers between devices  23 us (39%)
  Pallas kernels  13.9 us (23%)
  local copies, waits for them, and re-layouts  13.4 us (23%)
  waiting for transfers between devices  6.45 us (11%)
  other arithmetic  1.89 us (3%)
    ppermute x13, starting transfers between devices, partner(): lax.ppermute(x, axis, [(i, i ^ distance) for i in range(lax.axis_size(axi...  17.7 us
    pallas_call x3, Pallas kernels, shards(): pl.pallas_call(functools.partial(blend_kernel, count, depth, start, index...  7.81 us
    dynamic_slice x7, local copies, waits for them, and re-layouts, piece(): lax.dynamic_slice_in_dim(array, (rank ^ slot) * rows + start, size, axis=1)  6.61 us
    ppermute x13, waiting for transfers between devices, partner(): lax.ppermute(x, axis, [(i, i ^ distance) for i in range(lax.axis_size(axi...  6.45 us
    pallas_call x1, Pallas kernels, shards(): pl.pallas_call(functools.partial(shade_kernel, count, depth), out_shape=(...  4.17 us
    ppermute x1, starting transfers between devices, shards(): above = lax.ppermute(source[:, height - 1], 'sy', forward)  3.94 us
    unnamed x18, local copies, waits for them, and re-layouts  2.23 us
    dynamic_slice x4, local copies, waits for them, and re-layouts, shards(): lax.dynamic_slice_in_dim(field_bricks[slot], edge_column, LANES, axis=2)  2.21 us
  transfers between devices with their start and end apart: 15, of which 3 were waited for; matrix products, arithmetic and copies ran while one was open for 18% of the time, Pallas kernels for 20%

profile of v2, /device:TPU:0, one launch (start us, length us, event | category | flops | bytes accessed | tf_op | source)
XLA Modules:
  0.0 58.8 jit_solution(9123794338810747501)
XLA Ops:
  0.0 2.2 %constant_dynamic-slice_fusion.15 = (f32[2,32,2048]{2,1,0:T(8,128)}, f32[2,32,2048]{2,1,0:T(8,128)S(1)}) fusion(f32[2,128,2048]{2,1,0:T(8,128)} %field.1, s32[]{:T(128)S(6)} %select_n.49, s32[]{:T(128)S(6)} %select_n.48), kind=kLoop, calls=%fused_computation.18 | loop fusion | bytes 2097160 | tf_op jit(solution)/shard_map/dynamic_slice | solution.py:214
  2.2 3.9 %collective-permute-start.2 = (f32[2,32,2048]{2,1,0:T(8,128)}, f32[2,32,2048]{2,1,0:T(8,128)S(1)}, u32[]{:S(2)}, u32[]{:S(2)}) collective-permute-start(f32[2,32,2048]{2,1,0:T(8,128)} %get-tuple-element.37), channel_id=1, source_target_pairs={{0,3},{1,2},{2,1},{3,0},{4,7},{5,6},{6,5},{7,4},{8,11},{9,10},{10,... | collective-permute-start | bytes 1572872 | tf_op jit(solution)/shard_map/ppermute | solution.py:27
  6.1 0.8 %constant_dynamic-slice_fusion.14 = f32[2,32,2048]{2,1,0:T(8,128)} fusion(f32[2,128,2048]{2,1,0:T(8,128)S(1)} %copy-done, s32[]{:T(128)S(6)} %select_n.50), kind=kLoop, calls=%fused_computation.17 | loop fusion | bytes 1048580 | tf_op jit(solution)/shard_map/dynamic_slice | solution.py:214
  8.4 1.6 %copy.7 = f32[2,128,2048]{2,0,1:T(2,128)S(1)} copy(f32[2,128,2048]{2,1,0:T(8,128)S(1)} %copy-done) | data formatting | bytes 4194304 | tf_op jit(solution)/shard_map/optimization_barrier | solution.py:217
  10.6 3.9 %collective-permute-start.3 = (f32[2,2048]{1,0:T(2,128)}, f32[2,2048]{1,0:T(2,128)S(1)}, u32[]{:S(2)}, u32[]{:S(2)}) collective-permute-start(f32[2,2048]{1,0:T(2,128)} %get-tuple-element.36), channel_id=1, source_target_pairs={{0,4},{4,8},{8,12},{1,5},{5,9},{9,13},{2,6},{6,10},{10,14},{3,7},{... | collective-permute-start | bytes 49160 | tf_op jit(solution)/shard_map/ppermute | solution.py:229
  14.6 1.3 %collective-permute-start.4 = (f32[2,2048]{1,0:T(2,128)}, f32[2,2048]{1,0:T(2,128)}, u32[]{:S(2)}, u32[]{:S(2)}) collective-permute-start(f32[2,2048]{1,0:T(2,128)} %get-tuple-element.35), channel_id=1, source_target_pairs={{4,0},{8,4},{12,8},{5,1},{9,5},{13,9},{6,2},{10,6},{14,10},{7,3},{... | collective-permute-start | bytes 49160 | tf_op jit(solution)/shard_map/ppermute | solution.py:230
  15.9 1.6 %constant_dynamic-slice_fusion = (s32[2,8,2048]{2,1,0:T(8,128)}, s32[2,8,2048]{2,1,0:T(8,128)S(1)}) fusion(s32[2,128,2048]{2,1,0:T(8,128)} %bins.1, s32[]{:T(128)S(6)} %select_n.48, s32[]{:T(128)S(6)} %select_n.55), kind=kLoop, calls=%fused_computation.3 | loop fusion | bytes 524296 | tf_op jit(solution)/shard_map/dynamic_slice | solution.py:214
  17.5 1.0 %constant_dynamic-slice_fusion.1.refs_0_ = s32[2,16,2048]{2,1,0:T(8,128)S(1)} fusion(s32[2,128,2048]{2,1,0:T(8,128)} %bins.1, s32[]{:T(128)S(6)} %select_n.62), kind=kLoop, calls=%fused_computation.4 | loop fusion | bytes 524292 | tf_op jit(solution)/shard_map/dynamic_slice | solution.py:214
  18.5 1.3 %multiply_convert_fusion = s32[3,128]{1,0:T(4,128)} fusion(bf16[4,128]{1,0:T(4,128)(2,1)} %param.6), kind=kLoop, calls=%fused_computation.20 | loop fusion | flops 1152 | bytes 2304 | tf_op jit(solution)/shard_map/convert_element_type | solution.py:288
  21.0 1.6 %copy-done.1 = s32[2,128,2048]{2,1,0:T(8,128)S(1)} copy-done((s32[2,128,2048]{2,1,0:T(8,128)S(1)}, s32[2,128,2048]{2,1,0:T(8,128)}, u32[]{:S(2)}) %copy-start.1) | copy-done | bytes 2097176
  23.2 1.9 %pack.1 = (f32[8,1024]{1,0:T(8,128)S(1)}, f32[40,1024]{1,0:T(8,128)S(1)}, f32[40,1024]{1,0:T(8,128)S(1)}, f32[40,1024]{1,0:T(8,128)S(1)}) custom-call(s32[2]{0:T(128)S(1)} %copy-done.3, f32[2,2048]{1,0:T(2,128)S(1)} %collective-permute-done.3.above, f32[2,2048]{1,0:T(2,128)} %collective-permute-done.4.below, f32[2,128,2048]{2,1,0:T(8,128)S(1)} %copy-done, ...), custom_call_target="tpu_custom_call" | custom-call | bytes 1310720 | tf_op jit(solution)/shard_map/pack/pallas_call | solution.py:235
  25.2 1.6 %collective-permute-start.5 = (f32[40,1024]{1,0:T(8,128)S(1)}, f32[40,1024]{1,0:T(8,128)S(1)}, u32[]{:S(2)}, u32[]{:S(2)}) collective-permute-start(f32[40,1024]{1,0:T(8,128)S(1)} %get-tuple-element.20), channel_id=1, source_target_pairs={{0,1},{1,0},{2,3},{3,2},{4,5},{5,4},{6,7},{7,6},{8,9},{9,8},{10,11... | collective-permute-start | bytes 491528 | tf_op jit(solution)/shard_map/ppermute | solution.py:27
  26.7 1.5 %collective-permute-start.6 = (f32[40,1024]{1,0:T(8,128)S(1)}, f32[40,1024]{1,0:T(8,128)S(1)}, u32[]{:S(2)}, u32[]{:S(2)}) collective-permute-start(f32[40,1024]{1,0:T(8,128)S(1)} %get-tuple-element.21), channel_id=1, source_target_pairs={{0,2},{1,3},{2,0},{3,1},{4,6},{5,7},{6,4},{7,5},{8,10},{9,11},{10,... | collective-permute-start | bytes 491528 | tf_op jit(solution)/shard_map/ppermute | solution.py:27
  28.9 0.8 %collective-permute-done.1.refs_2_ = f32[2,32,2048]{2,1,0:T(8,128)} collective-permute-done((f32[2,32,2048]{2,1,0:T(8,128)}, f32[2,32,2048]{2,1,0:T(8,128)}, u32[]{:S(2)}, u32[]{:S(2)}) %collective-permute-start.1) | collective-permute-done | bytes 524320 | tf_op jit(solution)/shard_map/ppermute | solution.py:27
  29.7 1.7 %collective-permute-start.12 = (s32[2,16,2048]{2,1,0:T(8,128)S(1)}, s32[2,16,2048]{2,1,0:T(8,128)S(1)}, u32[]{:S(2)}, u32[]{:S(2)}) collective-permute-start(s32[2,16,2048]{2,1,0:T(8,128)S(1)} %get-tuple-element.33), channel_id=1, source_target_pairs={{0,1},{1,0},{2,3},{3,2},{4,5},{5,4},{6,7},{7,6},{8,9},{9,8},{10,11... | collective-permute-start | bytes 786440 | tf_op jit(solution)/shard_map/ppermute | solution.py:27
  33.1 1.4 %collective-permute-done.5.refs_5_.refs_1_ = f32[40,1024]{1,0:T(8,128)S(1)} collective-permute-done((f32[40,1024]{1,0:T(8,128)S(1)}, f32[40,1024]{1,0:T(8,128)S(1)}, u32[]{:S(2)}, u32[]{:S(2)}) %collective-permute-start.5) | collective-permute-done | bytes 163872 | tf_op jit(solution)/shard_map/ppermute | solution.py:27
  34.7 2.8 %collective-permute-start.14 = (s32[2,16,2048]{2,1,0:T(8,128)S(1)}, s32[2,16,2048]{2,1,0:T(8,128)S(1)}, u32[]{:S(2)}, u32[]{:S(2)}) collective-permute-start(s32[2,16,2048]{2,1,0:T(8,128)S(1)} %get-tuple-element.34), channel_id=1, source_target_pairs={{0,3},{1,2},{2,1},{3,0},{4,7},{5,6},{6,5},{7,4},{8,11},{9,10},{10,... | collective-permute-start | bytes 786440 | tf_op jit(solution)/shard_map/ppermute | solution.py:27
  37.4 2.0 %collective-permute-start.9 = (s32[2,8,2048]{2,1,0:T(8,128)S(1)}, s32[2,8,2048]{2,1,0:T(8,128)S(1)}, u32[]{:S(2)}, u32[]{:S(2)}) collective-permute-start(s32[2,8,2048]{2,1,0:T(8,128)S(1)} %get-tuple-element.31), channel_id=1, source_target_pairs={{0,1},{1,0},{2,3},{3,2},{4,5},{5,4},{6,7},{7,6},{8,9},{9,8},{10,11... | collective-permute-start | bytes 393224 | tf_op jit(solution)/shard_map/ppermute | solution.py:27
  39.4 4.2 %collective-permute-done.12.refs_1_ = s32[2,16,2048]{2,1,0:T(8,128)S(1)} collective-permute-done((s32[2,16,2048]{2,1,0:T(8,128)S(1)}, s32[2,16,2048]{2,1,0:T(8,128)S(1)}, u32[]{:S(2)}, u32[]{:S(2)}) %collective-permute-start.12) | collective-permute-done | bytes 262176 | tf_op jit(solution)/shard_map/ppermute | solution.py:27
  43.6 3.0 %collective-permute-start.11 = (s32[2,8,2048]{2,1,0:T(8,128)S(1)}, s32[2,8,2048]{2,1,0:T(8,128)S(1)}, u32[]{:S(2)}, u32[]{:S(2)}) collective-permute-start(s32[2,8,2048]{2,1,0:T(8,128)S(1)} %get-tuple-element.29), channel_id=1, source_target_pairs={{0,3},{1,2},{2,1},{3,0},{4,7},{5,6},{6,5},{7,4},{8,11},{9,10},{10,... | collective-permute-start | bytes 393224 | tf_op jit(solution)/shard_map/ppermute | solution.py:27
  46.7 4.2 %shade.1 = (f32[8,32,2048]{2,1,0:T(8,128)S(1)}, f32[8,32,2048]{2,1,0:T(8,128)S(1)}) custom-call(s32[2]{0:T(128)S(1)} %copy-done.4, f32[2,32,2048]{2,1,0:T(8,128)S(1)} %get-tuple-element.38.refs_0_, f32[2,32,2048]{2,1,0:T(8,128)} %collective-permute-done.refs_1_, f32[2,32,2048]{2,1,0:T(8,128)} %collective-permute-done.1.refs_2_, ...), custom_call_target="tpu_custom_call" | custom-call | flops 10485760 | bytes 8388608 | tf_op jit(solution)/shard_map/shade/pallas_call | solution.py:275
  50.9 2.2 %blend.3.refs_4_ = f32[4,32,2048]{2,1,0:T(8,128)} custom-call(s32[2]{0:T(128)S(1)} %copy-done.4, s32[2,8,128]{2,1,0:T(8,128)S(1)} %broadcast_in_dim.4.table, s32[32,128]{1,0:T(8,128)S(1)} %broadcast_in_dim.5.flips, f32[8,32,2048]{2,1,0:T(8,128)S(1)} %get-tuple-element.23.ordered, f32[8,32,2048]{2,1,0:T(8,128)S(1)} %get-tuple-element.24.shading, ...), custom_call_target="tpu_custom_call" | custom-call | flops 2621440 | bytes 2097152 | tf_op jit(solution)/shard_map/blend/pallas_call | solution.py:303
  53.2 3.3 %blend.4.refs_4_ = f32[4,32,2048]{2,1,0:T(8,128)} custom-call(s32[2]{0:T(128)S(1)} %copy-done.4, s32[2,8,128]{2,1,0:T(8,128)S(1)} %broadcast_in_dim.4.table, s32[32,128]{1,0:T(8,128)S(1)} %broadcast_in_dim.5.flips, f32[8,32,2048]{2,1,0:T(8,128)S(1)} %get-tuple-element.23.ordered, ...), custom_call_target="tpu_custom_call", output_to_operand_aliasing={{}: (9, {})} | custom-call | flops 5242880 | bytes 4194304 | tf_op jit(solution)/shard_map/blend/pallas_call | solution.py:303
  56.6 2.2 %blend.5 = f32[4,32,2048]{2,1,0:T(8,128)} custom-call(s32[2]{0:T(128)S(1)} %copy-done.4, s32[2,8,128]{2,1,0:T(8,128)S(1)} %broadcast_in_dim.4.table, s32[32,128]{1,0:T(8,128)S(1)} %broadcast_in_dim.5.flips, f32[8,32,2048]{2,1,0:T(8,128)S(1)} %get-tuple-element.23.ordered, ...), custom_call_target="tpu_custom_call", output_to_operand_aliasing={{}: (9, {})} | custom-call | flops 2621440 | bytes 2097152 | tf_op jit(solution)/shard_map/blend/pallas_call | solution.py:303
  (50 shorter events, 6.6 us)
Async XLA Ops:
  0.0 6.1 %copy-start = (f32[2,128,2048]{2,1,0:T(8,128)S(1)}, f32[2,128,2048]{2,1,0:T(8,128)}, u32[]{:S(2)}) copy-start(f32[2,128,2048]{2,1,0:T(8,128)} %field.1) | copy-start | bytes 6291460
  2.2 26.1 %collective-permute-start.2 = (f32[2,32,2048]{2,1,0:T(8,128)}, f32[2,32,2048]{2,1,0:T(8,128)S(1)}, u32[]{:S(2)}, u32[]{:S(2)}) collective-permute-start(f32[2,32,2048]{2,1,0:T(8,128)} %get-tuple-element.37), channel_id=1, source_target_pairs={{0,3},{1,2},{2,1},{3,0},{4,7},{5,6},{6,5},{7,4},{8,11},{9,10},{10,... | collective-permute-start | bytes 1572872 | tf_op jit(solution)/shard_map/ppermute | solution.py:27
  7.0 25.2 %collective-permute-start = (f32[2,32,2048]{2,1,0:T(8,128)}, f32[2,32,2048]{2,1,0:T(8,128)}, u32[]{:S(2)}, u32[]{:S(2)}) collective-permute-start(f32[2,32,2048]{2,1,0:T(8,128)} %constant_dynamic-slice_fusion.14), channel_id=1, source_target_pairs={{0,1},{1,0},{2,3},{3,2},{4,5},{5,4},{6,7},{7,6},{8,9},{9,8},{10,11... | collective-permute-start | bytes 1572872 | tf_op jit(solution)/shard_map/ppermute | solution.py:27
  8.4 21.3 %collective-permute-start.1 = (f32[2,32,2048]{2,1,0:T(8,128)}, f32[2,32,2048]{2,1,0:T(8,128)}, u32[]{:S(2)}, u32[]{:S(2)}) collective-permute-start(f32[2,32,2048]{2,1,0:T(8,128)} %constant_dynamic-slice_fusion.13), channel_id=1, source_target_pairs={{0,2},{1,3},{2,0},{3,1},{4,6},{5,7},{6,4},{7,5},{8,10},{9,11},{10,... | collective-permute-start | bytes 1572872 | tf_op jit(solution)/shard_map/ppermute | solution.py:27
  10.6 10.4 %collective-permute-start.3 = (f32[2,2048]{1,0:T(2,128)}, f32[2,2048]{1,0:T(2,128)S(1)}, u32[]{:S(2)}, u32[]{:S(2)}) collective-permute-start(f32[2,2048]{1,0:T(2,128)} %get-tuple-element.36), channel_id=1, source_target_pairs={{0,4},{4,8},{8,12},{1,5},{5,9},{9,13},{2,6},{6,10},{10,14},{3,7},{... | collective-permute-start | bytes 49160 | tf_op jit(solution)/shard_map/ppermute | solution.py:229
  14.6 6.5 %collective-permute-start.4 = (f32[2,2048]{1,0:T(2,128)}, f32[2,2048]{1,0:T(2,128)}, u32[]{:S(2)}, u32[]{:S(2)}) collective-permute-start(f32[2,2048]{1,0:T(2,128)} %get-tuple-element.35), channel_id=1, source_target_pairs={{4,0},{8,4},{12,8},{5,1},{9,5},{13,9},{6,2},{10,6},{14,10},{7,3},{... | collective-permute-start | bytes 49160 | tf_op jit(solution)/shard_map/ppermute | solution.py:230
  21.0 1.6 %copy-start.1 = (s32[2,128,2048]{2,1,0:T(8,128)S(1)}, s32[2,128,2048]{2,1,0:T(8,128)}, u32[]{:S(2)}) copy-start(s32[2,128,2048]{2,1,0:T(8,128)} %bins.1) | copy-start | bytes 6291460
  22.6 0.6 %copy-start.3 = (s32[2]{0:T(128)S(1)}, s32[2]{0:T(128)}, u32[]{:S(2)}) copy-start(s32[2]{0:T(128)} %pad_add_fusion.1.place) | copy-start | bytes 28
  23.2 9.7 %copy-start.5 = (f32[2,32,128]{2,1,0:T(8,128)S(1)}, f32[2,32,128]{2,1,0:T(8,128)}, u32[]{:S(2)}) copy-start(f32[2,32,128]{2,1,0:T(8,128)} %constant_dynamic-slice_fusion.12) | copy-start | bytes 98308
  25.1 21.4 %copy-start.6 = (s32[3,128]{1,0:T(4,128)S(1)}, s32[3,128]{1,0:T(4,128)}, u32[]{:S(2)}) copy-start(s32[3,128]{1,0:T(4,128)} %multiply_convert_fusion) | copy-start | bytes 4612
  25.1 21.4 %copy-start.7 = (bf16[4,128]{1,0:T(4,128)(2,1)S(1)}, bf16[4,128]{1,0:T(4,128)(2,1)}, u32[]{:S(2)}) copy-start(bf16[4,128]{1,0:T(4,128)(2,1)} %param.6) | copy-start | bytes 3076
  25.1 21.4 %copy-start.8 = (s32[128]{0:T(128)S(1)}, s32[128]{0:T(128)}, u32[]{:S(2)}) copy-start(s32[128]{0:T(128)} %param.7) | copy-start | bytes 1540
  25.1 21.5 %copy-start.4 = (s32[2]{0:T(128)S(1)}, s32[2]{0:T(128)}, u32[]{:S(2)}) copy-start(s32[2]{0:T(128)} %pad_add_fusion.1.place) | copy-start | bytes 28
  25.2 9.3 %collective-permute-start.5 = (f32[40,1024]{1,0:T(8,128)S(1)}, f32[40,1024]{1,0:T(8,128)S(1)}, u32[]{:S(2)}, u32[]{:S(2)}) collective-permute-start(f32[40,1024]{1,0:T(8,128)S(1)} %get-tuple-element.20), channel_id=1, source_target_pairs={{0,1},{1,0},{2,3},{3,2},{4,5},{5,4},{6,7},{7,6},{8,9},{9,8},{10,11... | collective-permute-start | bytes 491528 | tf_op jit(solution)/shard_map/ppermute | solution.py:27
  26.7 7.9 %collective-permute-start.6 = (f32[40,1024]{1,0:T(8,128)S(1)}, f32[40,1024]{1,0:T(8,128)S(1)}, u32[]{:S(2)}, u32[]{:S(2)}) collective-permute-start(f32[40,1024]{1,0:T(8,128)S(1)} %get-tuple-element.21), channel_id=1, source_target_pairs={{0,2},{1,3},{2,0},{3,1},{4,6},{5,7},{6,4},{7,5},{8,10},{9,11},{10,... | collective-permute-start | bytes 491528 | tf_op jit(solution)/shard_map/ppermute | solution.py:27
  28.3 22.6 %copy-start.2 = (s32[2,8,2048]{2,1,0:T(8,128)S(1)}, s32[2,8,2048]{2,1,0:T(8,128)}, u32[]{:S(2)}) copy-start(s32[2,8,2048]{2,1,0:T(8,128)} %get-tuple-element.27.refs_0_) | copy-start | bytes 393220
  28.3 9.1 %collective-permute-start.7 = (f32[40,1024]{1,0:T(8,128)S(1)}, f32[40,1024]{1,0:T(8,128)S(1)}, u32[]{:S(2)}, u32[]{:S(2)}) collective-permute-start(f32[40,1024]{1,0:T(8,128)S(1)} %get-tuple-element.22), channel_id=1, source_target_pairs={{0,3},{1,2},{2,1},{3,0},{4,7},{5,6},{6,5},{7,4},{8,11},{9,10},{10,... | collective-permute-start | bytes 491528 | tf_op jit(solution)/shard_map/ppermute | solution.py:27
  29.7 13.9 %collective-permute-start.12 = (s32[2,16,2048]{2,1,0:T(8,128)S(1)}, s32[2,16,2048]{2,1,0:T(8,128)S(1)}, u32[]{:S(2)}, u32[]{:S(2)}) collective-permute-start(s32[2,16,2048]{2,1,0:T(8,128)S(1)} %get-tuple-element.33), channel_id=1, source_target_pairs={{0,1},{1,0},{2,3},{3,2},{4,5},{5,4},{6,7},{7,6},{8,9},{9,8},{10,11... | collective-permute-start | bytes 786440 | tf_op jit(solution)/shard_map/ppermute | solution.py:27
  32.9 10.7 %collective-permute-start.8 = (f32[8,32,128]{2,1,0:T(8,128)S(1)}, f32[8,32,128]{2,1,0:T(8,128)S(1)}, u32[]{:S(2)}, u32[]{:S(2)}) collective-permute-start(f32[8,32,128]{2,1,0:T(8,128)S(1)} %pad_maximum_fusion), channel_id=1, source_target_pairs={{0,16},{16,0},{1,17},{17,1},{2,18},{18,2},{3,19},{19,3},{4,20},{20... | collective-permute-start | bytes 393224 | tf_op jit(solution)/shard_map/ppermute | solution.py:27
  34.5 18.7 %collective-permute-start.13 = (s32[2,16,2048]{2,1,0:T(8,128)S(1)}, s32[2,16,2048]{2,1,0:T(8,128)S(1)}, u32[]{:S(2)}, u32[]{:S(2)}) collective-permute-start(s32[2,16,2048]{2,1,0:T(8,128)S(1)} %get-tuple-element.32), channel_id=1, source_target_pairs={{0,2},{1,3},{2,0},{3,1},{4,6},{5,7},{6,4},{7,5},{8,10},{9,11},{10,... | collective-permute-start | bytes 786440 | tf_op jit(solution)/shard_map/ppermute | solution.py:27
  34.7 18.5 %collective-permute-start.14 = (s32[2,16,2048]{2,1,0:T(8,128)S(1)}, s32[2,16,2048]{2,1,0:T(8,128)S(1)}, u32[]{:S(2)}, u32[]{:S(2)}) collective-permute-start(s32[2,16,2048]{2,1,0:T(8,128)S(1)} %get-tuple-element.34), channel_id=1, source_target_pairs={{0,3},{1,2},{2,1},{3,0},{4,7},{5,6},{6,5},{7,4},{8,11},{9,10},{10,... | collective-permute-start | bytes 786440 | tf_op jit(solution)/shard_map/ppermute | solution.py:27
  37.4 19.1 %collective-permute-start.9 = (s32[2,8,2048]{2,1,0:T(8,128)S(1)}, s32[2,8,2048]{2,1,0:T(8,128)S(1)}, u32[]{:S(2)}, u32[]{:S(2)}) collective-permute-start(s32[2,8,2048]{2,1,0:T(8,128)S(1)} %get-tuple-element.31), channel_id=1, source_target_pairs={{0,1},{1,0},{2,3},{3,2},{4,5},{5,4},{6,7},{7,6},{8,9},{9,8},{10,11... | collective-permute-start | bytes 393224 | tf_op jit(solution)/shard_map/ppermute | solution.py:27
  43.6 13.0 %collective-permute-start.10 = (s32[2,8,2048]{2,1,0:T(8,128)S(1)}, s32[2,8,2048]{2,1,0:T(8,128)S(1)}, u32[]{:S(2)}, u32[]{:S(2)}) collective-permute-start(s32[2,8,2048]{2,1,0:T(8,128)S(1)} %get-tuple-element.30), channel_id=1, source_target_pairs={{0,2},{1,3},{2,0},{3,1},{4,6},{5,7},{6,4},{7,5},{8,10},{9,11},{10,... | collective-permute-start | bytes 393224 | tf_op jit(solution)/shard_map/ppermute | solution.py:27
  43.6 13.0 %collective-permute-start.11 = (s32[2,8,2048]{2,1,0:T(8,128)S(1)}, s32[2,8,2048]{2,1,0:T(8,128)S(1)}, u32[]{:S(2)}, u32[]{:S(2)}) collective-permute-start(s32[2,8,2048]{2,1,0:T(8,128)S(1)} %get-tuple-element.29), channel_id=1, source_target_pairs={{0,3},{1,2},{2,1},{3,0},{4,7},{5,6},{6,5},{7,4},{8,11},{9,10},{10,... | collective-permute-start | bytes 393224 | tf_op jit(solution)/shard_map/ppermute | solution.py:27

commit v3 on v2

--- a/solution.py
+++ b/solution.py
@@ -19,21 +19,42 @@
 VMEM_LIMIT = 40 * 1024 * 1024
 
 vmem = pl.BlockSpec(memory_space=pltpu.VMEM)
-smem = pl.BlockSpec(memory_space=pltpu.SMEM)
-anywhere = pl.BlockSpec(memory_space=pl.ANY)
+hbm = pl.BlockSpec(memory_space=pltpu.HBM)
 
 
 def partner(x, axis, distance):
     return lax.ppermute(x, axis, [(i, i ^ distance) for i in range(lax.axis_size(axis))])
 
 
-def pack_kernel(count, depth, place, above, below, field, bins, *refs):
+def split_kernel(count, depth, slots, field, *refs):
+    pieces = refs[: len(slots)]
+    last, first, ends, sems = refs[len(slots) :]
+    height = field.shape[1]
+    rows = height // count
+    rank = lax.axis_index("gz")
+    moves = [
+        pltpu.make_async_copy(field.at[:, height - ROWS :], ends.at[0], sems.at[0]),
+        pltpu.make_async_copy(field.at[:, :ROWS], ends.at[1], sems.at[1]),
+    ]
+    for index, slot in enumerate(slots):
+        start = pl.multiple_of((rank ^ slot) * rows, ROWS)
+        moves.append(pltpu.make_async_copy(field.at[:, pl.ds(start, rows)], pieces[index], sems.at[2 + index]))
+    for move in moves:
+        move.start()
+    for move in moves:
+        move.wait()
+    for j in range(depth):
+        last[j : j + 1, :] = ends[0, j, ROWS - 1 :, :]
+        first[j : j + 1, :] = ends[1, j, :1, :]
+
+
+def pack_kernel(count, depth, above, below, field, bins, *refs):
     messages = refs[:count]
     high, low, labels, sems = refs[count:]
     height, width = field.shape[1:]
     rows = height // count
     half = width // 2
-    rank = place[0]
+    rank = lax.axis_index("gz")
     copies = []
     for slot in range(count):
         target = rank ^ slot
@@ -66,7 +87,7 @@
                     messages[slot][first : first + ROWS, :] = labels[slot, j, :, cols].astype(jnp.float32)
 
 
-def shade_kernel(count, depth, place, *refs):
+def shade_kernel(count, depth, *refs):
     bricks = refs[:count]
     messages = refs[count : 2 * count]
     beside = refs[2 * count]
@@ -74,8 +95,8 @@
     rows, width = ordered.shape[1:]
     half = width // 2
     total = count * depth
-    rank = place[0]
-    side = place[1]
+    rank = lax.axis_index("gz")
+    side = lax.axis_index("sx")
     inside = slice(ROWS, ROWS + rows)
     zero_plane = jnp.zeros((rows, width), jnp.float32)
     ext[0, inside, LANES : LANES + width] = zero_plane
@@ -122,13 +143,13 @@
     lax.fori_loop(0, total, plane_step, 0)
 
 
-def blend_kernel(count, depth, start, packed, place, table, flips, ordered, shading, *refs):
+def blend_kernel(count, depth, start, packed, table, flips, ordered, shading, *refs):
     bricks = refs[:count]
     image, sorted_bins, result, sems = refs[-4:]
     total = count * depth
     rows, width = result.shape[1:]
     half = width // 2
-    rank = place[0]
+    rank = lax.axis_index("gz")
     for slot in range(count):
         for j in range(depth):
             at = (rank ^ slot) * depth + j
@@ -200,7 +221,6 @@
     count = lax.axis_size("gz")
     rank = lax.axis_index("gz").astype(jnp.int32)
     side = lax.axis_index("sx").astype(jnp.int32)
-    place = jnp.stack([rank, side])
     rows = height // count
     total = count * depth
     cuts = [(0, ROWS)]
@@ -216,18 +236,27 @@
     def after(array, *others):
         return lax.optimization_barrier((array, *others))[0]
 
-    own_field = piece(field, 0, 0, rows)
-    field_bricks = {0: own_field}
-    source = field
-    for slot in partners:
-        cut = piece(source, slot, 0, rows)
-        source = after(field, cut)
-        field_bricks[slot] = partner(cut, "gz", slot)
+    lead = piece(field, partners[0], 0, rows)
+    field_bricks = {partners[0]: partner(lead, "gz", partners[0])}
+    *cut, last, first = pl.pallas_call(
+        functools.partial(split_kernel, count, depth, partners[1:]),
+        out_shape=[jax.ShapeDtypeStruct((depth, rows, width), jnp.float32)] * (count - 2)
+        + [jax.ShapeDtypeStruct((depth, width), jnp.float32)] * 2,
+        in_specs=[hbm],
+        out_specs=[vmem] * count,
+        scratch_shapes=[pltpu.VMEM((2, depth, ROWS, width), jnp.float32), pltpu.SemaphoreType.DMA((count,))],
+        compiler_params=pltpu.CompilerParams(vmem_limit_bytes=VMEM_LIMIT),
+        cost_estimate=pl.CostEstimate(flops=0, bytes_accessed=8 * count * depth * rows * width, transcendentals=0),
+        name="split",
+    )(after(field, lead))
+    for slot, sent in zip(partners[1:], cut):
+        field_bricks[slot] = partner(sent, "gz", slot)
+    field_bricks[0] = piece(after(field, *cut), 0, 0, rows)
 
     forward = [(i, i + 1) for i in range(lax.axis_size("sy") - 1)]
     backward = [(target, origin) for origin, target in forward]
-    above = lax.ppermute(source[:, height - 1], "sy", forward)
-    below = lax.ppermute(source[:, 0], "sy", backward)
+    above = lax.ppermute(last, "sy", forward)
+    below = lax.ppermute(first, "sy", backward)
 
     half = width // 2
     edge_rows = 4 * depth
@@ -237,7 +266,7 @@
         out_shape=[
             jax.ShapeDtypeStruct((message_rows if slot else edge_rows, half), jnp.float32) for slot in range(count)
         ],
-        in_specs=[smem, vmem, vmem, anywhere, anywhere],
+        in_specs=[vmem, vmem, hbm, hbm],
         out_specs=[vmem] * count,
         scratch_shapes=[
             pltpu.VMEM((count, depth, ROWS, width), jnp.float32),
@@ -248,14 +277,35 @@
         compiler_params=pltpu.CompilerParams(vmem_limit_bytes=VMEM_LIMIT),
         cost_estimate=pl.CostEstimate(flops=0, bytes_accessed=8 * count * message_rows * half, transcendentals=0),
         name="pack",
-    )(place, above, below, field, bins)
+    )(above, below, field, bins)
     later_bins = after(bins, *messages)
     arrived = {0: messages[0]}
     for slot in partners:
         arrived[slot] = partner(messages[slot], "gz", slot)
 
+    edge_column = (1 - side) * (width - LANES)
+    slab = jnp.concatenate(
+        [lax.dynamic_slice_in_dim(field_bricks[slot], edge_column, LANES, axis=2) for slot in range(count)], axis=0
+    )
+    beside = partner(slab, "sx", 1)
+
+    cells = total * rows * width
+    planes = jax.ShapeDtypeStruct((total, rows, width), jnp.float32)
+    ordered, shading = pl.pallas_call(
+        functools.partial(shade_kernel, count, depth),
+        out_shape=(planes, planes),
+        in_specs=[vmem] * (2 * count + 1),
+        out_specs=(vmem, vmem),
+        scratch_shapes=[pltpu.VMEM((total + 2, rows + 2 * ROWS, width + 2 * LANES), jnp.float32)],
+        compiler_params=pltpu.CompilerParams(vmem_limit_bytes=VMEM_LIMIT),
+        cost_estimate=pl.CostEstimate(flops=20 * cells, bytes_accessed=16 * cells, transcendentals=cells),
+        name="shade",
+    )(*[field_bricks[slot] for slot in range(count)], *[arrived[slot] for slot in range(count)], beside)
+
     bins_bricks = [[piece(bins, 0, *cuts[0])] + [arrived[slot] for slot in range(1, count)]]
-    for start, size in cuts[1:]:
+    for index, (start, size) in enumerate(cuts[1:]):
+        if index:
+            later_bins = after(later_bins, shading)
         own = piece(bins, 0, start, size)
         bricks = {0: own}
         cut = [piece(later_bins, slot, start, size) for slot in partners]
@@ -264,25 +314,6 @@
             bricks[slot] = partner(sent, "gz", slot)
         bins_bricks.append([bricks[slot] for slot in range(count)])
 
-    edge_column = (1 - side) * (width - LANES)
-    slab = jnp.concatenate(
-        [lax.dynamic_slice_in_dim(field_bricks[slot], edge_column, LANES, axis=2) for slot in range(count)], axis=0
-    )
-    beside = partner(slab, "sx", 1)
-
-    cells = total * rows * width
-    planes = jax.ShapeDtypeStruct((total, rows, width), jnp.float32)
-    ordered, shading = pl.pallas_call(
-        functools.partial(shade_kernel, count, depth),
-        out_shape=(planes, planes),
-        in_specs=[smem] + [vmem] * (2 * count + 1),
-        out_specs=(vmem, vmem),
-        scratch_shapes=[pltpu.VMEM((total + 2, rows + 2 * ROWS, width + 2 * LANES), jnp.float32)],
-        compiler_params=pltpu.CompilerParams(vmem_limit_bytes=VMEM_LIMIT),
-        cost_estimate=pl.CostEstimate(flops=20 * cells, bytes_accessed=16 * cells, transcendentals=cells),
-        name="shade",
-    )(place, *[field_bricks[slot] for slot in range(count)], *[arrived[slot] for slot in range(count)], beside)
-
     flips = lax.dynamic_slice_in_dim(march_order, rank * rows, rows, axis=0)
     flips = jnp.broadcast_to(flips[:, None], (rows, LANES))
     colours = (table[:3].astype(jnp.float32) * (1.0 / COLOUR_UNIT)).astype(jnp.int32)
@@ -292,11 +323,11 @@
 
     image = None
     for index, ((start, size), bricks) in enumerate(zip(cuts, bins_bricks)):
-        operands = [place, entries, flips, ordered, shading, *bricks]
-        in_specs = [smem] + [vmem] * (len(operands) - 1)
+        operands = [entries, flips, ordered, shading, *bricks]
+        in_specs = [vmem] * len(operands)
         aliases = {}
         if image is not None:
-            in_specs.append(anywhere)
+            in_specs.append(hbm)
             aliases = {len(operands): 0}
             operands.append(image)
         cells = total * size * width
@@ -304,7 +335,7 @@
             functools.partial(blend_kernel, count, depth, start, index == 0),
             out_shape=jax.ShapeDtypeStruct((4, rows, width), jnp.float32),
             in_specs=in_specs,
-            out_specs=anywhere,
+            out_specs=hbm,
             scratch_shapes=[
                 pltpu.VMEM((total, size, width), jnp.int32),
                 pltpu.VMEM((4, size, width), jnp.float32),

time: 59.3 us -> 55.6 us (0.938)
  other arithmetic: 1.89 us -> 0.03 us
  local copies, waits for them, and re-layouts: 13.4 us -> 12 us
  starting transfers between devices: 23 us -> 21.7 us
    unnamed x18 -> x20, local copies, waits for them, and re-layouts: 2.23 us -> 3.97 us
    pallas_call x3, Pallas kernels: 7.81 us -> 6.19 us  [shards(): pl.pallas_call(functools.partial(blend_kernel, count, depth, start, index...]
    optimization_barrier x1 -> x0, local copies, waits for them, and re-layouts: 1.62 us -> none  [after(): return lax.optimization_barrier((array, *others))[0]]
    ppermute x13, starting transfers between devices: 17.7 us -> 16.5 us  [partner(): lax.ppermute(x, axis, [(i, i ^ distance) for i in range(lax.axis_size(axi...]
    convert_element_type x1, other arithmetic: 1.27 us -> 0.01 us  [shards(): (table[:3].astype(jnp.float32) * (1.0 / COLOUR_UNIT)).astype(jnp.int32)]
    ppermute x2, waiting for transfers between devices: 0.01 us -> 1.26 us  [the longest x1 1.26 us: shards(): below = lax.ppermute(first, 'sy', backward)]
    pallas_call x0 -> x1, Pallas kernels: none -> 1.24 us  [shards(): pl.pallas_call(functools.partial(split_kernel, count, depth, partners[1:]...]
    dynamic_slice x7 -> x6, local copies, waits for them, and re-layouts: 6.61 us -> 5.66 us  [piece(): lax.dynamic_slice_in_dim(array, (rank ^ slot) * rows + start, size, axis=1)]
  transfers between devices with their start and end apart: 15 -> 15, of which waited for: 3 -> 5; matrix products, arithmetic and copies ran while one was open for 18% -> 11% of each run, Pallas kernels for 20% -> 23%
where the time goes in v3:
time: 55.6 us; the launch traced here: 55 us
  starting transfers between devices  21.7 us (39%)
  Pallas kernels  14.2 us (26%)
  local copies, waits for them, and re-layouts  12 us (22%)
  waiting for transfers between devices  6.81 us (12%)
    ppermute x13, starting transfers between devices, partner(): lax.ppermute(x, axis, [(i, i ^ distance) for i in range(lax.axis_size(axi...  16.5 us
    pallas_call x3, Pallas kernels, shards(): pl.pallas_call(functools.partial(blend_kernel, count, depth, start, index...  6.19 us
    dynamic_slice x6, local copies, waits for them, and re-layouts, piece(): lax.dynamic_slice_in_dim(array, (rank ^ slot) * rows + start, size, axis=1)  5.66 us
    ppermute x13, waiting for transfers between devices, partner(): lax.ppermute(x, axis, [(i, i ^ distance) for i in range(lax.axis_size(axi...  5.55 us
    pallas_call x1, Pallas kernels, shards(): pl.pallas_call(functools.partial(shade_kernel, count, depth), out_shape=(...  4.16 us
    unnamed x20, local copies, waits for them, and re-layouts  3.97 us
    ppermute x1, starting transfers between devices, shards(): above = lax.ppermute(last, 'sy', forward)  3.92 us
    pallas_call x1, Pallas kernels, shards(): pl.pallas_call(functools.partial(pack_kernel, count, depth), out_shape=[j...  2.64 us
  transfers between devices with their start and end apart: 15, of which 5 were waited for; matrix products, arithmetic and copies ran while one was open for 11% of the time, Pallas kernels for 23%

profile of v3, /device:TPU:0, one launch (start us, length us, event | category | flops | bytes accessed | tf_op | source)
XLA Modules:
  0.0 55.0 jit_solution(2750378177290286501)
XLA Ops:
  0.0 1.9 %constant_dynamic-slice_fusion.14 = f32[2,32,2048]{2,1,0:T(8,128)} fusion(f32[2,128,2048]{2,1,0:T(8,128)} %field.2, s32[]{:T(128)S(6)} %select_n.43), kind=kLoop, calls=%fused_computation.15 | loop fusion | bytes 1048580 | tf_op jit(solution)/shard_map/dynamic_slice | solution.py:234
  1.9 3.9 %collective-permute-start.2 = (f32[2,32,2048]{2,1,0:T(8,128)}, f32[2,32,2048]{2,1,0:T(8,128)S(1)}, u32[]{:S(2)}, u32[]{:S(2)}) collective-permute-start(f32[2,32,2048]{2,1,0:T(8,128)} %constant_dynamic-slice_fusion.14), channel_id=1, source_target_pairs={{0,3},{1,2},{2,1},{3,0},{4,7},{5,6},{6,5},{7,4},{8,11},{9,10},{10,... | collective-permute-start | bytes 1572872 | tf_op jit(solution)/shard_map/ppermute | solution.py:26
  5.8 1.6 %copy-done = f32[2,128,2048]{2,1,0:T(8,128)S(1)} copy-done((f32[2,128,2048]{2,1,0:T(8,128)S(1)}, f32[2,128,2048]{2,1,0:T(8,128)}, u32[]{:S(2)}) %copy-start) | copy-done | bytes 2097176
  7.4 1.2 %split.1 = (f32[2,32,2048]{2,1,0:T(8,128)}, f32[2,32,2048]{2,1,0:T(8,128)}, f32[2,2048]{1,0:T(2,128)}, f32[2,2048]{1,0:T(2,128)}) custom-call(f32[2,128,2048]{2,1,0:T(8,128)S(1)} %copy-done), custom_call_target="tpu_custom_call" | custom-call | bytes 4194304 | tf_op jit(solution)/shard_map/split/pallas_call | solution.py:241
  9.3 3.9 %collective-permute-start.3 = (f32[2,2048]{1,0:T(2,128)}, f32[2,2048]{1,0:T(2,128)S(1)}, u32[]{:S(2)}, u32[]{:S(2)}) collective-permute-start(f32[2,2048]{1,0:T(2,128)} %get-tuple-element.24), channel_id=1, source_target_pairs={{0,4},{4,8},{8,12},{1,5},{5,9},{9,13},{2,6},{6,10},{10,14},{3,7},{... | collective-permute-start | bytes 49160 | tf_op jit(solution)/shard_map/ppermute | solution.py:258
  13.2 1.3 %collective-permute-start.4 = (f32[2,2048]{1,0:T(2,128)}, f32[2,2048]{1,0:T(2,128)}, u32[]{:S(2)}, u32[]{:S(2)}) collective-permute-start(f32[2,2048]{1,0:T(2,128)} %get-tuple-element.25), channel_id=1, source_target_pairs={{4,0},{8,4},{12,8},{5,1},{9,5},{13,9},{6,2},{10,6},{14,10},{7,3},{... | collective-permute-start | bytes 49160 | tf_op jit(solution)/shard_map/ppermute | solution.py:259
  14.6 1.6 %constant_dynamic-slice_fusion = (s32[2,8,2048]{2,1,0:T(8,128)S(1)}, s32[2,8,2048]{2,1,0:T(8,128)}) fusion(s32[2,128,2048]{2,1,0:T(8,128)} %bins.1, s32[]{:T(128)S(6)} %select_n.42, s32[]{:T(128)S(6)} %select_n.47), kind=kLoop, calls=%fused_computation.1 | loop fusion | bytes 524296 | tf_op jit(solution)/shard_map/dynamic_slice | solution.py:234
  17.9 1.3 %collective-permute-done.4.below = f32[2,2048]{1,0:T(2,128)} collective-permute-done((f32[2,2048]{1,0:T(2,128)}, f32[2,2048]{1,0:T(2,128)}, u32[]{:S(2)}, u32[]{:S(2)}) %collective-permute-start.4) | collective-permute-done | bytes 16416 | tf_op jit(solution)/shard_map/ppermute | solution.py:259
  19.2 1.6 %copy-done.2 = s32[2,128,2048]{2,1,0:T(8,128)S(1)} copy-done((s32[2,128,2048]{2,1,0:T(8,128)S(1)}, s32[2,128,2048]{2,1,0:T(8,128)}, u32[]{:S(2)}) %copy-start.2) | copy-done | bytes 2097176
  20.8 2.6 %pack.1 = (f32[8,1024]{1,0:T(8,128)S(1)}, f32[40,1024]{1,0:T(8,128)}, f32[40,1024]{1,0:T(8,128)}, f32[40,1024]{1,0:T(8,128)}) custom-call(f32[2,2048]{1,0:T(2,128)S(1)} %collective-permute-done.3.above, f32[2,2048]{1,0:T(2,128)} %collective-permute-done.4.below, f32[2,128,2048]{2,1,0:T(8,128)S(1)} %copy-done.1, s32[2,128,2048]{2,1,0:T(8,128)S(1)} %copy-done.2), custom_call_target="tpu_custom_call" | custom-call | bytes 1310720 | tf_op jit(solution)/shard_map/pack/pallas_call | solution.py:264
  23.4 1.6 %collective-permute-start.5 = (f32[40,1024]{1,0:T(8,128)}, f32[40,1024]{1,0:T(8,128)S(1)}, u32[]{:S(2)}, u32[]{:S(2)}) collective-permute-start(f32[40,1024]{1,0:T(8,128)} %get-tuple-element.27), channel_id=1, source_target_pairs={{0,1},{1,0},{2,3},{3,2},{4,5},{5,4},{6,7},{7,6},{8,9},{9,8},{10,11... | collective-permute-start | bytes 491528 | tf_op jit(solution)/shard_map/ppermute | solution.py:26
  25.0 1.5 %collective-permute-start.6 = (f32[40,1024]{1,0:T(8,128)}, f32[40,1024]{1,0:T(8,128)S(1)}, u32[]{:S(2)}, u32[]{:S(2)}) collective-permute-start(f32[40,1024]{1,0:T(8,128)} %get-tuple-element.28), channel_id=1, source_target_pairs={{0,2},{1,3},{2,0},{3,1},{4,6},{5,7},{6,4},{7,5},{8,10},{9,11},{10,... | collective-permute-start | bytes 491528 | tf_op jit(solution)/shard_map/ppermute | solution.py:26
  27.1 2.2 %collective-permute-done.1.refs_2_ = f32[2,32,2048]{2,1,0:T(8,128)} collective-permute-done((f32[2,32,2048]{2,1,0:T(8,128)}, f32[2,32,2048]{2,1,0:T(8,128)}, u32[]{:S(2)}, u32[]{:S(2)}) %collective-permute-start.1) | collective-permute-done | bytes 524320 | tf_op jit(solution)/shard_map/ppermute | solution.py:26
  29.4 1.7 %collective-permute-start.12 = (s32[2,16,2048]{2,1,0:T(8,128)S(1)}, s32[2,16,2048]{2,1,0:T(8,128)S(1)}, u32[]{:S(2)}, u32[]{:S(2)}) collective-permute-start(s32[2,16,2048]{2,1,0:T(8,128)S(1)} %get-tuple-element.41), channel_id=1, source_target_pairs={{0,1},{1,0},{2,3},{3,2},{4,5},{5,4},{6,7},{7,6},{8,9},{9,8},{10,11... | collective-permute-start | bytes 786440 | tf_op jit(solution)/shard_map/ppermute | solution.py:26
  32.7 1.4 %collective-permute-done.5.refs_5_.refs_1_ = f32[40,1024]{1,0:T(8,128)S(1)} collective-permute-done((f32[40,1024]{1,0:T(8,128)}, f32[40,1024]{1,0:T(8,128)S(1)}, u32[]{:S(2)}, u32[]{:S(2)}) %collective-permute-start.5) | collective-permute-done | bytes 163872 | tf_op jit(solution)/shard_map/ppermute | solution.py:26
  34.3 2.8 %collective-permute-start.14 = (s32[2,16,2048]{2,1,0:T(8,128)S(1)}, s32[2,16,2048]{2,1,0:T(8,128)S(1)}, u32[]{:S(2)}, u32[]{:S(2)}) collective-permute-start(s32[2,16,2048]{2,1,0:T(8,128)S(1)} %get-tuple-element.42), channel_id=1, source_target_pairs={{0,3},{1,2},{2,1},{3,0},{4,7},{5,6},{6,5},{7,4},{8,11},{9,10},{10,... | collective-permute-start | bytes 786440 | tf_op jit(solution)/shard_map/ppermute | solution.py:26
  37.8 4.2 %shade.1 = (f32[8,32,2048]{2,1,0:T(8,128)S(1)}, f32[8,32,2048]{2,1,0:T(8,128)S(1)}) custom-call(f32[2,32,2048]{2,1,0:T(8,128)S(1)} %constant_dynamic-slice_fusion.13.refs_0_, f32[2,32,2048]{2,1,0:T(8,128)} %collective-permute-done.refs_1_, f32[2,32,2048]{2,1,0:T(8,128)} %collective-permute-done.1.refs_2_, f32[2,32,2048]{2,1,0:T(8,128)S(1)} %collective-permute-done.2.refs_3_, ...), custom_call_target="tpu_custom_call" | custom-call | flops 10485760 | bytes 8388608 | tf_op jit(solution)/shard_map/shade/pallas_call | solution.py:294
  42.0 1.1 %constant_dynamic-slice_fusion.2 = (s32[2,8,2048]{2,1,0:T(8,128)S(1)}, s32[2,8,2048]{2,1,0:T(8,128)S(1)}, s32[2,8,2048]{2,1,0:T(8,128)S(1)}) fusion(s32[2,128,2048]{2,1,0:T(8,128)} %bins.1, s32[]{:T(128)S(6)} %select_n.53, s32[]{:T(128)S(6)} %select_n.52, s32[]{:T(128)S(6)} %select_n.51), kind=kLoop, calls=%fused_computation.3 | loop fusion | bytes 786444 | tf_op jit(solution)/shard_map/dynamic_slice | solution.py:234
  43.1 2.0 %collective-permute-start.9 = (s32[2,8,2048]{2,1,0:T(8,128)S(1)}, s32[2,8,2048]{2,1,0:T(8,128)S(1)}, u32[]{:S(2)}, u32[]{:S(2)}) collective-permute-start(s32[2,8,2048]{2,1,0:T(8,128)S(1)} %get-tuple-element.39), channel_id=1, source_target_pairs={{0,1},{1,0},{2,3},{3,2},{4,5},{5,4},{6,7},{7,6},{8,9},{9,8},{10,11... | collective-permute-start | bytes 393224 | tf_op jit(solution)/shard_map/ppermute | solution.py:26
  45.1 1.5 %collective-permute-start.10 = (s32[2,8,2048]{2,1,0:T(8,128)S(1)}, s32[2,8,2048]{2,1,0:T(8,128)S(1)}, u32[]{:S(2)}, u32[]{:S(2)}) collective-permute-start(s32[2,8,2048]{2,1,0:T(8,128)S(1)} %get-tuple-element.38), channel_id=1, source_target_pairs={{0,2},{1,3},{2,0},{3,1},{4,6},{5,7},{6,4},{7,5},{8,10},{9,11},{10,... | collective-permute-start | bytes 393224 | tf_op jit(solution)/shard_map/ppermute | solution.py:26
  46.8 1.7 %blend.3.refs_4_ = f32[4,32,2048]{2,1,0:T(8,128)} custom-call(s32[2,8,128]{2,1,0:T(8,128)S(1)} %broadcast_in_dim.4.table, s32[32,128]{1,0:T(8,128)S(1)} %broadcast_in_dim.5.flips, f32[8,32,2048]{2,1,0:T(8,128)S(1)} %get-tuple-element.30.ordered, f32[8,32,2048]{2,1,0:T(8,128)S(1)} %get-tuple-element.31.shading, s32[2,8,2048]{2,1,0:T(8,128)S(1)} %get-tuple-element.35.refs_0_, ...), custom_call_target="tpu_custom_call" | custom-call | flops 2621440 | bytes 2097152 | tf_op jit(solution)/shard_map/blend/pallas_call | solution.py:334
  48.6 2.8 %blend.4.refs_4_ = f32[4,32,2048]{2,1,0:T(8,128)} custom-call(s32[2,8,128]{2,1,0:T(8,128)S(1)} %broadcast_in_dim.4.table, s32[32,128]{1,0:T(8,128)S(1)} %broadcast_in_dim.5.flips, f32[8,32,2048]{2,1,0:T(8,128)S(1)} %get-tuple-element.30.ordered, f32[8,32,2048]{2,1,0:T(8,128)S(1)} %get-tuple-element.31.shading, ...), custom_call_target="tpu_custom_call", output_to_operand_aliasing={{}: (8, {})} | custom-call | flops 5242880 | bytes 4194304 | tf_op jit(solution)/shard_map/blend/pallas_call | solution.py:334
  51.7 1.6 %collective-permute-done.10.refs_2_ = s32[2,8,2048]{2,1,0:T(8,128)S(1)} collective-permute-done((s32[2,8,2048]{2,1,0:T(8,128)S(1)}, s32[2,8,2048]{2,1,0:T(8,128)S(1)}, u32[]{:S(2)}, u32[]{:S(2)}) %collective-permute-start.10) | collective-permute-done | bytes 131104 | tf_op jit(solution)/shard_map/ppermute | solution.py:26
  53.3 1.7 %blend.5 = f32[4,32,2048]{2,1,0:T(8,128)} custom-call(s32[2,8,128]{2,1,0:T(8,128)S(1)} %broadcast_in_dim.4.table, s32[32,128]{1,0:T(8,128)S(1)} %broadcast_in_dim.5.flips, f32[8,32,2048]{2,1,0:T(8,128)S(1)} %get-tuple-element.30.ordered, f32[8,32,2048]{2,1,0:T(8,128)S(1)} %get-tuple-element.31.shading, ...), custom_call_target="tpu_custom_call", output_to_operand_aliasing={{}: (8, {})} | custom-call | flops 2621440 | bytes 2097152 | tf_op jit(solution)/shard_map/blend/pallas_call | solution.py:334
  (49 shorter events, 6.1 us)
Async XLA Ops:
  1.9 24.7 %collective-permute-start.2 = (f32[2,32,2048]{2,1,0:T(8,128)}, f32[2,32,2048]{2,1,0:T(8,128)S(1)}, u32[]{:S(2)}, u32[]{:S(2)}) collective-permute-start(f32[2,32,2048]{2,1,0:T(8,128)} %constant_dynamic-slice_fusion.14), channel_id=1, source_target_pairs={{0,3},{1,2},{2,1},{3,0},{4,7},{5,6},{6,5},{7,4},{8,11},{9,10},{10,... | collective-permute-start | bytes 1572872 | tf_op jit(solution)/shard_map/ppermute | solution.py:26
  5.8 1.6 %copy-start = (f32[2,128,2048]{2,1,0:T(8,128)S(1)}, f32[2,128,2048]{2,1,0:T(8,128)}, u32[]{:S(2)}) copy-start(f32[2,128,2048]{2,1,0:T(8,128)} %field.2) | copy-start | bytes 6291460
  7.4 7.1 %copy-start.1 = (f32[2,128,2048]{2,1,0:T(8,128)S(1)}, f32[2,128,2048]{2,1,0:T(8,128)}, u32[]{:S(2)}) copy-start(f32[2,128,2048]{2,1,0:T(8,128)} %field.2) | copy-start | bytes 6291460
  8.6 23.2 %collective-permute-start = (f32[2,32,2048]{2,1,0:T(8,128)}, f32[2,32,2048]{2,1,0:T(8,128)}, u32[]{:S(2)}, u32[]{:S(2)}) collective-permute-start(f32[2,32,2048]{2,1,0:T(8,128)} %get-tuple-element.21), channel_id=1, source_target_pairs={{0,1},{1,0},{2,3},{3,2},{4,5},{5,4},{6,7},{7,6},{8,9},{9,8},{10,11... | collective-permute-start | bytes 1572872 | tf_op jit(solution)/shard_map/ppermute | solution.py:26
  9.2 20.1 %collective-permute-start.1 = (f32[2,32,2048]{2,1,0:T(8,128)}, f32[2,32,2048]{2,1,0:T(8,128)}, u32[]{:S(2)}, u32[]{:S(2)}) collective-permute-start(f32[2,32,2048]{2,1,0:T(8,128)} %get-tuple-element.22), channel_id=1, source_target_pairs={{0,2},{1,3},{2,0},{3,1},{4,6},{5,7},{6,4},{7,5},{8,10},{9,11},{10,... | collective-permute-start | bytes 1572872 | tf_op jit(solution)/shard_map/ppermute | solution.py:26
  9.3 8.6 %collective-permute-start.3 = (f32[2,2048]{1,0:T(2,128)}, f32[2,2048]{1,0:T(2,128)S(1)}, u32[]{:S(2)}, u32[]{:S(2)}) collective-permute-start(f32[2,2048]{1,0:T(2,128)} %get-tuple-element.24), channel_id=1, source_target_pairs={{0,4},{4,8},{8,12},{1,5},{5,9},{9,13},{2,6},{6,10},{10,14},{3,7},{... | collective-permute-start | bytes 49160 | tf_op jit(solution)/shard_map/ppermute | solution.py:258
  13.2 5.9 %collective-permute-start.4 = (f32[2,2048]{1,0:T(2,128)}, f32[2,2048]{1,0:T(2,128)}, u32[]{:S(2)}, u32[]{:S(2)}) collective-permute-start(f32[2,2048]{1,0:T(2,128)} %get-tuple-element.25), channel_id=1, source_target_pairs={{4,0},{8,4},{12,8},{5,1},{9,5},{13,9},{6,2},{10,6},{14,10},{7,3},{... | collective-permute-start | bytes 49160 | tf_op jit(solution)/shard_map/ppermute | solution.py:259
  19.2 1.6 %copy-start.2 = (s32[2,128,2048]{2,1,0:T(8,128)S(1)}, s32[2,128,2048]{2,1,0:T(8,128)}, u32[]{:S(2)}) copy-start(s32[2,128,2048]{2,1,0:T(8,128)} %bins.1) | copy-start | bytes 6291460
  20.8 11.8 %copy-start.6 = (f32[2,32,128]{2,1,0:T(8,128)S(1)}, f32[2,32,128]{2,1,0:T(8,128)}, u32[]{:S(2)}) copy-start(f32[2,32,128]{2,1,0:T(8,128)} %constant_dynamic-slice_fusion.12) | copy-start | bytes 98308
  20.8 11.9 %copy-start.7 = (bf16[4,128]{1,0:T(4,128)(2,1)S(1)}, bf16[4,128]{1,0:T(4,128)(2,1)}, u32[]{:S(2)}) copy-start(bf16[4,128]{1,0:T(4,128)(2,1)} %param.6) | copy-start | bytes 3076
  23.4 9.2 %copy-start.4 = (f32[8,1024]{1,0:T(8,128)}, f32[8,1024]{1,0:T(8,128)S(1)}, u32[]{:S(2)}) copy-start(f32[8,1024]{1,0:T(8,128)S(1)} %get-tuple-element.26.refs_4_) | copy-start | bytes 98308
  23.4 10.7 %collective-permute-start.5 = (f32[40,1024]{1,0:T(8,128)}, f32[40,1024]{1,0:T(8,128)S(1)}, u32[]{:S(2)}, u32[]{:S(2)}) collective-permute-start(f32[40,1024]{1,0:T(8,128)} %get-tuple-element.27), channel_id=1, source_target_pairs={{0,1},{1,0},{2,3},{3,2},{4,5},{5,4},{6,7},{7,6},{8,9},{9,8},{10,11... | collective-permute-start | bytes 491528 | tf_op jit(solution)/shard_map/ppermute | solution.py:26
  25.0 9.3 %collective-permute-start.6 = (f32[40,1024]{1,0:T(8,128)}, f32[40,1024]{1,0:T(8,128)S(1)}, u32[]{:S(2)}, u32[]{:S(2)}) collective-permute-start(f32[40,1024]{1,0:T(8,128)} %get-tuple-element.28), channel_id=1, source_target_pairs={{0,2},{1,3},{2,0},{3,1},{4,6},{5,7},{6,4},{7,5},{8,10},{9,11},{10,... | collective-permute-start | bytes 491528 | tf_op jit(solution)/shard_map/ppermute | solution.py:26
  26.5 20.1 %copy-start.8 = (bf16[4,128]{1,0:T(4,128)(2,1)S(1)}, bf16[4,128]{1,0:T(4,128)(2,1)}, u32[]{:S(2)}) copy-start(bf16[4,128]{1,0:T(4,128)(2,1)} %param.6) | copy-start | bytes 3076
  26.6 20.1 %copy-start.9 = (s32[128]{0:T(128)S(1)}, s32[128]{0:T(128)}, u32[]{:S(2)}) copy-start(s32[128]{0:T(128)} %param.7) | copy-start | bytes 1540
  26.6 10.5 %collective-permute-start.7 = (f32[40,1024]{1,0:T(8,128)}, f32[40,1024]{1,0:T(8,128)S(1)}, u32[]{:S(2)}, u32[]{:S(2)}) collective-permute-start(f32[40,1024]{1,0:T(8,128)} %get-tuple-element.29), channel_id=1, source_target_pairs={{0,3},{1,2},{2,1},{3,0},{4,7},{5,6},{6,5},{7,4},{8,11},{9,10},{10,... | collective-permute-start | bytes 491528 | tf_op jit(solution)/shard_map/ppermute | solution.py:26
  29.4 17.3 %collective-permute-start.12 = (s32[2,16,2048]{2,1,0:T(8,128)S(1)}, s32[2,16,2048]{2,1,0:T(8,128)S(1)}, u32[]{:S(2)}, u32[]{:S(2)}) collective-permute-start(s32[2,16,2048]{2,1,0:T(8,128)S(1)} %get-tuple-element.41), channel_id=1, source_target_pairs={{0,1},{1,0},{2,3},{3,2},{4,5},{5,4},{6,7},{7,6},{8,9},{9,8},{10,11... | collective-permute-start | bytes 786440 | tf_op jit(solution)/shard_map/ppermute | solution.py:26
  32.6 4.5 %collective-permute-start.8 = (f32[8,32,128]{2,1,0:T(8,128)S(1)}, f32[8,32,128]{2,1,0:T(8,128)S(1)}, u32[]{:S(2)}, u32[]{:S(2)}) collective-permute-start(f32[8,32,128]{2,1,0:T(8,128)S(1)} %pad_maximum_fusion), channel_id=1, source_target_pairs={{0,16},{16,0},{1,17},{17,1},{2,18},{18,2},{3,19},{19,3},{4,20},{20... | collective-permute-start | bytes 393224 | tf_op jit(solution)/shard_map/ppermute | solution.py:26
  34.1 14.5 %collective-permute-start.13 = (s32[2,16,2048]{2,1,0:T(8,128)S(1)}, s32[2,16,2048]{2,1,0:T(8,128)S(1)}, u32[]{:S(2)}, u32[]{:S(2)}) collective-permute-start(s32[2,16,2048]{2,1,0:T(8,128)S(1)} %get-tuple-element.40), channel_id=1, source_target_pairs={{0,2},{1,3},{2,0},{3,1},{4,6},{5,7},{6,4},{7,5},{8,10},{9,11},{10,... | collective-permute-start | bytes 786440 | tf_op jit(solution)/shard_map/ppermute | solution.py:26
  34.3 14.3 %collective-permute-start.14 = (s32[2,16,2048]{2,1,0:T(8,128)S(1)}, s32[2,16,2048]{2,1,0:T(8,128)S(1)}, u32[]{:S(2)}, u32[]{:S(2)}) collective-permute-start(s32[2,16,2048]{2,1,0:T(8,128)S(1)} %get-tuple-element.42), channel_id=1, source_target_pairs={{0,3},{1,2},{2,1},{3,0},{4,7},{5,6},{6,5},{7,4},{8,11},{9,10},{10,... | collective-permute-start | bytes 786440 | tf_op jit(solution)/shard_map/ppermute | solution.py:26
  43.1 8.6 %collective-permute-start.9 = (s32[2,8,2048]{2,1,0:T(8,128)S(1)}, s32[2,8,2048]{2,1,0:T(8,128)S(1)}, u32[]{:S(2)}, u32[]{:S(2)}) collective-permute-start(s32[2,8,2048]{2,1,0:T(8,128)S(1)} %get-tuple-element.39), channel_id=1, source_target_pairs={{0,1},{1,0},{2,3},{3,2},{4,5},{5,4},{6,7},{7,6},{8,9},{9,8},{10,11... | collective-permute-start | bytes 393224 | tf_op jit(solution)/shard_map/ppermute | solution.py:26
  45.1 8.2 %collective-permute-start.10 = (s32[2,8,2048]{2,1,0:T(8,128)S(1)}, s32[2,8,2048]{2,1,0:T(8,128)S(1)}, u32[]{:S(2)}, u32[]{:S(2)}) collective-permute-start(s32[2,8,2048]{2,1,0:T(8,128)S(1)} %get-tuple-element.38), channel_id=1, source_target_pairs={{0,2},{1,3},{2,0},{3,1},{4,6},{5,7},{6,4},{7,5},{8,10},{9,11},{10,... | collective-permute-start | bytes 393224 | tf_op jit(solution)/shard_map/ppermute | solution.py:26
  46.6 6.7 %collective-permute-start.11 = (s32[2,8,2048]{2,1,0:T(8,128)S(1)}, s32[2,8,2048]{2,1,0:T(8,128)S(1)}, u32[]{:S(2)}, u32[]{:S(2)}) collective-permute-start(s32[2,8,2048]{2,1,0:T(8,128)S(1)} %get-tuple-element.37), channel_id=1, source_target_pairs={{0,3},{1,2},{2,1},{3,0},{4,7},{5,6},{6,5},{7,4},{8,11},{9,10},{10,... | collective-permute-start | bytes 393224 | tf_op jit(solution)/shard_map/ppermute | solution.py:26
  48.6 4.7 %copy-start.3 = (s32[2,8,2048]{2,1,0:T(8,128)S(1)}, s32[2,8,2048]{2,1,0:T(8,128)}, u32[]{:S(2)}) copy-start(s32[2,8,2048]{2,1,0:T(8,128)} %get-tuple-element.36.refs_0_) | copy-start | bytes 393220
  (1 other events, 0.8 us)

commit v4 on v0

v4 whole, which is shorter than its diff:
```python
import functools

import jax
import jax.numpy as jnp
from jax import lax
from jax.experimental import pallas as pl
from jax.experimental.pallas import tpu as pltpu
from jax.sharding import PartitionSpec as P

light_x = 0.36
light_y = 0.48
light_z = 0.8
LANES = 128
ROWS = 8
COLOUR_UNIT = 2.0**-12
OPACITY_UNIT = 2.0**-13
HALF_WORD = 16
LOG2_E = 1.4426950408889634
UNROLLED = 32
COPIES = 4
VMEM_LIMIT = 40 * 1024 * 1024

vmem = pl.BlockSpec(memory_space=pltpu.VMEM)
hbm = pl.BlockSpec(memory_space=pltpu.HBM)


def partner(x, axis, distance):
    return lax.ppermute(x, axis, [(i, i ^ distance) for i in range(lax.axis_size(axis))])


def in_hbm(array):
    return pltpu.with_memory_space_constraint(array, pltpu.HBM)


def after(array, *others):
    return lax.optimization_barrier((array, *others))[0]


def run_copies(moves):
    for move in moves:
        move.start()
    for move in moves:
        move.wait()


def lead_kernel(count, slot, field, piece, sem):
    rows = piece.shape[1]
    start = pl.multiple_of((lax.axis_index("gz") ^ slot) * rows, ROWS)
    run_copies([pltpu.make_async_copy(field.at[:, pl.ds(start, rows)], piece, sem)])


def split_kernel(count, depth, slots, field, *refs):
    pieces = refs[: len(slots)]
    last, first, ends, sems = refs[len(slots) :]
    height = field.shape[1]
    rows = height // count
    rank = lax.axis_index("gz")
    moves = [
        pltpu.make_async_copy(field.at[:, height - ROWS :], ends.at[0], sems.at[0]),
        pltpu.make_async_copy(field.at[:, :ROWS], ends.at[1], sems.at[1]),
    ]
    for index, slot in enumerate(slots):
        start = pl.multiple_of((rank ^ slot) * rows, ROWS)
        moves.append(pltpu.make_async_copy(field.at[:, pl.ds(start, rows)], pieces[index], sems.at[2 + index]))
    run_copies(moves)
    for j in range(depth):
        last[j : j + 1, :] = ends[0, j, ROWS - 1 :, :]
        first[j : j + 1, :] = ends[1, j, :1, :]


def pack_kernel(count, depth, early, later, above, below, table, march, field, bins, *refs):
    messages = refs[: count - 1]
    edges, entries, flips, *pieces, high, low, labels, sems, cut_sems = refs[count - 1 :]
    height, width = field.shape[1:]
    rows = height // count
    half = width // 2
    rank = lax.axis_index("gz")
    copies = []
    for slot in range(count):
        target = rank ^ slot
        top = pl.multiple_of(jnp.maximum(target * rows - ROWS, 0), ROWS)
        bottom = pl.multiple_of(jnp.minimum(target * rows + rows, height - ROWS), ROWS)
        start = pl.multiple_of(target * rows, ROWS)
        moves = [
            pltpu.make_async_copy(field.at[:, pl.ds(top, ROWS)], high.at[slot], sems.at[slot, 0]),
            pltpu.make_async_copy(field.at[:, pl.ds(bottom, ROWS)], low.at[slot], sems.at[slot, 1]),
        ]
        if slot:
            moves.append(
                pltpu.make_async_copy(bins.at[:, pl.ds(start, early)], labels.at[slot - 1], sems.at[slot, 2])
            )
        for move in moves:
            move.start()
        copies.append(moves)
    cuts = []
    for index, (slot, top, size) in enumerate(later):
        start = pl.multiple_of((rank ^ slot) * rows + top, ROWS)
        cuts.append(pltpu.make_async_copy(bins.at[:, pl.ds(start, size)], pieces[index], cut_sems.at[index]))
        cuts[-1].start()
    pair = pack_entries(table[...].astype(jnp.float32))
    for word in range(2):
        entries[word] = pair[word]
    for row in range(rows):
        flips[row : row + 1, :] = jnp.full((1, LANES), march[rank * rows + row], jnp.int32)
    for slot in range(count):
        target = rank ^ slot
        for move in copies[slot]:
            move.wait()
        message = messages[slot - 1] if slot else edges
        for j in range(depth):
            upper = jnp.where(target == 0, above[j : j + 1, :], high[slot, j, ROWS - 1 : ROWS, :])
            lower = jnp.where(target == count - 1, below[j : j + 1, :], low[slot, j, 0:1, :])
            for h in range(2):
                cols = slice(h * half, (h + 1) * half)
                at = 2 * depth * h + j
                message[at : at + 1, :] = upper[:, cols]
                message[at + depth : at + depth + 1, :] = lower[:, cols]
                if slot:
                    first = 4 * depth + (2 * j + h) * early
                    message[first : first + early, :] = labels[slot - 1, j, :, cols].astype(jnp.float32)
    for move in cuts:
        move.wait()


def side_kernel(count, depth, field, *refs):
    bricks = (None,) + refs[: count - 1]
    slab, own, sem = refs[count - 1 :]
    rows = slab.shape[1]
    width = field.shape[2]
    side = lax.axis_index("sx")
    start = pl.multiple_of(lax.axis_index("gz") * rows, ROWS)
    column = pl.multiple_of((1 - side) * (width - LANES), LANES)
    move = pltpu.make_async_copy(field.at[:, pl.ds(start, rows), pl.ds(column, LANES)], own, sem)
    move.start()
    for slot in range(1, count):
        for j in range(depth):
            slab[slot * depth + j] = jnp.where(
                side == 1, bricks[slot][j, :, :LANES], bricks[slot][j, :, width - LANES :]
            )
    move.wait()
    for j in range(depth):
        slab[j] = own[j]


def pack_entries(table):
    units = [1.0 / COLOUR_UNIT] * 3 + [1.0 / OPACITY_UNIT]
    rows = [
        jnp.broadcast_to((table[c : c + 1, :] * units[c]).astype(jnp.int32), (ROWS, table.shape[1])) for c in range(4)
    ]
    return rows[0] | rows[1] << HALF_WORD, rows[2] | rows[3] << HALF_WORD


def look(entries, labels):
    return jnp.take_along_axis(entries, labels, axis=1, mode="promise_in_bounds")


def low_part(words):
    return (words & ((1 << HALF_WORD) - 1)).astype(jnp.float32)


def high_part(words):
    return (words >> HALF_WORD).astype(jnp.float32)


def blend_rows(count, depth, words, back, scaled, span, shading, shaded, result, here, finish):
    rank = lax.axis_index("gz")
    tiles = result.shape[2] // LANES
    unroll = max(min(tiles // COPIES, UNROLLED // (count * depth)), 1)
    ahead = [
        [jnp.where((rank ^ other) < (rank ^ slot), 1.0, 0.0) for other in range(count)] for slot in range(count)
    ]

    def blend_tile(cols, h):
        found = [words(cell, cols, h) for cell in range(count * depth)]
        taus = [high_part(found[cell][1]) * scaled[cell, span, cols] for cell in range(count * depth)]
        inner = []
        for slot in range(count):
            sums = [taus[slot * depth]]
            for j in range(1, depth):
                sums.append(sums[-1] + taus[slot * depth + j])
            inner.append(sums)
        whole = sum(sums[-1] for sums in inner)
        sign = jnp.where(back, 1.0, -1.0)
        shift = jnp.where(back, -whole, 0.0)
        colour = [jnp.zeros((ROWS, LANES), jnp.float32) for _ in range(3)]
        for slot in range(count):
            front = sum(inner[other][-1] * ahead[slot][other] for other in range(count) if other != slot)
            reached = [front] + [front + part for part in inner[slot]]
            through = [jnp.exp2(sign * part + shift) for part in reached]
            for j in range(depth):
                cell = slot * depth + j
                weight = jnp.abs(through[j] - through[j + 1]) * shading[cell, shaded, cols]
                colour[0] = colour[0] + weight * low_part(found[cell][0])
                colour[1] = colour[1] + weight * high_part(found[cell][0])
                colour[2] = colour[2] + weight * low_part(found[cell][1])
        for c in range(3):
            result[c, here, cols] = colour[c]
        result[3, here, cols] = 1.0 - jnp.exp2(-whole)

    quarter = tiles // COPIES
    for part in range(COPIES):
        h = 2 * part // COPIES
        if unroll == quarter:
            for tile in range(part * quarter, (part + 1) * quarter):
                blend_tile(slice(tile * LANES, (tile + 1) * LANES), h)
        else:

            def tile_step(step, _, part=part, h=h):
                for tile in range(unroll):
                    left = (part * quarter + step * unroll + tile) * LANES
                    blend_tile(pl.ds(pl.multiple_of(left, LANES), LANES), h)
                return 0

            lax.fori_loop(0, quarter // unroll, tile_step, 0)
        finish(part)


def copy_out(result, image, sems, top, start):
    columns = result.shape[2] // COPIES
    return [
        pltpu.make_async_copy(
            result.at[:, top : top + ROWS, part * columns : (part + 1) * columns],
            image.at[:, start + top : start + top + ROWS, part * columns : (part + 1) * columns],
            sems.at[top // ROWS, part],
        )
        for part in range(COPIES)
    ]


def shade_tile(ext, at, top, width, dy_of, store):
    here = slice(ROWS + top, 2 * ROWS + top)
    lane = lax.broadcasted_iota(jnp.int32, (ROWS, LANES), 1)
    first = lane == 0
    last = lane == LANES - 1
    tiles = [ext[at + 1, here, left : left + LANES] for left in range(0, width + 2 * LANES, LANES)]
    toward = [pltpu.roll(tile, LANES - 1, 1) for tile in tiles]
    away = [pltpu.roll(tile, 1, 1) for tile in tiles]
    for c in range(1, width // LANES + 1):
        cols = slice(c * LANES, (c + 1) * LANES)
        dx = jnp.where(last, toward[c + 1], toward[c]) - jnp.where(first, away[c - 1], away[c])
        dy = dy_of(
            c - 1,
            ext[at + 1, ROWS + top + 1 : 2 * ROWS + top + 1, cols]
            - ext[at + 1, ROWS + top - 1 : 2 * ROWS + top - 1, cols],
        )
        dz = ext[at + 2, here, cols] - ext[at, here, cols]
        facing = jnp.abs((0.5 * light_x) * dx + (0.5 * light_y) * dy + (0.5 * light_z) * dz)
        square = 0.25 * (dx * dx + dy * dy + dz * dz) + 1.0
        store(c - 1, 0.3 * COLOUR_UNIT + (0.7 * COLOUR_UNIT) * facing * lax.rsqrt(square))


def inner_kernel(count, depth, field, edges, beside, entries, *refs):
    parts = len(refs) - (count - 1) - 7
    bricks = refs[: count - 1]
    own_bins = refs[count - 1 : count - 1 + parts]
    ext, scaled, inner, known, token, own_brick, sem = refs[count - 1 + parts :]
    rows, width = scaled.shape[1:]
    half = width // 2
    total = count * depth
    rank = lax.axis_index("gz")
    side = lax.axis_index("sx")
    inside = slice(ROWS, ROWS + rows)
    move = pltpu.make_async_copy(field.at[:, pl.ds(pl.multiple_of(rank * rows, ROWS), rows)], own_brick, sem)
    move.start()
    bricks = (own_brick, *bricks)
    zero_plane = jnp.zeros((rows, width), jnp.float32)
    zero_row = jnp.zeros((ROWS, width), jnp.float32)
    ext[0, inside, LANES : LANES + width] = zero_plane
    ext[total + 1, inside, LANES : LANES + width] = zero_plane
    for slot in reversed(range(count)):
        if slot == 0:
            move.wait()
        for j in range(depth):
            at = (rank ^ slot) * depth + j
            plane = bricks[slot][j]
            scaled[slot * depth + j] = plane * (OPACITY_UNIT * LOG2_E)
            ext[at + 1, inside, LANES : LANES + width] = plane
            ext[at + 1, :ROWS, LANES : LANES + width] = zero_row
            ext[at + 1, ROWS + rows :, LANES : LANES + width] = zero_row
            if slot == 0:
                for h in range(2):
                    cols = slice(LANES + h * half, LANES + (h + 1) * half)
                    row = 2 * depth * h + j
                    ext[at + 1, ROWS - 1 : ROWS, cols] = edges[row : row + 1, :]
                    ext[at + 1, ROWS + rows : ROWS + rows + 1, cols] = edges[row + depth : row + depth + 1, :]
            column = beside[slot * depth + j]
            ext[at + 1, inside, :LANES] = jnp.where(side == 1, column, 0.0)
            ext[at + 1, inside, LANES + width :] = jnp.where(side == 0, column, 0.0)
    pair = (entries[0], entries[1])
    start = 0
    for part in own_bins:
        size = part.shape[1]
        for j in range(depth):
            for top in range(0, size, ROWS):
                for left in range(0, width, LANES):
                    cols = slice(left, left + LANES)
                    labels = part[j, top : top + ROWS, cols]
                    for word in range(2):
                        known[word, j, start + top : start + top + ROWS, cols] = look(pair[word], labels)
        start += size

    def plane_step(cell, _):
        at = (rank ^ (cell // depth)) * depth + cell % depth
        for top in range(ROWS, rows - ROWS, ROWS):

            def store(c, value, top=top):
                inner[cell, top - ROWS : top, c * LANES : (c + 1) * LANES] = value

            shade_tile(ext, at, top, width, lambda c, dy: dy, store)
        return 0

    if rows > 2 * ROWS:
        lax.fori_loop(0, total, plane_step, 0)
    else:
        inner[...] = jnp.zeros_like(inner)
    token[...] = jnp.zeros_like(token)


def outer_kernel(count, depth, entries, flips, ext, scaled, inner, known, *refs):
    messages = refs[: count - 1]
    outer, image, result, sems = refs[count - 1 :]
    rows, width = scaled.shape[1:]
    early = result.shape[1]
    half = width // 2
    rank = lax.axis_index("gz")
    pair = (entries[0], entries[1])
    row_of = lax.broadcasted_iota(jnp.int32, (ROWS, LANES), 0)

    def shade(top):
        for cell in range(count * depth):
            slot, j = divmod(cell, depth)
            at = (rank ^ slot) * depth + j

            def dy_of(c, dy, slot=slot, j=j):
                if slot == 0:
                    return dy
                h, left = c * LANES // half, c * LANES % half
                row = 2 * depth * h + j
                cols = slice(left, left + LANES)
                if top == 0:
                    dy = dy - jnp.where(row_of == 0, messages[slot - 1][row : row + 1, cols], 0.0)
                if top == rows - ROWS:
                    beyond = messages[slot - 1][row + depth : row + depth + 1, cols]
                    dy = dy + jnp.where(row_of == ROWS - 1, beyond, 0.0)
                return dy

            def store(c, value, cell=cell):
                place = 0 if top == 0 else ROWS
                outer[cell, place : place + ROWS, c * LANES : (c + 1) * LANES] = value

            shade_tile(ext, at, top, width, dy_of, store)

    shade(0)
    copies = []
    for top in range(0, early, ROWS):
        here = slice(top, top + ROWS)

        def words(cell, cols, h, top=top):
            slot, j = divmod(cell, depth)
            if slot == 0:
                return tuple(known[word, j, top : top + ROWS, cols] for word in range(2))
            left = cols.start - h * half
            left = pl.ds(left if isinstance(left, int) else pl.multiple_of(left, LANES), LANES)
            row = 4 * depth + (2 * j + h) * early + top
            labels = messages[slot - 1][row : row + ROWS, left].astype(jnp.int32)
            return look(pair[0], labels), look(pair[1], labels)

        parts = copy_out(result, image, sems, top, 0)
        shading, shaded = (outer, slice(0, ROWS)) if top == 0 else (inner, slice(top - ROWS, top))
        blend_rows(
            count, depth, words, flips[here, :] == 1, scaled, here, shading, shaded, result, here,
            lambda part, parts=parts: parts[part].start(),
        )
        copies += parts
    if rows > ROWS:
        shade(rows - ROWS)
    for move in copies:
        move.wait()


def look_kernel(depth, entries, brick, found):
    rows, width = found.shape[2:]
    for j in range(depth):
        for top in range(0, rows, ROWS):
            for left in range(0, width, LANES):
                at = (slice(top, top + ROWS), slice(left, left + LANES))
                labels = brick[(j, *at)]
                for word in range(2):
                    found[(word, j, *at)] = look(entries[word], labels)


def blend_kernel(count, depth, start, late, lead, entries, flips, scaled, shading, known, found, *refs):
    bricks = refs[: count - 2]
    image, result, sems = refs[-3:]
    rows = result.shape[1]
    pair = (entries[0], entries[1])
    unknown = [slot for slot in range(1, count) if slot != lead]
    copies = []
    for top in range(0, rows, ROWS):
        here = slice(top, top + ROWS)
        span = slice(start + top, start + top + ROWS)
        inner = start + top + ROWS < scaled.shape[1]
        shaded = slice(start + top - ROWS, start + top) if inner else slice(ROWS, 2 * ROWS)

        def words(cell, cols, h, here=here, span=span, top=top):
            slot, j = divmod(cell, depth)
            if slot == 0:
                return tuple(known[word, j, span, cols] for word in range(2))
            if slot == lead:
                begin = start + top - late
                return tuple(found[word, j, begin : begin + ROWS, cols] for word in range(2))
            labels = bricks[unknown.index(slot)][j, here, cols]
            return look(pair[0], labels), look(pair[1], labels)

        parts = copy_out(result, image, sems, top, start)
        blend_rows(
            count, depth, words, flips[span, :] == 1, scaled, span, shading, shaded, result, here,
            lambda part, parts=parts: parts[part].start(),
        )
        copies += parts
    for move in copies:
        move.wait()


def shards(field, bins, table, march_order):
    depth, height, width = field.shape
    count = lax.axis_size("gz")
    rank = lax.axis_index("gz").astype(jnp.int32)
    rows = height // count
    total = count * depth
    half = width // 2
    slots = range(count)
    partners = sorted(range(1, count), key=lambda slot: (-slot.bit_count(), slot))
    lead, *others = partners
    params = pltpu.CompilerParams(vmem_limit_bytes=VMEM_LIMIT)

    def cost(cells):
        return pl.CostEstimate(flops=20 * cells, bytes_accessed=8 * cells, transcendentals=cells)

    done = {}
    order = {"message": lambda index: [("field", 0)], "bins": lambda index: [("message", index), "inner"]}

    def send(name, array, slot):
        index = partners.index(slot)
        waits = [done[key] for key in order.get(name, lambda index: ())(index)]
        done[name, index] = partner(after(array, *waits), "gz", slot)
        return done[name, index]

    bricks = {}
    sent = pl.pallas_call(
        functools.partial(lead_kernel, count, lead),
        out_shape=pltpu.VMEM((depth, rows, width), jnp.float32),
        in_specs=[hbm],
        out_specs=vmem,
        scratch_shapes=[pltpu.SemaphoreType.DMA],
        compiler_params=params,
        cost_estimate=cost(depth * rows * width),
        name="lead",
    )(in_hbm(field))
    bricks[lead] = send("field", sent, lead)

    *pieces, last, first = pl.pallas_call(
        functools.partial(split_kernel, count, depth, others),
        out_shape=[pltpu.VMEM((depth, rows, width), jnp.float32)] * len(others)
        + [pltpu.VMEM((depth, width), jnp.float32)] * 2,
        in_specs=[hbm],
        out_specs=[vmem] * count,
        scratch_shapes=[pltpu.VMEM((2, depth, ROWS, width), jnp.float32), pltpu.SemaphoreType.DMA((count,))],
        compiler_params=params,
        cost_estimate=cost(depth * height * width),
        name="split",
    )(in_hbm(after(field, sent)))
    for slot, sent in zip(others, pieces):
        bricks[slot] = send("field", sent, slot)

    forward = [(i, i + 1) for i in range(lax.axis_size("sy") - 1)]
    backward = [(target, origin) for origin, target in forward]
    above = lax.ppermute(last, "sy", forward)
    below = lax.ppermute(first, "sy", backward)

    early = max(rows // 2 // ROWS, 1) * ROWS
    late = rows - early
    later = []
    if late:
        later = [(0, 0, rows), (lead, early, late)]
        pieces = [(early, late - ROWS), (rows - ROWS, ROWS)] if late > ROWS else [(early, late)]
        later += [(slot, top, size) for top, size in pieces for slot in others]
    else:
        pieces = []
        later = [(0, 0, rows)]
    message_rows = 4 * depth + 2 * depth * early
    packed = pl.pallas_call(
        functools.partial(pack_kernel, count, depth, early, later),
        out_shape=[pltpu.VMEM((message_rows, half), jnp.float32)] * (count - 1)
        + [
            jax.ShapeDtypeStruct((4 * depth, half), jnp.float32),
            jax.ShapeDtypeStruct((2, ROWS, table.shape[1]), jnp.int32),
            jax.ShapeDtypeStruct((rows, LANES), jnp.int32),
        ]
        + [jax.ShapeDtypeStruct((depth, size, width), jnp.int32) for _, _, size in later],
        in_specs=[vmem, vmem, vmem, pl.BlockSpec(memory_space=pltpu.SMEM), hbm, hbm],
        out_specs=[vmem] * (count + 2 + len(later)),
        scratch_shapes=[
            pltpu.VMEM((count, depth, ROWS, width), jnp.float32),
            pltpu.VMEM((count, depth, ROWS, width), jnp.float32),
            pltpu.VMEM((count - 1, depth, early, width), jnp.int32),
            pltpu.SemaphoreType.DMA((count, 3)),
            pltpu.SemaphoreType.DMA((len(later),)),
        ],
        compiler_params=params,
        cost_estimate=cost(depth * height * width),
        name="pack",
    )(above, below, table, march_order, in_hbm(field), in_hbm(bins))
    messages = {}
    for slot in partners:
        messages[slot] = send("message", packed[slot - 1], slot)
    edges, entries, flips = packed[count - 1 : count + 2]
    cuts = packed[count + 2 :]

    slab = pl.pallas_call(
        functools.partial(side_kernel, count, depth),
        out_shape=pltpu.VMEM((total, rows, LANES), jnp.float32),
        in_specs=[hbm] + [vmem] * (count - 1),
        out_specs=vmem,
        scratch_shapes=[pltpu.VMEM((depth, rows, LANES), jnp.float32), pltpu.SemaphoreType.DMA],
        compiler_params=params,
        cost_estimate=cost(total * rows * LANES),
        name="side",
    )(in_hbm(field), *[bricks[slot] for slot in slots[1:]])
    beside = partner(slab, "sx", 1)

    ext, scaled, inner, known, token = pl.pallas_call(
        functools.partial(inner_kernel, count, depth),
        out_shape=(
            pltpu.VMEM((total + 2, rows + 2 * ROWS, width + 2 * LANES), jnp.float32),
            pltpu.VMEM((total, rows, width), jnp.float32),
            pltpu.VMEM((total, max(rows - 2 * ROWS, ROWS), width), jnp.float32),
            pltpu.VMEM((2, depth, rows, width), jnp.int32),
            jax.ShapeDtypeStruct((ROWS, LANES), jnp.float32),
        ),
        in_specs=[hbm] + [vmem] * (count + 3),
        out_specs=[vmem] * 5,
        scratch_shapes=[pltpu.VMEM((depth, rows, width), jnp.float32), pltpu.SemaphoreType.DMA],
        compiler_params=params,
        cost_estimate=cost(total * rows * width),
        name="inner",
    )(in_hbm(field), edges, beside, entries, *[bricks[slot] for slot in slots[1:]], cuts[0])
    done["inner"] = token

    image_shape = jax.ShapeDtypeStruct((4, rows, width), jnp.float32)
    outer, image = pl.pallas_call(
        functools.partial(outer_kernel, count, depth),
        out_shape=(pltpu.VMEM((total, 2 * ROWS, width), jnp.float32), image_shape),
        in_specs=[vmem] * (count + 5),
        out_specs=(vmem, hbm),
        scratch_shapes=[
            pltpu.VMEM((4, early, width), jnp.float32),
            pltpu.SemaphoreType.DMA((early // ROWS, COPIES)),
        ],
        compiler_params=params,
        cost_estimate=cost(total * rows * width),
        name="outer",
    )(entries, flips, ext, scaled, inner, known, *[messages[slot] for slot in slots[1:]])
    if not late:
        return image

    arrived = [send("bins", cut, slot) for (slot, _, _), cut in zip(later[1:], cuts[1:])]
    found = pl.pallas_call(
        functools.partial(look_kernel, depth),
        out_shape=pltpu.VMEM((2, depth, late, width), jnp.int32),
        in_specs=[vmem] * 2,
        out_specs=vmem,
        compiler_params=params,
        cost_estimate=cost(depth * late * width),
        name="look",
    )(entries, arrived[0])
    for index, (top, size) in enumerate(pieces):
        labels = arrived[1 + index * len(others) : 1 + (index + 1) * len(others)]
        labels = [labels[others.index(slot)] for slot in sorted(others)]
        shading = outer if top + size == rows else inner
        operands = [entries, flips, scaled, shading, known, found, *labels, image]
        image = pl.pallas_call(
            functools.partial(blend_kernel, count, depth, top, early, lead),
            out_shape=image_shape,
            in_specs=[vmem] * (len(operands) - 1) + [hbm],
            out_specs=hbm,
            scratch_shapes=[
                pltpu.VMEM((4, size, width), jnp.float32),
                pltpu.SemaphoreType.DMA((size // ROWS, COPIES)),
            ],
            input_output_aliases={len(operands) - 1: 0},
            compiler_params=params,
            cost_estimate=cost(total * size * width),
            name="blend",
        )(*operands)
    return image


def solution(mesh):
    placed = (P("gz", "sy", "sx"), P("gz", "sy", "sx"), P(), P("sy"))
    return jax.shard_map(
        shards, mesh=mesh, in_specs=placed, out_specs=P(None, ("sy", "gz"), "sx"), check_vma=False
    )
```

time: 199 us -> 54 us (0.27)
  waiting for transfers between devices: 68.2 us -> 18.2 us
  local copies, waits for them, and re-layouts: 49.6 us -> 0.01 us
  matrix products: 40.8 us -> 0 us
  other arithmetic: 17.5 us -> 0 us
  Pallas kernels: 0 us -> 15.3 us
  starting transfers between devices: 22 us -> 20 us
    ppermute x8 -> x14, waiting for transfers between devices: 68.2 us -> 18.2 us  [the longest x12 13.9 us: partner(): lax.ppermute(x, axis, [(i, i ^ distance) for i in range(lax.axis_size(axi...]
    dot_general x16 -> x0, matrix products: 40.8 us -> none  [lookup(): jnp.einsum('kn,nrw->krw', table, onehot, preferred_element_type=jnp.float32)]
    dynamic_update_slice x16 -> x0, local copies, waits for them, and re-layouts: 17.6 us -> none  [classify(): looked = lax.map(lookup, blocked)]
    pallas_call x0 -> x9, Pallas kernels: none -> 15.3 us  [the longest x1 4.12 us: shards(): pl.pallas_call(functools.partial(inner_kernel, count, depth), out_shape=(...]
    eq x16 -> x0, local copies, waits for them, and re-layouts: 14.6 us -> none  [lookup(): onehot = (block_bins[None] == labels[:, None, None]).astype(jnp.bfloat16)]
    slice x7 -> x0, local copies, waits for them, and re-layouts: 11.3 us -> none  [the longest x1 6.29 us: classify(): emitted = looked[:3] * (shading * opacity)[None]]
    mul x5 -> x0, other arithmetic: 8.2 us -> none  [the longest x2 7.77 us: classify(): emitted = looked[:3] * (shading * opacity)[None]]
    select_n x4 -> x0, other arithmetic: 4.82 us -> none  [the longest x2 3.05 us: shards(): front = jnp.where(in_front, kept, arrived)]
  transfers between devices with their start and end apart: 8 -> 14, of which waited for: 4 -> 8; matrix products, arithmetic and copies ran while one was open for 43% -> 0% of each run, Pallas kernels for 0% -> 24%
where the time goes in v4:
time: 54 us; the launch traced here: 53.7 us
  starting transfers between devices  20 us (37%)
  waiting for transfers between devices  18.2 us (34%)
  Pallas kernels  15.3 us (28%)
    ppermute x12, starting transfers between devices, partner(): lax.ppermute(x, axis, [(i, i ^ distance) for i in range(lax.axis_size(axi...  14.8 us
    ppermute x12, waiting for transfers between devices, partner(): lax.ppermute(x, axis, [(i, i ^ distance) for i in range(lax.axis_size(axi...  13.9 us
    ppermute x1, waiting for transfers between devices, shards(): below = lax.ppermute(first, 'sy', backward)  4.21 us
    pallas_call x1, Pallas kernels, shards(): pl.pallas_call(functools.partial(inner_kernel, count, depth), out_shape=(...  4.12 us
    ppermute x1, starting transfers between devices, shards(): above = lax.ppermute(last, 'sy', forward)  3.93 us
    pallas_call x1, Pallas kernels, shards(): pl.pallas_call(functools.partial(pack_kernel, count, depth, early, later)...  2.63 us
    pallas_call x1, Pallas kernels, shards(): pl.pallas_call(functools.partial(outer_kernel, count, depth), out_shape=(...  2.5 us
    pallas_call x2, Pallas kernels, shards(): pl.pallas_call(functools.partial(blend_kernel, count, depth, top, early,...  2.46 us
  transfers between devices with their start and end apart: 14, of which 8 were waited for; matrix products, arithmetic and copies ran while one was open for 0% of the time, Pallas kernels for 24%

profile of v4, /device:TPU:0, one launch (start us, length us, event | category | flops | bytes accessed | tf_op | source)
XLA Modules:
  0.0 53.7 jit_solution(14326875895699949239)
XLA Ops:
  0.0 1.1 %lead.1 = f32[2,32,2048]{2,1,0:T(8,128)S(1)} custom-call(f32[2,128,2048]{2,1,0:T(8,128)} %field.8), custom_call_target="tpu_custom_call" | custom-call | flops 2621440 | bytes 1048576 | tf_op jit(solution)/shard_map/lead/pallas_call | solution.py:450
  1.1 4.0 %collective-permute-start.4 = (f32[2,32,2048]{2,1,0:T(8,128)S(1)}, f32[2,32,2048]{2,1,0:T(8,128)S(1)}, u32[]{:S(2)}, u32[]{:S(2)}) collective-permute-start(f32[2,32,2048]{2,1,0:T(8,128)S(1)} %lead.1), channel_id=1, source_target_pairs={{0,3},{1,2},{2,1},{3,0},{4,7},{5,6},{6,5},{7,4},{8,11},{9,10},{10,... | collective-permute-start | bytes 1572872 | tf_op jit(solution)/shard_map/ppermute | solution.py:28
  5.0 1.4 %split.1 = (f32[2,32,2048]{2,1,0:T(8,128)S(1)}, f32[2,32,2048]{2,1,0:T(8,128)S(1)}, f32[2,2048]{1,0:T(2,128)S(1)}, f32[2,2048]{1,0:T(2,128)S(1)}) custom-call(f32[2,128,2048]{2,1,0:T(8,128)} %field.8), custom_call_target="tpu_custom_call" | custom-call | flops 10485760 | bytes 4194304 | tf_op jit(solution)/shard_map/split/pallas_call | solution.py:462
  6.4 0.6 %collective-permute-start.2 = (f32[2,32,2048]{2,1,0:T(8,128)S(1)}, f32[2,32,2048]{2,1,0:T(8,128)S(1)}, u32[]{:S(2)}, u32[]{:S(2)}) collective-permute-start(f32[2,32,2048]{2,1,0:T(8,128)S(1)} %get-tuple-element.43), channel_id=1, source_target_pairs={{0,1},{1,0},{2,3},{3,2},{4,5},{5,4},{6,7},{7,6},{8,9},{9,8},{10,11... | collective-permute-start | bytes 1572872 | tf_op jit(solution)/shard_map/ppermute | solution.py:28
  7.1 3.9 %collective-permute-start = (f32[2,2048]{1,0:T(2,128)S(1)}, f32[2,2048]{1,0:T(2,128)S(1)}, u32[]{:S(2)}, u32[]{:S(2)}) collective-permute-start(f32[2,2048]{1,0:T(2,128)S(1)} %get-tuple-element.38), channel_id=1, source_target_pairs={{0,4},{4,8},{8,12},{1,5},{5,9},{9,13},{2,6},{6,10},{10,14},{3,7},{... | collective-permute-start | bytes 49160 | tf_op jit(solution)/shard_map/ppermute | solution.py:478
  11.0 1.3 %collective-permute-start.1 = (f32[2,2048]{1,0:T(2,128)S(1)}, f32[2,2048]{1,0:T(2,128)S(1)}, u32[]{:S(2)}, u32[]{:S(2)}) collective-permute-start(f32[2,2048]{1,0:T(2,128)S(1)} %get-tuple-element.39), channel_id=1, source_target_pairs={{4,0},{8,4},{12,8},{5,1},{9,5},{13,9},{6,2},{10,6},{14,10},{7,3},{... | collective-permute-start | bytes 49160 | tf_op jit(solution)/shard_map/ppermute | solution.py:479
  12.4 4.2 %collective-permute-done.1.below = f32[2,2048]{1,0:T(2,128)S(1)} collective-permute-done((f32[2,2048]{1,0:T(2,128)S(1)}, f32[2,2048]{1,0:T(2,128)S(1)}, u32[]{:S(2)}, u32[]{:S(2)}) %collective-permute-start.1) | collective-permute-done | bytes 16416 | tf_op jit(solution)/shard_map/ppermute | solution.py:479
  16.7 2.6 %pack.1 = (f32[72,1024]{1,0:T(8,128)S(1)}, f32[72,1024]{1,0:T(8,128)S(1)}, f32[72,1024]{1,0:T(8,128)S(1)}, f32[8,1024]{1,0:T(8,128)S(1)}, s32[2,8,128]{2,1,0:T(8...) custom-call(f32[2,2048]{1,0:T(2,128)S(1)} %collective-permute-done.a, ...), custom_call_target="tpu_custom_call" | custom-call | flops 10485760 | bytes 4194304 | tf_op jit(solution)/shard_map/pack/pallas_call | solution.py:492
  19.3 2.5 %collective-permute-start.8 = (f32[72,1024]{1,0:T(8,128)S(1)}, f32[72,1024]{1,0:T(8,128)S(1)}, u32[]{:S(2)}, u32[]{:S(2)}) collective-permute-start(f32[72,1024]{1,0:T(8,128)S(1)} %get-tuple-element.55), channel_id=1, source_target_pairs={{0,3},{1,2},{2,1},{3,0},{4,7},{5,6},{6,5},{7,4},{8,11},{9,10},{10,... | collective-permute-start | bytes 884744 | tf_op jit(solution)/shard_map/ppermute | solution.py:28
  22.3 0.5 collective-permute-start.6
  22.9 6.8 %collective-permute-done.2.refs_0_ = f32[2,32,2048]{2,1,0:T(8,128)S(1)} collective-permute-done((f32[2,32,2048]{2,1,0:T(8,128)S(1)}, f32[2,32,2048]{2,1,0:T(8,128)S(1)}, u32[]{:S(2)}, u32[]{:S(2)}) %collective-permute-start.2) | collective-permute-done | bytes 524320 | tf_op jit(solution)/shard_map/ppermute | solution.py:28
  29.7 0.8 %side.1 = f32[8,32,128]{2,1,0:T(8,128)S(1)} custom-call(f32[2,128,2048]{2,1,0:T(8,128)} %field.8, f32[2,32,2048]{2,1,0:T(8,128)S(1)} %collective-permute-done.2.refs_0_, f32[2,32,2048]{2,1,0:T(8,128)S(1)} %collective-permute-done.3.refs_1_, f32[2,32,2048]{2,1,0:T(8,128)S(1)} %collective-permute-done.4.refs_2_), custom_call_target="tpu_custom_call" | custom-call | flops 655360 | bytes 262144 | tf_op jit(solution)/shard_map/side/pallas_call | solution.py:520
  30.5 1.3 %collective-permute-done.5.beside = f32[8,32,128]{2,1,0:T(8,128)S(1)} collective-permute-done((f32[8,32,128]{2,1,0:T(8,128)S(1)}, f32[8,32,128]{2,1,0:T(8,128)S(1)}, u32[]{:S(2)}, u32[]{:S(2)}) %collective-permute-start.5) | collective-permute-done | bytes 131104 | tf_op jit(solution)/shard_map/ppermute | solution.py:28
  31.8 4.1 %inner.1 = (f32[10,48,2304]{2,1,0:T(8,128)S(1)}, f32[8,32,2048]{2,1,0:T(8,128)S(1)}, f32[8,16,2048]{2,1,0:T(8,128)S(1)}, s32[2,2,32,2048]{3,2,1,0:T(8,128)S(1)}, f32[8,128]{1,0:T(8,128)}) custom-call(f32[2,128,2048]{2,1,0:T(8,128)} %field.8, f32[8,1024]{1,0:T(8,128)S(1)} %get-tuple-element.42.edges, f32[8,32,128]{2,1,0:T(8,128)S(1)} %collective-permute-done.5.beside, ...), custom_call_target="tpu_custom_call" | custom-call | flops 10485760 | bytes 4194304 | tf_op jit(solution)/shard_map/inner/pallas_call | solution.py:532
  36.0 2.5 %collective-permute-start.9 = (s32[2,16,2048]{2,1,0:T(8,128)S(1)}, s32[2,16,2048]{2,1,0:T(8,128)S(1)}, u32[]{:S(2)}, u32[]{:S(2)}) collective-permute-start(s32[2,16,2048]{2,1,0:T(8,128)S(1)} %get-tuple-element.59), channel_id=1, source_target_pairs={{0,3},{1,2},{2,1},{3,0},{4,7},{5,6},{6,5},{7,4},{8,11},{9,10},{10,... | collective-permute-start | bytes 786440 | tf_op jit(solution)/shard_map/ppermute | solution.py:28
  38.5 3.1 %collective-permute-done.7.refs_1_ = f32[72,1024]{1,0:T(8,128)S(1)} collective-permute-done((f32[72,1024]{1,0:T(8,128)S(1)}, f32[72,1024]{1,0:T(8,128)S(1)}, u32[]{:S(2)}, u32[]{:S(2)}) %collective-permute-start.7) | collective-permute-done | bytes 294944 | tf_op jit(solution)/shard_map/ppermute | solution.py:28
  41.6 0.7 %collective-permute-done.6.refs_0_ = f32[72,1024]{1,0:T(8,128)S(1)} collective-permute-done((f32[72,1024]{1,0:T(8,128)S(1)}, f32[72,1024]{1,0:T(8,128)S(1)}, u32[]{:S(2)}, u32[]{:S(2)}) %collective-permute-start.6) | collective-permute-done | bytes 294944 | tf_op jit(solution)/shard_map/ppermute | solution.py:28
  42.3 1.5 %collective-permute-start.12 = (s32[2,8,2048]{2,1,0:T(8,128)S(1)}, s32[2,8,2048]{2,1,0:T(8,128)S(1)}, u32[]{:S(2)}, u32[]{:S(2)}) collective-permute-start(s32[2,8,2048]{2,1,0:T(8,128)S(1)} %get-tuple-element.65), channel_id=1, source_target_pairs={{0,1},{1,0},{2,3},{3,2},{4,5},{5,4},{6,7},{7,6},{8,9},{9,8},{10,11... | collective-permute-start | bytes 393224 | tf_op jit(solution)/shard_map/ppermute | solution.py:28
  43.8 1.3 %collective-permute-start.13 = (s32[2,8,2048]{2,1,0:T(8,128)S(1)}, s32[2,8,2048]{2,1,0:T(8,128)S(1)}, u32[]{:S(2)}, u32[]{:S(2)}) collective-permute-start(s32[2,8,2048]{2,1,0:T(8,128)S(1)} %get-tuple-element.67), channel_id=1, source_target_pairs={{0,2},{1,3},{2,0},{3,1},{4,6},{5,7},{6,4},{7,5},{8,10},{9,11},{10,... | collective-permute-start | bytes 393224 | tf_op jit(solution)/shard_map/ppermute | solution.py:28
  45.6 0.7 %collective-permute-start.11 = (s32[2,8,2048]{2,1,0:T(8,128)S(1)}, s32[2,8,2048]{2,1,0:T(8,128)S(1)}, u32[]{:S(2)}, u32[]{:S(2)}) collective-permute-start(s32[2,8,2048]{2,1,0:T(8,128)S(1)} %get-tuple-element.63), channel_id=1, source_target_pairs={{0,2},{1,3},{2,0},{3,1},{4,6},{5,7},{6,4},{7,5},{8,10},{9,11},{10,... | collective-permute-start | bytes 393224 | tf_op jit(solution)/shard_map/ppermute | solution.py:28
  46.4 2.5 %outer.1 = (f32[8,16,2048]{2,1,0:T(8,128)S(1)}, f32[4,32,2048]{2,1,0:T(8,128)}) custom-call(s32[2,8,128]{2,1,0:T(8,128)S(1)} %get-tuple-element.40.entries, s32[32,128]{1,0:T(8,128)S(1)} %get-tuple-element.41.flips, f32[10,48,2304]{2,1,0:T(8,128)S(1)} %get-tuple-element.47.ext, f32[8,32,2048]{2,1,0:T(8,128)S(1)} %get-tuple-element.46.scaled, ...), custom_call_target="tpu_custom_call" | custom-call | flops 10485760 | bytes 4194304 | tf_op jit(solution)/shard_map/outer/pallas_call | solution.py:551
  49.3 1.5 %collective-permute-done.12.refs_0_ = s32[2,8,2048]{2,1,0:T(8,128)S(1)} collective-permute-done((s32[2,8,2048]{2,1,0:T(8,128)S(1)}, s32[2,8,2048]{2,1,0:T(8,128)S(1)}, u32[]{:S(2)}, u32[]{:S(2)}) %collective-permute-start.12) | collective-permute-done | bytes 131104 | tf_op jit(solution)/shard_map/ppermute | solution.py:28
  50.8 1.2 %blend.2.refs_2_ = f32[4,32,2048]{2,1,0:T(8,128)} custom-call(s32[2,8,128]{2,1,0:T(8,128)S(1)} %get-tuple-element.40.entries, s32[32,128]{1,0:T(8,128)S(1)} %get-tuple-element.41.flips, f32[8,32,2048]{2,1,0:T(8,128)S(1)} %get-tuple-element.46.scaled, f32[8,16,2048]{2,1,0:T(8,128)S(1)} %get-tuple-element.48.inner.shading, ...), custom_call_target="tpu_custom_call", output_to_operand_aliasing={{}: (8, {})} | custom-call | flops 2621440 | bytes 1048576 | tf_op jit(solution)/shard_map/blend/pallas_call | solution.py:582
  52.4 1.2 %blend.3 = f32[4,32,2048]{2,1,0:T(8,128)} custom-call(s32[2,8,128]{2,1,0:T(8,128)S(1)} %get-tuple-element.40.entries, s32[32,128]{1,0:T(8,128)S(1)} %get-tuple-element.41.flips, f32[8,32,2048]{2,1,0:T(8,128)S(1)} %get-tuple-element.46.scaled, f32[8,16,2048]{2,1,0:T(8,128)S(1)} %get-tuple-element.56.shading, ...), custom_call_target="tpu_custom_call", output_to_operand_aliasing={{}: (8, {})} | custom-call | flops 2621440 | bytes 1048576 | tf_op jit(solution)/shard_map/blend/pallas_call | solution.py:582
  (17 shorter events, 2.1 us)
Async XLA Ops:
  0.0 16.7 %copy-start.1 = (s32[128]{0:T(128)S(1)}, s32[128]{0:T(128)}, u32[]{:S(2)}) copy-start(s32[128]{0:T(128)} %march.1) | copy-start | bytes 1540
  0.0 16.7 %copy-start = (bf16[4,128]{1,0:T(4,128)(2,1)S(1)}, bf16[4,128]{1,0:T(4,128)(2,1)}, u32[]{:S(2)}) copy-start(bf16[4,128]{1,0:T(4,128)(2,1)} %table.1) | copy-start | bytes 3076
  1.1 18.2 %collective-permute-start.4 = (f32[2,32,2048]{2,1,0:T(8,128)S(1)}, f32[2,32,2048]{2,1,0:T(8,128)S(1)}, u32[]{:S(2)}, u32[]{:S(2)}) collective-permute-start(f32[2,32,2048]{2,1,0:T(8,128)S(1)} %lead.1), channel_id=1, source_target_pairs={{0,3},{1,2},{2,1},{3,0},{4,7},{5,6},{6,5},{7,4},{8,11},{9,10},{10,... | collective-permute-start | bytes 1572872 | tf_op jit(solution)/shard_map/ppermute | solution.py:28
  6.4 23.2 %collective-permute-start.2 = (f32[2,32,2048]{2,1,0:T(8,128)S(1)}, f32[2,32,2048]{2,1,0:T(8,128)S(1)}, u32[]{:S(2)}, u32[]{:S(2)}) collective-permute-start(f32[2,32,2048]{2,1,0:T(8,128)S(1)} %get-tuple-element.43), channel_id=1, source_target_pairs={{0,1},{1,0},{2,3},{3,2},{4,5},{5,4},{6,7},{7,6},{8,9},{9,8},{10,11... | collective-permute-start | bytes 1572872 | tf_op jit(solution)/shard_map/ppermute | solution.py:28
  7.0 22.6 %collective-permute-start.3 = (f32[2,32,2048]{2,1,0:T(8,128)S(1)}, f32[2,32,2048]{2,1,0:T(8,128)S(1)}, u32[]{:S(2)}, u32[]{:S(2)}) collective-permute-start(f32[2,32,2048]{2,1,0:T(8,128)S(1)} %get-tuple-element.44), channel_id=1, source_target_pairs={{0,2},{1,3},{2,0},{3,1},{4,6},{5,7},{6,4},{7,5},{8,10},{9,11},{10,... | collective-permute-start | bytes 1572872 | tf_op jit(solution)/shard_map/ppermute | solution.py:28
  7.1 5.4 %collective-permute-start = (f32[2,2048]{1,0:T(2,128)S(1)}, f32[2,2048]{1,0:T(2,128)S(1)}, u32[]{:S(2)}, u32[]{:S(2)}) collective-permute-start(f32[2,2048]{1,0:T(2,128)S(1)} %get-tuple-element.38), channel_id=1, source_target_pairs={{0,4},{4,8},{8,12},{1,5},{5,9},{9,13},{2,6},{6,10},{10,14},{3,7},{... | collective-permute-start | bytes 49160 | tf_op jit(solution)/shard_map/ppermute | solution.py:478
  11.0 5.6 %collective-permute-start.1 = (f32[2,2048]{1,0:T(2,128)S(1)}, f32[2,2048]{1,0:T(2,128)S(1)}, u32[]{:S(2)}, u32[]{:S(2)}) collective-permute-start(f32[2,2048]{1,0:T(2,128)S(1)} %get-tuple-element.39), channel_id=1, source_target_pairs={{4,0},{8,4},{12,8},{5,1},{9,5},{13,9},{6,2},{10,6},{14,10},{7,3},{... | collective-permute-start | bytes 49160 | tf_op jit(solution)/shard_map/ppermute | solution.py:479
  19.3 16.7 %collective-permute-start.8 = (f32[72,1024]{1,0:T(8,128)S(1)}, f32[72,1024]{1,0:T(8,128)S(1)}, u32[]{:S(2)}, u32[]{:S(2)}) collective-permute-start(f32[72,1024]{1,0:T(8,128)S(1)} %get-tuple-element.55), channel_id=1, source_target_pairs={{0,3},{1,2},{2,1},{3,0},{4,7},{5,6},{6,5},{7,4},{8,11},{9,10},{10,... | collective-permute-start | bytes 884744 | tf_op jit(solution)/shard_map/ppermute | solution.py:28
  21.8 19.8 %collective-permute-start.7 = (f32[72,1024]{1,0:T(8,128)S(1)}, f32[72,1024]{1,0:T(8,128)S(1)}, u32[]{:S(2)}, u32[]{:S(2)}) collective-permute-start(f32[72,1024]{1,0:T(8,128)S(1)} %get-tuple-element.53), channel_id=1, source_target_pairs={{0,2},{1,3},{2,0},{3,1},{4,6},{5,7},{6,4},{7,5},{8,10},{9,11},{10,... | collective-permute-start | bytes 884744 | tf_op jit(solution)/shard_map/ppermute | solution.py:28
  22.3 20.0 %collective-permute-start.6 = (f32[72,1024]{1,0:T(8,128)S(1)}, f32[72,1024]{1,0:T(8,128)S(1)}, u32[]{:S(2)}, u32[]{:S(2)}) collective-permute-start(f32[72,1024]{1,0:T(8,128)S(1)} %get-tuple-element.51), channel_id=1, source_target_pairs={{0,1},{1,0},{2,3},{3,2},{4,5},{5,4},{6,7},{7,6},{8,9},{9,8},{10,11... | collective-permute-start | bytes 884744 | tf_op jit(solution)/shard_map/ppermute | solution.py:28
  30.4 1.4 %collective-permute-start.5 = (f32[8,32,128]{2,1,0:T(8,128)S(1)}, f32[8,32,128]{2,1,0:T(8,128)S(1)}, u32[]{:S(2)}, u32[]{:S(2)}) collective-permute-start(f32[8,32,128]{2,1,0:T(8,128)S(1)} %side.1), channel_id=1, source_target_pairs={{0,16},{16,0},{1,17},{17,1},{2,18},{18,2},{3,19},{19,3},{4,20},{20... | collective-permute-start | bytes 393224 | tf_op jit(solution)/shard_map/ppermute | solution.py:28
  36.0 12.9 %collective-permute-start.9 = (s32[2,16,2048]{2,1,0:T(8,128)S(1)}, s32[2,16,2048]{2,1,0:T(8,128)S(1)}, u32[]{:S(2)}, u32[]{:S(2)}) collective-permute-start(s32[2,16,2048]{2,1,0:T(8,128)S(1)} %get-tuple-element.59), channel_id=1, source_target_pairs={{0,3},{1,2},{2,1},{3,0},{4,7},{5,6},{6,5},{7,4},{8,11},{9,10},{10,... | collective-permute-start | bytes 786440 | tf_op jit(solution)/shard_map/ppermute | solution.py:28
  42.3 8.4 %collective-permute-start.12 = (s32[2,8,2048]{2,1,0:T(8,128)S(1)}, s32[2,8,2048]{2,1,0:T(8,128)S(1)}, u32[]{:S(2)}, u32[]{:S(2)}) collective-permute-start(s32[2,8,2048]{2,1,0:T(8,128)S(1)} %get-tuple-element.65), channel_id=1, source_target_pairs={{0,1},{1,0},{2,3},{3,2},{4,5},{5,4},{6,7},{7,6},{8,9},{9,8},{10,11... | collective-permute-start | bytes 393224 | tf_op jit(solution)/shard_map/ppermute | solution.py:28
  43.8 6.9 %collective-permute-start.13 = (s32[2,8,2048]{2,1,0:T(8,128)S(1)}, s32[2,8,2048]{2,1,0:T(8,128)S(1)}, u32[]{:S(2)}, u32[]{:S(2)}) collective-permute-start(s32[2,8,2048]{2,1,0:T(8,128)S(1)} %get-tuple-element.67), channel_id=1, source_target_pairs={{0,2},{1,3},{2,0},{3,1},{4,6},{5,7},{6,4},{7,5},{8,10},{9,11},{10,... | collective-permute-start | bytes 393224 | tf_op jit(solution)/shard_map/ppermute | solution.py:28
  45.1 7.3 %collective-permute-start.10 = (s32[2,8,2048]{2,1,0:T(8,128)S(1)}, s32[2,8,2048]{2,1,0:T(8,128)S(1)}, u32[]{:S(2)}, u32[]{:S(2)}) collective-permute-start(s32[2,8,2048]{2,1,0:T(8,128)S(1)} %get-tuple-element.61), channel_id=1, source_target_pairs={{0,1},{1,0},{2,3},{3,2},{4,5},{5,4},{6,7},{7,6},{8,9},{9,8},{10,11... | collective-permute-start | bytes 393224 | tf_op jit(solution)/shard_map/ppermute | solution.py:28
  45.6 6.8 %collective-permute-start.11 = (s32[2,8,2048]{2,1,0:T(8,128)S(1)}, s32[2,8,2048]{2,1,0:T(8,128)S(1)}, u32[]{:S(2)}, u32[]{:S(2)}) collective-permute-start(s32[2,8,2048]{2,1,0:T(8,128)S(1)} %get-tuple-element.63), channel_id=1, source_target_pairs={{0,2},{1,3},{2,0},{3,1},{4,6},{5,7},{6,4},{7,5},{8,10},{9,11},{10,... | collective-permute-start | bytes 393224 | tf_op jit(solution)/shard_map/ppermute | solution.py:28

commit v5 on v4

--- a/solution.py
+++ b/solution.py
@@ -438,7 +438,7 @@
         return pl.CostEstimate(flops=20 * cells, bytes_accessed=8 * cells, transcendentals=cells)
 
     done = {}
-    order = {"message": lambda index: [("field", 0)], "bins": lambda index: [("message", index), "inner"]}
+    order = {"message": lambda index: [("field", 0)], "bins": lambda index: [("message", 0), "inner"]}
 
     def send(name, array, slot):
         index = partners.index(slot)
@@ -478,7 +478,7 @@
     above = lax.ppermute(last, "sy", forward)
     below = lax.ppermute(first, "sy", backward)
 
-    early = max(rows // 2 // ROWS, 1) * ROWS
+    early = max(rows - ROWS, ROWS)
     late = rows - early
     later = []
     if late:

time: 54 us -> 54 us (level)
  waiting for transfers between devices: 18.2 us -> 22.1 us
  starting transfers between devices: 20 us -> 17 us
  Pallas kernels: 15.3 us -> 14.5 us
    ppermute x12 -> x10, waiting for transfers between devices: 13.9 us -> 17.7 us  [partner(): lax.ppermute(x, axis, [(i, i ^ distance) for i in range(lax.axis_size(axi...]
    ppermute x12 -> x10, starting transfers between devices: 14.8 us -> 11.8 us  [partner(): lax.ppermute(x, axis, [(i, i ^ distance) for i in range(lax.axis_size(axi...]
    pallas_call x2 -> x1, Pallas kernels: 2.46 us -> 1.23 us  [shards(): pl.pallas_call(functools.partial(blend_kernel, count, depth, top, early,...]
    pallas_call x1, Pallas kernels: 2.5 us -> 3.08 us  [shards(): pl.pallas_call(functools.partial(outer_kernel, count, depth), out_shape=(...]
  transfers between devices with their start and end apart: 14 -> 12, of which waited for: 8 -> 8; matrix products, arithmetic and copies ran while one was open for 0% -> 0% of each run, Pallas kernels for 24% -> 23%
where the time goes in v5:
time: 54 us; the launch traced here: 53.6 us
  waiting for transfers between devices  22.1 us (41%)
  starting transfers between devices  17 us (31%)
  Pallas kernels  14.5 us (27%)
    ppermute x10, waiting for transfers between devices, partner(): lax.ppermute(x, axis, [(i, i ^ distance) for i in range(lax.axis_size(axi...  17.7 us
    ppermute x10, starting transfers between devices, partner(): lax.ppermute(x, axis, [(i, i ^ distance) for i in range(lax.axis_size(axi...  11.8 us
    ppermute x1, waiting for transfers between devices, shards(): below = lax.ppermute(first, 'sy', backward)  4.21 us
    pallas_call x1, Pallas kernels, shards(): pl.pallas_call(functools.partial(inner_kernel, count, depth), out_shape=(...  4.12 us
    ppermute x1, starting transfers between devices, shards(): above = lax.ppermute(last, 'sy', forward)  3.93 us
    pallas_call x1, Pallas kernels, shards(): pl.pallas_call(functools.partial(outer_kernel, count, depth), out_shape=(...  3.08 us
    pallas_call x1, Pallas kernels, shards(): pl.pallas_call(functools.partial(pack_kernel, count, depth, early, later)...  2.63 us
    pallas_call x1, Pallas kernels, shards(): pl.pallas_call(functools.partial(split_kernel, count, depth, others), out...  1.38 us
  transfers between devices with their start and end apart: 12, of which 8 were waited for; matrix products, arithmetic and copies ran while one was open for 0% of the time, Pallas kernels for 23%

profile of v5, /device:TPU:0, one launch (start us, length us, event | category | flops | bytes accessed | tf_op | source)
XLA Modules:
  0.0 53.6 jit_solution(11800917280502666314)
XLA Ops:
  0.0 1.1 %lead.1 = f32[2,32,2048]{2,1,0:T(8,128)S(1)} custom-call(f32[2,128,2048]{2,1,0:T(8,128)} %field.8), custom_call_target="tpu_custom_call" | custom-call | flops 2621440 | bytes 1048576 | tf_op jit(solution)/shard_map/lead/pallas_call | solution.py:450
  1.1 4.0 %collective-permute-start.4 = (f32[2,32,2048]{2,1,0:T(8,128)S(1)}, f32[2,32,2048]{2,1,0:T(8,128)S(1)}, u32[]{:S(2)}, u32[]{:S(2)}) collective-permute-start(f32[2,32,2048]{2,1,0:T(8,128)S(1)} %lead.1), channel_id=1, source_target_pairs={{0,3},{1,2},{2,1},{3,0},{4,7},{5,6},{6,5},{7,4},{8,11},{9,10},{10,... | collective-permute-start | bytes 1572872 | tf_op jit(solution)/shard_map/ppermute | solution.py:28
  5.0 1.4 %split.1 = (f32[2,32,2048]{2,1,0:T(8,128)S(1)}, f32[2,32,2048]{2,1,0:T(8,128)S(1)}, f32[2,2048]{1,0:T(2,128)S(1)}, f32[2,2048]{1,0:T(2,128)S(1)}) custom-call(f32[2,128,2048]{2,1,0:T(8,128)} %field.8), custom_call_target="tpu_custom_call" | custom-call | flops 10485760 | bytes 4194304 | tf_op jit(solution)/shard_map/split/pallas_call | solution.py:462
  6.4 0.6 %collective-permute-start.2 = (f32[2,32,2048]{2,1,0:T(8,128)S(1)}, f32[2,32,2048]{2,1,0:T(8,128)S(1)}, u32[]{:S(2)}, u32[]{:S(2)}) collective-permute-start(f32[2,32,2048]{2,1,0:T(8,128)S(1)} %get-tuple-element.39), channel_id=1, source_target_pairs={{0,1},{1,0},{2,3},{3,2},{4,5},{5,4},{6,7},{7,6},{8,9},{9,8},{10,11... | collective-permute-start | bytes 1572872 | tf_op jit(solution)/shard_map/ppermute | solution.py:28
  7.1 3.9 %collective-permute-start = (f32[2,2048]{1,0:T(2,128)S(1)}, f32[2,2048]{1,0:T(2,128)S(1)}, u32[]{:S(2)}, u32[]{:S(2)}) collective-permute-start(f32[2,2048]{1,0:T(2,128)S(1)} %get-tuple-element.34), channel_id=1, source_target_pairs={{0,4},{4,8},{8,12},{1,5},{5,9},{9,13},{2,6},{6,10},{10,14},{3,7},{... | collective-permute-start | bytes 49160 | tf_op jit(solution)/shard_map/ppermute | solution.py:478
  11.0 1.3 %collective-permute-start.1 = (f32[2,2048]{1,0:T(2,128)S(1)}, f32[2,2048]{1,0:T(2,128)S(1)}, u32[]{:S(2)}, u32[]{:S(2)}) collective-permute-start(f32[2,2048]{1,0:T(2,128)S(1)} %get-tuple-element.35), channel_id=1, source_target_pairs={{4,0},{8,4},{12,8},{5,1},{9,5},{13,9},{6,2},{10,6},{14,10},{7,3},{... | collective-permute-start | bytes 49160 | tf_op jit(solution)/shard_map/ppermute | solution.py:479
  12.4 4.2 %collective-permute-done.1.below = f32[2,2048]{1,0:T(2,128)S(1)} collective-permute-done((f32[2,2048]{1,0:T(2,128)S(1)}, f32[2,2048]{1,0:T(2,128)S(1)}, u32[]{:S(2)}, u32[]{:S(2)}) %collective-permute-start.1) | collective-permute-done | bytes 16416 | tf_op jit(solution)/shard_map/ppermute | solution.py:479
  16.7 2.6 %pack.1 = (f32[104,1024]{1,0:T(8,128)S(1)}, f32[104,1024]{1,0:T(8,128)S(1)}, f32[104,1024]{1,0:T(8,128)S(1)}, f32[8,1024]{1,0:T(8,128)S(1)}, s32[2,8,128]{2,1,0:...) custom-call(f32[2,2048]{1,0:T(2,128)S(1)} %collective-permute-done.a, ...), custom_call_target="tpu_custom_call" | custom-call | flops 10485760 | bytes 4194304 | tf_op jit(solution)/shard_map/pack/pallas_call | solution.py:492
  19.3 2.5 %collective-permute-start.8 = (f32[104,1024]{1,0:T(8,128)S(1)}, f32[104,1024]{1,0:T(8,128)S(1)}, u32[]{:S(2)}, u32[]{:S(2)}) collective-permute-start(f32[104,1024]{1,0:T(8,128)S(1)} %get-tuple-element.51), channel_id=1, source_target_pairs={{0,3},{1,2},{2,1},{3,0},{4,7},{5,6},{6,5},{7,4},{8,11},{9,10},{10,... | collective-permute-start | bytes 1277960 | tf_op jit(solution)/shard_map/ppermute | solution.py:28
  21.8 0.5 collective-permute-start.7
  22.3 0.5 collective-permute-start.6
  22.9 6.8 %collective-permute-done.2.refs_0_ = f32[2,32,2048]{2,1,0:T(8,128)S(1)} collective-permute-done((f32[2,32,2048]{2,1,0:T(8,128)S(1)}, f32[2,32,2048]{2,1,0:T(8,128)S(1)}, u32[]{:S(2)}, u32[]{:S(2)}) %collective-permute-start.2) | collective-permute-done | bytes 524320 | tf_op jit(solution)/shard_map/ppermute | solution.py:28
  29.7 0.8 %side.1 = f32[8,32,128]{2,1,0:T(8,128)S(1)} custom-call(f32[2,128,2048]{2,1,0:T(8,128)} %field.8, f32[2,32,2048]{2,1,0:T(8,128)S(1)} %collective-permute-done.2.refs_0_, f32[2,32,2048]{2,1,0:T(8,128)S(1)} %collective-permute-done.3.refs_1_, f32[2,32,2048]{2,1,0:T(8,128)S(1)} %collective-permute-done.4.refs_2_), custom_call_target="tpu_custom_call" | custom-call | flops 655360 | bytes 262144 | tf_op jit(solution)/shard_map/side/pallas_call | solution.py:520
  30.5 1.3 %collective-permute-done.5.beside = f32[8,32,128]{2,1,0:T(8,128)S(1)} collective-permute-done((f32[8,32,128]{2,1,0:T(8,128)S(1)}, f32[8,32,128]{2,1,0:T(8,128)S(1)}, u32[]{:S(2)}, u32[]{:S(2)}) %collective-permute-start.5) | collective-permute-done | bytes 131104 | tf_op jit(solution)/shard_map/ppermute | solution.py:28
  31.8 4.1 %inner.1 = (f32[10,48,2304]{2,1,0:T(8,128)S(1)}, f32[8,32,2048]{2,1,0:T(8,128)S(1)}, f32[8,16,2048]{2,1,0:T(8,128)S(1)}, s32[2,2,32,2048]{3,2,1,0:T(8,128)S(1)}, f32[8,128]{1,0:T(8,128)}) custom-call(f32[2,128,2048]{2,1,0:T(8,128)} %field.8, f32[8,1024]{1,0:T(8,128)S(1)} %get-tuple-element.38.edges, f32[8,32,128]{2,1,0:T(8,128)S(1)} %collective-permute-done.5.beside, ...), custom_call_target="tpu_custom_call" | custom-call | flops 10485760 | bytes 4194304 | tf_op jit(solution)/shard_map/inner/pallas_call | solution.py:532
  36.0 2.3 %collective-permute-done.8.refs_2_ = f32[104,1024]{1,0:T(8,128)S(1)} collective-permute-done((f32[104,1024]{1,0:T(8,128)S(1)}, f32[104,1024]{1,0:T(8,128)S(1)}, u32[]{:S(2)}, u32[]{:S(2)}) %collective-permute-start.8) | collective-permute-done | bytes 426016 | tf_op jit(solution)/shard_map/ppermute | solution.py:28
  38.3 3.0 %collective-permute-start.9 = (s32[2,8,2048]{2,1,0:T(8,128)S(1)}, s32[2,8,2048]{2,1,0:T(8,128)S(1)}, u32[]{:S(2)}, u32[]{:S(2)}) collective-permute-start(s32[2,8,2048]{2,1,0:T(8,128)S(1)} %get-tuple-element.55), channel_id=1, source_target_pairs={{0,3},{1,2},{2,1},{3,0},{4,7},{5,6},{6,5},{7,4},{8,11},{9,10},{10,... | collective-permute-start | bytes 393224 | tf_op jit(solution)/shard_map/ppermute | solution.py:28
  41.2 0.5 collective-permute-start.10
  41.8 5.6 %collective-permute-done.7.refs_1_ = f32[104,1024]{1,0:T(8,128)S(1)} collective-permute-done((f32[104,1024]{1,0:T(8,128)S(1)}, f32[104,1024]{1,0:T(8,128)S(1)}, u32[]{:S(2)}, u32[]{:S(2)}) %collective-permute-start.7) | collective-permute-done | bytes 426016 | tf_op jit(solution)/shard_map/ppermute | solution.py:28
  47.4 0.6 %collective-permute-done.6.refs_0_ = f32[104,1024]{1,0:T(8,128)S(1)} collective-permute-done((f32[104,1024]{1,0:T(8,128)S(1)}, f32[104,1024]{1,0:T(8,128)S(1)}, u32[]{:S(2)}, u32[]{:S(2)}) %collective-permute-start.6) | collective-permute-done | bytes 426016 | tf_op jit(solution)/shard_map/ppermute | solution.py:28
  47.9 3.1 %outer.1 = (f32[8,16,2048]{2,1,0:T(8,128)S(1)}, f32[4,32,2048]{2,1,0:T(8,128)}) custom-call(s32[2,8,128]{2,1,0:T(8,128)S(1)} %get-tuple-element.36.entries, s32[32,128]{1,0:T(8,128)S(1)} %get-tuple-element.37.flips, f32[10,48,2304]{2,1,0:T(8,128)S(1)} %get-tuple-element.43.ext, f32[8,32,2048]{2,1,0:T(8,128)S(1)} %get-tuple-element.42.scaled, ...), custom_call_target="tpu_custom_call" | custom-call | flops 10485760 | bytes 4194304 | tf_op jit(solution)/shard_map/outer/pallas_call | solution.py:551
  51.0 0.2 look.1.found
  51.3 1.2 %collective-permute-done.10.refs_0_ = s32[2,8,2048]{2,1,0:T(8,128)S(1)} collective-permute-done((s32[2,8,2048]{2,1,0:T(8,128)S(1)}, s32[2,8,2048]{2,1,0:T(8,128)S(1)}, u32[]{:S(2)}, u32[]{:S(2)}) %collective-permute-start.10) | collective-permute-done | bytes 131104 | tf_op jit(solution)/shard_map/ppermute | solution.py:28
  52.4 1.2 %blend.1 = f32[4,32,2048]{2,1,0:T(8,128)} custom-call(s32[2,8,128]{2,1,0:T(8,128)S(1)} %get-tuple-element.36.entries, s32[32,128]{1,0:T(8,128)S(1)} %get-tuple-element.37.flips, f32[8,32,2048]{2,1,0:T(8,128)S(1)} %get-tuple-element.42.scaled, f32[8,16,2048]{2,1,0:T(8,128)S(1)} %get-tuple-element.52.shading, ...), custom_call_target="tpu_custom_call", output_to_operand_aliasing={{}: (8, {})} | custom-call | flops 2621440 | bytes 1048576 | tf_op jit(solution)/shard_map/blend/pallas_call | solution.py:582
  (12 shorter events, 0.3 us)
Async XLA Ops:
  0.0 16.7 %copy-start.1 = (s32[128]{0:T(128)S(1)}, s32[128]{0:T(128)}, u32[]{:S(2)}) copy-start(s32[128]{0:T(128)} %march.1) | copy-start | bytes 1540
  0.0 16.7 %copy-start = (bf16[4,128]{1,0:T(4,128)(2,1)S(1)}, bf16[4,128]{1,0:T(4,128)(2,1)}, u32[]{:S(2)}) copy-start(bf16[4,128]{1,0:T(4,128)(2,1)} %table.1) | copy-start | bytes 3076
  1.1 18.2 %collective-permute-start.4 = (f32[2,32,2048]{2,1,0:T(8,128)S(1)}, f32[2,32,2048]{2,1,0:T(8,128)S(1)}, u32[]{:S(2)}, u32[]{:S(2)}) collective-permute-start(f32[2,32,2048]{2,1,0:T(8,128)S(1)} %lead.1), channel_id=1, source_target_pairs={{0,3},{1,2},{2,1},{3,0},{4,7},{5,6},{6,5},{7,4},{8,11},{9,10},{10,... | collective-permute-start | bytes 1572872 | tf_op jit(solution)/shard_map/ppermute | solution.py:28
  6.4 23.2 %collective-permute-start.2 = (f32[2,32,2048]{2,1,0:T(8,128)S(1)}, f32[2,32,2048]{2,1,0:T(8,128)S(1)}, u32[]{:S(2)}, u32[]{:S(2)}) collective-permute-start(f32[2,32,2048]{2,1,0:T(8,128)S(1)} %get-tuple-element.39), channel_id=1, source_target_pairs={{0,1},{1,0},{2,3},{3,2},{4,5},{5,4},{6,7},{7,6},{8,9},{9,8},{10,11... | collective-permute-start | bytes 1572872 | tf_op jit(solution)/shard_map/ppermute | solution.py:28
  7.0 22.6 %collective-permute-start.3 = (f32[2,32,2048]{2,1,0:T(8,128)S(1)}, f32[2,32,2048]{2,1,0:T(8,128)S(1)}, u32[]{:S(2)}, u32[]{:S(2)}) collective-permute-start(f32[2,32,2048]{2,1,0:T(8,128)S(1)} %get-tuple-element.40), channel_id=1, source_target_pairs={{0,2},{1,3},{2,0},{3,1},{4,6},{5,7},{6,4},{7,5},{8,10},{9,11},{10,... | collective-permute-start | bytes 1572872 | tf_op jit(solution)/shard_map/ppermute | solution.py:28
  7.1 5.4 %collective-permute-start = (f32[2,2048]{1,0:T(2,128)S(1)}, f32[2,2048]{1,0:T(2,128)S(1)}, u32[]{:S(2)}, u32[]{:S(2)}) collective-permute-start(f32[2,2048]{1,0:T(2,128)S(1)} %get-tuple-element.34), channel_id=1, source_target_pairs={{0,4},{4,8},{8,12},{1,5},{5,9},{9,13},{2,6},{6,10},{10,14},{3,7},{... | collective-permute-start | bytes 49160 | tf_op jit(solution)/shard_map/ppermute | solution.py:478
  11.0 5.6 %collective-permute-start.1 = (f32[2,2048]{1,0:T(2,128)S(1)}, f32[2,2048]{1,0:T(2,128)S(1)}, u32[]{:S(2)}, u32[]{:S(2)}) collective-permute-start(f32[2,2048]{1,0:T(2,128)S(1)} %get-tuple-element.35), channel_id=1, source_target_pairs={{4,0},{8,4},{12,8},{5,1},{9,5},{13,9},{6,2},{10,6},{14,10},{7,3},{... | collective-permute-start | bytes 49160 | tf_op jit(solution)/shard_map/ppermute | solution.py:479
  19.3 18.9 %collective-permute-start.8 = (f32[104,1024]{1,0:T(8,128)S(1)}, f32[104,1024]{1,0:T(8,128)S(1)}, u32[]{:S(2)}, u32[]{:S(2)}) collective-permute-start(f32[104,1024]{1,0:T(8,128)S(1)} %get-tuple-element.51), channel_id=1, source_target_pairs={{0,3},{1,2},{2,1},{3,0},{4,7},{5,6},{6,5},{7,4},{8,11},{9,10},{10,... | collective-permute-start | bytes 1277960 | tf_op jit(solution)/shard_map/ppermute | solution.py:28
  21.8 25.6 %collective-permute-start.7 = (f32[104,1024]{1,0:T(8,128)S(1)}, f32[104,1024]{1,0:T(8,128)S(1)}, u32[]{:S(2)}, u32[]{:S(2)}) collective-permute-start(f32[104,1024]{1,0:T(8,128)S(1)} %get-tuple-element.49), channel_id=1, source_target_pairs={{0,2},{1,3},{2,0},{3,1},{4,6},{5,7},{6,4},{7,5},{8,10},{9,11},{10,... | collective-permute-start | bytes 1277960 | tf_op jit(solution)/shard_map/ppermute | solution.py:28
  22.3 25.6 %collective-permute-start.6 = (f32[104,1024]{1,0:T(8,128)S(1)}, f32[104,1024]{1,0:T(8,128)S(1)}, u32[]{:S(2)}, u32[]{:S(2)}) collective-permute-start(f32[104,1024]{1,0:T(8,128)S(1)} %get-tuple-element.47), channel_id=1, source_target_pairs={{0,1},{1,0},{2,3},{3,2},{4,5},{5,4},{6,7},{7,6},{8,9},{9,8},{10,11... | collective-permute-start | bytes 1277960 | tf_op jit(solution)/shard_map/ppermute | solution.py:28
  30.4 1.4 %collective-permute-start.5 = (f32[8,32,128]{2,1,0:T(8,128)S(1)}, f32[8,32,128]{2,1,0:T(8,128)S(1)}, u32[]{:S(2)}, u32[]{:S(2)}) collective-permute-start(f32[8,32,128]{2,1,0:T(8,128)S(1)} %side.1), channel_id=1, source_target_pairs={{0,16},{16,0},{1,17},{17,1},{2,18},{18,2},{3,19},{19,3},{4,20},{20... | collective-permute-start | bytes 393224 | tf_op jit(solution)/shard_map/ppermute | solution.py:28
  38.3 12.8 %collective-permute-start.9 = (s32[2,8,2048]{2,1,0:T(8,128)S(1)}, s32[2,8,2048]{2,1,0:T(8,128)S(1)}, u32[]{:S(2)}, u32[]{:S(2)}) collective-permute-start(s32[2,8,2048]{2,1,0:T(8,128)S(1)} %get-tuple-element.55), channel_id=1, source_target_pairs={{0,3},{1,2},{2,1},{3,0},{4,7},{5,6},{6,5},{7,4},{8,11},{9,10},{10,... | collective-permute-start | bytes 393224 | tf_op jit(solution)/shard_map/ppermute | solution.py:28
  41.2 11.2 %collective-permute-start.10 = (s32[2,8,2048]{2,1,0:T(8,128)S(1)}, s32[2,8,2048]{2,1,0:T(8,128)S(1)}, u32[]{:S(2)}, u32[]{:S(2)}) collective-permute-start(s32[2,8,2048]{2,1,0:T(8,128)S(1)} %get-tuple-element.57), channel_id=1, source_target_pairs={{0,1},{1,0},{2,3},{3,2},{4,5},{5,4},{6,7},{7,6},{8,9},{9,8},{10,11... | collective-permute-start | bytes 393224 | tf_op jit(solution)/shard_map/ppermute | solution.py:28
  41.7 10.7 %collective-permute-start.11 = (s32[2,8,2048]{2,1,0:T(8,128)S(1)}, s32[2,8,2048]{2,1,0:T(8,128)S(1)}, u32[]{:S(2)}, u32[]{:S(2)}) collective-permute-start(s32[2,8,2048]{2,1,0:T(8,128)S(1)} %get-tuple-element.59), channel_id=1, source_target_pairs={{0,2},{1,3},{2,0},{3,1},{4,6},{5,7},{6,4},{7,5},{8,10},{9,11},{10,... | collective-permute-start | bytes 393224 | tf_op jit(solution)/shard_map/ppermute | solution.py:28

commit v6 on v4

--- a/solution.py
+++ b/solution.py
@@ -97,7 +97,7 @@
         start = pl.multiple_of((rank ^ slot) * rows + top, ROWS)
         cuts.append(pltpu.make_async_copy(bins.at[:, pl.ds(start, size)], pieces[index], cut_sems.at[index]))
         cuts[-1].start()
-    pair = pack_entries(table[...].astype(jnp.float32))
+    pair = pack_entries(table)
     for word in range(2):
         entries[word] = pair[word]
     for row in range(rows):
@@ -510,7 +510,7 @@
         compiler_params=params,
         cost_estimate=cost(depth * height * width),
         name="pack",
-    )(above, below, table, march_order, in_hbm(field), in_hbm(bins))
+    )(above, below, table.astype(jnp.float32), march_order, in_hbm(field), in_hbm(bins))
     messages = {}
     for slot in partners:
         messages[slot] = send("message", packed[slot - 1], slot)

time: 54 us -> 54 us (level)
  no operation moved by 1% of the time
where the time goes in v6:
time: 54 us; the launch traced here: 53.7 us
  starting transfers between devices  20 us (37%)
  waiting for transfers between devices  18.2 us (34%)
  Pallas kernels  15.3 us (28%)
    ppermute x12, starting transfers between devices, partner(): lax.ppermute(x, axis, [(i, i ^ distance) for i in range(lax.axis_size(axi...  14.8 us
    ppermute x12, waiting for transfers between devices, partner(): lax.ppermute(x, axis, [(i, i ^ distance) for i in range(lax.axis_size(axi...  13.9 us
    ppermute x1, waiting for transfers between devices, shards(): below = lax.ppermute(first, 'sy', backward)  4.21 us
    pallas_call x1, Pallas kernels, shards(): pl.pallas_call(functools.partial(inner_kernel, count, depth), out_shape=(...  4.12 us
    ppermute x1, starting transfers between devices, shards(): above = lax.ppermute(last, 'sy', forward)  3.93 us
    pallas_call x1, Pallas kernels, shards(): pl.pallas_call(functools.partial(pack_kernel, count, depth, early, later)...  2.63 us
    pallas_call x1, Pallas kernels, shards(): pl.pallas_call(functools.partial(outer_kernel, count, depth), out_shape=(...  2.5 us
    pallas_call x2, Pallas kernels, shards(): pl.pallas_call(functools.partial(blend_kernel, count, depth, top, early,...  2.46 us
  transfers between devices with their start and end apart: 14, of which 8 were waited for; matrix products, arithmetic and copies ran while one was open for 0% of the time, Pallas kernels for 24%

profile of v6, /device:TPU:0, one launch (start us, length us, event | category | flops | bytes accessed | tf_op | source)
XLA Modules:
  0.0 53.7 jit_solution(12887307630225294783)
XLA Ops:
  0.0 1.1 %lead.1 = f32[2,32,2048]{2,1,0:T(8,128)S(1)} custom-call(f32[2,128,2048]{2,1,0:T(8,128)} %field.8), custom_call_target="tpu_custom_call" | custom-call | flops 2621440 | bytes 1048576 | tf_op jit(solution)/shard_map/lead/pallas_call | solution.py:450
  1.1 4.0 %collective-permute-start.4 = (f32[2,32,2048]{2,1,0:T(8,128)S(1)}, f32[2,32,2048]{2,1,0:T(8,128)S(1)}, u32[]{:S(2)}, u32[]{:S(2)}) collective-permute-start(f32[2,32,2048]{2,1,0:T(8,128)S(1)} %lead.1), channel_id=1, source_target_pairs={{0,3},{1,2},{2,1},{3,0},{4,7},{5,6},{6,5},{7,4},{8,11},{9,10},{10,... | collective-permute-start | bytes 1572872 | tf_op jit(solution)/shard_map/ppermute | solution.py:28
  5.0 1.4 %split.1 = (f32[2,32,2048]{2,1,0:T(8,128)S(1)}, f32[2,32,2048]{2,1,0:T(8,128)S(1)}, f32[2,2048]{1,0:T(2,128)S(1)}, f32[2,2048]{1,0:T(2,128)S(1)}) custom-call(f32[2,128,2048]{2,1,0:T(8,128)} %field.8), custom_call_target="tpu_custom_call" | custom-call | flops 10485760 | bytes 4194304 | tf_op jit(solution)/shard_map/split/pallas_call | solution.py:462
  6.4 0.6 %collective-permute-start.2 = (f32[2,32,2048]{2,1,0:T(8,128)S(1)}, f32[2,32,2048]{2,1,0:T(8,128)S(1)}, u32[]{:S(2)}, u32[]{:S(2)}) collective-permute-start(f32[2,32,2048]{2,1,0:T(8,128)S(1)} %get-tuple-element.43), channel_id=1, source_target_pairs={{0,1},{1,0},{2,3},{3,2},{4,5},{5,4},{6,7},{7,6},{8,9},{9,8},{10,11... | collective-permute-start | bytes 1572872 | tf_op jit(solution)/shard_map/ppermute | solution.py:28
  7.1 3.9 %collective-permute-start = (f32[2,2048]{1,0:T(2,128)S(1)}, f32[2,2048]{1,0:T(2,128)S(1)}, u32[]{:S(2)}, u32[]{:S(2)}) collective-permute-start(f32[2,2048]{1,0:T(2,128)S(1)} %get-tuple-element.38), channel_id=1, source_target_pairs={{0,4},{4,8},{8,12},{1,5},{5,9},{9,13},{2,6},{6,10},{10,14},{3,7},{... | collective-permute-start | bytes 49160 | tf_op jit(solution)/shard_map/ppermute | solution.py:478
  11.0 1.3 %collective-permute-start.1 = (f32[2,2048]{1,0:T(2,128)S(1)}, f32[2,2048]{1,0:T(2,128)S(1)}, u32[]{:S(2)}, u32[]{:S(2)}) collective-permute-start(f32[2,2048]{1,0:T(2,128)S(1)} %get-tuple-element.39), channel_id=1, source_target_pairs={{4,0},{8,4},{12,8},{5,1},{9,5},{13,9},{6,2},{10,6},{14,10},{7,3},{... | collective-permute-start | bytes 49160 | tf_op jit(solution)/shard_map/ppermute | solution.py:479
  12.4 4.2 %collective-permute-done.1.below = f32[2,2048]{1,0:T(2,128)S(1)} collective-permute-done((f32[2,2048]{1,0:T(2,128)S(1)}, f32[2,2048]{1,0:T(2,128)S(1)}, u32[]{:S(2)}, u32[]{:S(2)}) %collective-permute-start.1) | collective-permute-done | bytes 16416 | tf_op jit(solution)/shard_map/ppermute | solution.py:479
  16.7 2.6 %pack.1 = (f32[72,1024]{1,0:T(8,128)S(1)}, f32[72,1024]{1,0:T(8,128)S(1)}, f32[72,1024]{1,0:T(8,128)S(1)}, f32[8,1024]{1,0:T(8,128)S(1)}, s32[2,8,128]{2,1,0:T(8...) custom-call(f32[2,2048]{1,0:T(2,128)S(1)} %collective-permute-done.a, ...), custom_call_target="tpu_custom_call" | custom-call | flops 10485760 | bytes 4194304 | tf_op jit(solution)/shard_map/pack/pallas_call | solution.py:492
  19.3 2.5 %collective-permute-start.8 = (f32[72,1024]{1,0:T(8,128)S(1)}, f32[72,1024]{1,0:T(8,128)S(1)}, u32[]{:S(2)}, u32[]{:S(2)}) collective-permute-start(f32[72,1024]{1,0:T(8,128)S(1)} %get-tuple-element.55), channel_id=1, source_target_pairs={{0,3},{1,2},{2,1},{3,0},{4,7},{5,6},{6,5},{7,4},{8,11},{9,10},{10,... | collective-permute-start | bytes 884744 | tf_op jit(solution)/shard_map/ppermute | solution.py:28
  22.3 0.5 collective-permute-start.6
  22.9 6.8 %collective-permute-done.2.refs_0_ = f32[2,32,2048]{2,1,0:T(8,128)S(1)} collective-permute-done((f32[2,32,2048]{2,1,0:T(8,128)S(1)}, f32[2,32,2048]{2,1,0:T(8,128)S(1)}, u32[]{:S(2)}, u32[]{:S(2)}) %collective-permute-start.2) | collective-permute-done | bytes 524320 | tf_op jit(solution)/shard_map/ppermute | solution.py:28
  29.7 0.8 %side.1 = f32[8,32,128]{2,1,0:T(8,128)S(1)} custom-call(f32[2,128,2048]{2,1,0:T(8,128)} %field.8, f32[2,32,2048]{2,1,0:T(8,128)S(1)} %collective-permute-done.2.refs_0_, f32[2,32,2048]{2,1,0:T(8,128)S(1)} %collective-permute-done.3.refs_1_, f32[2,32,2048]{2,1,0:T(8,128)S(1)} %collective-permute-done.4.refs_2_), custom_call_target="tpu_custom_call" | custom-call | flops 655360 | bytes 262144 | tf_op jit(solution)/shard_map/side/pallas_call | solution.py:520
  30.5 1.3 %collective-permute-done.5.beside = f32[8,32,128]{2,1,0:T(8,128)S(1)} collective-permute-done((f32[8,32,128]{2,1,0:T(8,128)S(1)}, f32[8,32,128]{2,1,0:T(8,128)S(1)}, u32[]{:S(2)}, u32[]{:S(2)}) %collective-permute-start.5) | collective-permute-done | bytes 131104 | tf_op jit(solution)/shard_map/ppermute | solution.py:28
  31.8 4.1 %inner.1 = (f32[10,48,2304]{2,1,0:T(8,128)S(1)}, f32[8,32,2048]{2,1,0:T(8,128)S(1)}, f32[8,16,2048]{2,1,0:T(8,128)S(1)}, s32[2,2,32,2048]{3,2,1,0:T(8,128)S(1)}, f32[8,128]{1,0:T(8,128)}) custom-call(f32[2,128,2048]{2,1,0:T(8,128)} %field.8, f32[8,1024]{1,0:T(8,128)S(1)} %get-tuple-element.42.edges, f32[8,32,128]{2,1,0:T(8,128)S(1)} %collective-permute-done.5.beside, ...), custom_call_target="tpu_custom_call" | custom-call | flops 10485760 | bytes 4194304 | tf_op jit(solution)/shard_map/inner/pallas_call | solution.py:532
  36.0 2.5 %collective-permute-start.9 = (s32[2,16,2048]{2,1,0:T(8,128)S(1)}, s32[2,16,2048]{2,1,0:T(8,128)S(1)}, u32[]{:S(2)}, u32[]{:S(2)}) collective-permute-start(s32[2,16,2048]{2,1,0:T(8,128)S(1)} %get-tuple-element.59), channel_id=1, source_target_pairs={{0,3},{1,2},{2,1},{3,0},{4,7},{5,6},{6,5},{7,4},{8,11},{9,10},{10,... | collective-permute-start | bytes 786440 | tf_op jit(solution)/shard_map/ppermute | solution.py:28
  38.5 3.1 %collective-permute-done.7.refs_1_ = f32[72,1024]{1,0:T(8,128)S(1)} collective-permute-done((f32[72,1024]{1,0:T(8,128)S(1)}, f32[72,1024]{1,0:T(8,128)S(1)}, u32[]{:S(2)}, u32[]{:S(2)}) %collective-permute-start.7) | collective-permute-done | bytes 294944 | tf_op jit(solution)/shard_map/ppermute | solution.py:28
  41.6 0.7 %collective-permute-done.6.refs_0_ = f32[72,1024]{1,0:T(8,128)S(1)} collective-permute-done((f32[72,1024]{1,0:T(8,128)S(1)}, f32[72,1024]{1,0:T(8,128)S(1)}, u32[]{:S(2)}, u32[]{:S(2)}) %collective-permute-start.6) | collective-permute-done | bytes 294944 | tf_op jit(solution)/shard_map/ppermute | solution.py:28
  42.3 1.5 %collective-permute-start.12 = (s32[2,8,2048]{2,1,0:T(8,128)S(1)}, s32[2,8,2048]{2,1,0:T(8,128)S(1)}, u32[]{:S(2)}, u32[]{:S(2)}) collective-permute-start(s32[2,8,2048]{2,1,0:T(8,128)S(1)} %get-tuple-element.65), channel_id=1, source_target_pairs={{0,1},{1,0},{2,3},{3,2},{4,5},{5,4},{6,7},{7,6},{8,9},{9,8},{10,11... | collective-permute-start | bytes 393224 | tf_op jit(solution)/shard_map/ppermute | solution.py:28
  43.8 1.3 %collective-permute-start.13 = (s32[2,8,2048]{2,1,0:T(8,128)S(1)}, s32[2,8,2048]{2,1,0:T(8,128)S(1)}, u32[]{:S(2)}, u32[]{:S(2)}) collective-permute-start(s32[2,8,2048]{2,1,0:T(8,128)S(1)} %get-tuple-element.67), channel_id=1, source_target_pairs={{0,2},{1,3},{2,0},{3,1},{4,6},{5,7},{6,4},{7,5},{8,10},{9,11},{10,... | collective-permute-start | bytes 393224 | tf_op jit(solution)/shard_map/ppermute | solution.py:28
  45.6 0.7 %collective-permute-start.11 = (s32[2,8,2048]{2,1,0:T(8,128)S(1)}, s32[2,8,2048]{2,1,0:T(8,128)S(1)}, u32[]{:S(2)}, u32[]{:S(2)}) collective-permute-start(s32[2,8,2048]{2,1,0:T(8,128)S(1)} %get-tuple-element.63), channel_id=1, source_target_pairs={{0,2},{1,3},{2,0},{3,1},{4,6},{5,7},{6,4},{7,5},{8,10},{9,11},{10,... | collective-permute-start | bytes 393224 | tf_op jit(solution)/shard_map/ppermute | solution.py:28
  46.4 2.5 %outer.1 = (f32[8,16,2048]{2,1,0:T(8,128)S(1)}, f32[4,32,2048]{2,1,0:T(8,128)}) custom-call(s32[2,8,128]{2,1,0:T(8,128)S(1)} %get-tuple-element.40.entries, s32[32,128]{1,0:T(8,128)S(1)} %get-tuple-element.41.flips, f32[10,48,2304]{2,1,0:T(8,128)S(1)} %get-tuple-element.47.ext, f32[8,32,2048]{2,1,0:T(8,128)S(1)} %get-tuple-element.46.scaled, ...), custom_call_target="tpu_custom_call" | custom-call | flops 10485760 | bytes 4194304 | tf_op jit(solution)/shard_map/outer/pallas_call | solution.py:551
  49.3 1.5 %collective-permute-done.12.refs_0_ = s32[2,8,2048]{2,1,0:T(8,128)S(1)} collective-permute-done((s32[2,8,2048]{2,1,0:T(8,128)S(1)}, s32[2,8,2048]{2,1,0:T(8,128)S(1)}, u32[]{:S(2)}, u32[]{:S(2)}) %collective-permute-start.12) | collective-permute-done | bytes 131104 | tf_op jit(solution)/shard_map/ppermute | solution.py:28
  50.8 1.2 %blend.2.refs_2_ = f32[4,32,2048]{2,1,0:T(8,128)} custom-call(s32[2,8,128]{2,1,0:T(8,128)S(1)} %get-tuple-element.40.entries, s32[32,128]{1,0:T(8,128)S(1)} %get-tuple-element.41.flips, f32[8,32,2048]{2,1,0:T(8,128)S(1)} %get-tuple-element.46.scaled, f32[8,16,2048]{2,1,0:T(8,128)S(1)} %get-tuple-element.48.inner.shading, ...), custom_call_target="tpu_custom_call", output_to_operand_aliasing={{}: (8, {})} | custom-call | flops 2621440 | bytes 1048576 | tf_op jit(solution)/shard_map/blend/pallas_call | solution.py:582
  52.4 1.2 %blend.3 = f32[4,32,2048]{2,1,0:T(8,128)} custom-call(s32[2,8,128]{2,1,0:T(8,128)S(1)} %get-tuple-element.40.entries, s32[32,128]{1,0:T(8,128)S(1)} %get-tuple-element.41.flips, f32[8,32,2048]{2,1,0:T(8,128)S(1)} %get-tuple-element.46.scaled, f32[8,16,2048]{2,1,0:T(8,128)S(1)} %get-tuple-element.56.shading, ...), custom_call_target="tpu_custom_call", output_to_operand_aliasing={{}: (8, {})} | custom-call | flops 2621440 | bytes 1048576 | tf_op jit(solution)/shard_map/blend/pallas_call | solution.py:582
  (18 shorter events, 2.1 us)
Async XLA Ops:
  0.0 12.3 %copy-start.1 = (bf16[4,128]{1,0:T(4,128)(2,1)S(1)}, bf16[4,128]{1,0:T(4,128)(2,1)}, u32[]{:S(2)}) copy-start(bf16[4,128]{1,0:T(4,128)(2,1)} %param.6) | copy-start | bytes 3076
  0.0 16.7 %copy-start = (s32[128]{0:T(128)S(1)}, s32[128]{0:T(128)}, u32[]{:S(2)}) copy-start(s32[128]{0:T(128)} %march.1) | copy-start | bytes 1540
  1.1 18.2 %collective-permute-start.4 = (f32[2,32,2048]{2,1,0:T(8,128)S(1)}, f32[2,32,2048]{2,1,0:T(8,128)S(1)}, u32[]{:S(2)}, u32[]{:S(2)}) collective-permute-start(f32[2,32,2048]{2,1,0:T(8,128)S(1)} %lead.1), channel_id=1, source_target_pairs={{0,3},{1,2},{2,1},{3,0},{4,7},{5,6},{6,5},{7,4},{8,11},{9,10},{10,... | collective-permute-start | bytes 1572872 | tf_op jit(solution)/shard_map/ppermute | solution.py:28
  6.4 23.2 %collective-permute-start.2 = (f32[2,32,2048]{2,1,0:T(8,128)S(1)}, f32[2,32,2048]{2,1,0:T(8,128)S(1)}, u32[]{:S(2)}, u32[]{:S(2)}) collective-permute-start(f32[2,32,2048]{2,1,0:T(8,128)S(1)} %get-tuple-element.43), channel_id=1, source_target_pairs={{0,1},{1,0},{2,3},{3,2},{4,5},{5,4},{6,7},{7,6},{8,9},{9,8},{10,11... | collective-permute-start | bytes 1572872 | tf_op jit(solution)/shard_map/ppermute | solution.py:28
  7.0 22.6 %collective-permute-start.3 = (f32[2,32,2048]{2,1,0:T(8,128)S(1)}, f32[2,32,2048]{2,1,0:T(8,128)S(1)}, u32[]{:S(2)}, u32[]{:S(2)}) collective-permute-start(f32[2,32,2048]{2,1,0:T(8,128)S(1)} %get-tuple-element.44), channel_id=1, source_target_pairs={{0,2},{1,3},{2,0},{3,1},{4,6},{5,7},{6,4},{7,5},{8,10},{9,11},{10,... | collective-permute-start | bytes 1572872 | tf_op jit(solution)/shard_map/ppermute | solution.py:28
  7.1 5.4 %collective-permute-start = (f32[2,2048]{1,0:T(2,128)S(1)}, f32[2,2048]{1,0:T(2,128)S(1)}, u32[]{:S(2)}, u32[]{:S(2)}) collective-permute-start(f32[2,2048]{1,0:T(2,128)S(1)} %get-tuple-element.38), channel_id=1, source_target_pairs={{0,4},{4,8},{8,12},{1,5},{5,9},{9,13},{2,6},{6,10},{10,14},{3,7},{... | collective-permute-start | bytes 49160 | tf_op jit(solution)/shard_map/ppermute | solution.py:478
  11.0 5.6 %collective-permute-start.1 = (f32[2,2048]{1,0:T(2,128)S(1)}, f32[2,2048]{1,0:T(2,128)S(1)}, u32[]{:S(2)}, u32[]{:S(2)}) collective-permute-start(f32[2,2048]{1,0:T(2,128)S(1)} %get-tuple-element.39), channel_id=1, source_target_pairs={{4,0},{8,4},{12,8},{5,1},{9,5},{13,9},{6,2},{10,6},{14,10},{7,3},{... | collective-permute-start | bytes 49160 | tf_op jit(solution)/shard_map/ppermute | solution.py:479
  19.3 16.7 %collective-permute-start.8 = (f32[72,1024]{1,0:T(8,128)S(1)}, f32[72,1024]{1,0:T(8,128)S(1)}, u32[]{:S(2)}, u32[]{:S(2)}) collective-permute-start(f32[72,1024]{1,0:T(8,128)S(1)} %get-tuple-element.55), channel_id=1, source_target_pairs={{0,3},{1,2},{2,1},{3,0},{4,7},{5,6},{6,5},{7,4},{8,11},{9,10},{10,... | collective-permute-start | bytes 884744 | tf_op jit(solution)/shard_map/ppermute | solution.py:28
  21.8 19.8 %collective-permute-start.7 = (f32[72,1024]{1,0:T(8,128)S(1)}, f32[72,1024]{1,0:T(8,128)S(1)}, u32[]{:S(2)}, u32[]{:S(2)}) collective-permute-start(f32[72,1024]{1,0:T(8,128)S(1)} %get-tuple-element.53), channel_id=1, source_target_pairs={{0,2},{1,3},{2,0},{3,1},{4,6},{5,7},{6,4},{7,5},{8,10},{9,11},{10,... | collective-permute-start | bytes 884744 | tf_op jit(solution)/shard_map/ppermute | solution.py:28
  22.3 20.0 %collective-permute-start.6 = (f32[72,1024]{1,0:T(8,128)S(1)}, f32[72,1024]{1,0:T(8,128)S(1)}, u32[]{:S(2)}, u32[]{:S(2)}) collective-permute-start(f32[72,1024]{1,0:T(8,128)S(1)} %get-tuple-element.51), channel_id=1, source_target_pairs={{0,1},{1,0},{2,3},{3,2},{4,5},{5,4},{6,7},{7,6},{8,9},{9,8},{10,11... | collective-permute-start | bytes 884744 | tf_op jit(solution)/shard_map/ppermute | solution.py:28
  30.4 1.4 %collective-permute-start.5 = (f32[8,32,128]{2,1,0:T(8,128)S(1)}, f32[8,32,128]{2,1,0:T(8,128)S(1)}, u32[]{:S(2)}, u32[]{:S(2)}) collective-permute-start(f32[8,32,128]{2,1,0:T(8,128)S(1)} %side.1), channel_id=1, source_target_pairs={{0,16},{16,0},{1,17},{17,1},{2,18},{18,2},{3,19},{19,3},{4,20},{20... | collective-permute-start | bytes 393224 | tf_op jit(solution)/shard_map/ppermute | solution.py:28
  36.0 12.9 %collective-permute-start.9 = (s32[2,16,2048]{2,1,0:T(8,128)S(1)}, s32[2,16,2048]{2,1,0:T(8,128)S(1)}, u32[]{:S(2)}, u32[]{:S(2)}) collective-permute-start(s32[2,16,2048]{2,1,0:T(8,128)S(1)} %get-tuple-element.59), channel_id=1, source_target_pairs={{0,3},{1,2},{2,1},{3,0},{4,7},{5,6},{6,5},{7,4},{8,11},{9,10},{10,... | collective-permute-start | bytes 786440 | tf_op jit(solution)/shard_map/ppermute | solution.py:28
  42.3 8.4 %collective-permute-start.12 = (s32[2,8,2048]{2,1,0:T(8,128)S(1)}, s32[2,8,2048]{2,1,0:T(8,128)S(1)}, u32[]{:S(2)}, u32[]{:S(2)}) collective-permute-start(s32[2,8,2048]{2,1,0:T(8,128)S(1)} %get-tuple-element.65), channel_id=1, source_target_pairs={{0,1},{1,0},{2,3},{3,2},{4,5},{5,4},{6,7},{7,6},{8,9},{9,8},{10,11... | collective-permute-start | bytes 393224 | tf_op jit(solution)/shard_map/ppermute | solution.py:28
  43.8 6.9 %collective-permute-start.13 = (s32[2,8,2048]{2,1,0:T(8,128)S(1)}, s32[2,8,2048]{2,1,0:T(8,128)S(1)}, u32[]{:S(2)}, u32[]{:S(2)}) collective-permute-start(s32[2,8,2048]{2,1,0:T(8,128)S(1)} %get-tuple-element.67), channel_id=1, source_target_pairs={{0,2},{1,3},{2,0},{3,1},{4,6},{5,7},{6,4},{7,5},{8,10},{9,11},{10,... | collective-permute-start | bytes 393224 | tf_op jit(solution)/shard_map/ppermute | solution.py:28
  45.1 7.3 %collective-permute-start.10 = (s32[2,8,2048]{2,1,0:T(8,128)S(1)}, s32[2,8,2048]{2,1,0:T(8,128)S(1)}, u32[]{:S(2)}, u32[]{:S(2)}) collective-permute-start(s32[2,8,2048]{2,1,0:T(8,128)S(1)} %get-tuple-element.61), channel_id=1, source_target_pairs={{0,1},{1,0},{2,3},{3,2},{4,5},{5,4},{6,7},{7,6},{8,9},{9,8},{10,11... | collective-permute-start | bytes 393224 | tf_op jit(solution)/shard_map/ppermute | solution.py:28
  45.6 6.8 %collective-permute-start.11 = (s32[2,8,2048]{2,1,0:T(8,128)S(1)}, s32[2,8,2048]{2,1,0:T(8,128)S(1)}, u32[]{:S(2)}, u32[]{:S(2)}) collective-permute-start(s32[2,8,2048]{2,1,0:T(8,128)S(1)} %get-tuple-element.63), channel_id=1, source_target_pairs={{0,2},{1,3},{2,0},{3,1},{4,6},{5,7},{6,4},{7,5},{8,10},{9,11},{10,... | collective-permute-start | bytes 393224 | tf_op jit(solution)/shard_map/ppermute | solution.py:28

commit v7 on v6

--- a/solution.py
+++ b/solution.py
@@ -162,40 +162,51 @@
     return (words >> HALF_WORD).astype(jnp.float32)
 
 
-def blend_rows(count, depth, words, back, scaled, span, shading, shaded, result, here, finish):
-    rank = lax.axis_index("gz")
+def in_front(sums, bit):
+    if len(sums) == 1:
+        return [None], sums[0]
+    middle = len(sums) // 2
+    low, low_sum = in_front(sums[:middle], bit - 1)
+    high, high_sum = in_front(sums[middle:], bit - 1)
+    swapped = jnp.where(lax.axis_index("gz") >> bit & 1 == 1, 1.0, 0.0)
+    low_adds = high_sum * swapped
+    high_adds = low_sum * (1.0 - swapped)
+    fronts = [low_adds if front is None else front + low_adds for front in low]
+    fronts += [high_adds if front is None else front + high_adds for front in high]
+    return fronts, low_sum + high_sum
+
+
+def cell_values(words, scaled, shade):
+    return high_part(words[1]) * scaled, shade, (low_part(words[0]), high_part(words[0]), low_part(words[1]))
+
+
+def blend_rows(count, depth, values, back, result, here, finish):
     tiles = result.shape[2] // LANES
     unroll = max(min(tiles // COPIES, UNROLLED // (count * depth)), 1)
-    ahead = [
-        [jnp.where((rank ^ other) < (rank ^ slot), 1.0, 0.0) for other in range(count)] for slot in range(count)
-    ]
 
     def blend_tile(cols, h):
-        found = [words(cell, cols, h) for cell in range(count * depth)]
-        taus = [high_part(found[cell][1]) * scaled[cell, span, cols] for cell in range(count * depth)]
+        cells = [values(cell, cols, h) for cell in range(count * depth)]
         inner = []
         for slot in range(count):
-            sums = [taus[slot * depth]]
+            sums = [cells[slot * depth][0]]
             for j in range(1, depth):
-                sums.append(sums[-1] + taus[slot * depth + j])
+                sums.append(sums[-1] + cells[slot * depth + j][0])
             inner.append(sums)
-        whole = sum(sums[-1] for sums in inner)
-        sign = jnp.where(back, 1.0, -1.0)
+        fronts, whole = in_front([sums[-1] for sums in inner], count.bit_length() - 2)
         shift = jnp.where(back, -whole, 0.0)
         colour = [jnp.zeros((ROWS, LANES), jnp.float32) for _ in range(3)]
         for slot in range(count):
-            front = sum(inner[other][-1] * ahead[slot][other] for other in range(count) if other != slot)
-            reached = [front] + [front + part for part in inner[slot]]
-            through = [jnp.exp2(sign * part + shift) for part in reached]
+            base = fronts[slot] + shift
+            through = [jnp.exp2(base)] + [jnp.exp2(base + part) for part in inner[slot]]
             for j in range(depth):
-                cell = slot * depth + j
-                weight = jnp.abs(through[j] - through[j + 1]) * shading[cell, shaded, cols]
-                colour[0] = colour[0] + weight * low_part(found[cell][0])
-                colour[1] = colour[1] + weight * high_part(found[cell][0])
-                colour[2] = colour[2] + weight * low_part(found[cell][1])
+                _, shade, colours = cells[slot * depth + j]
+                weight = jnp.abs(through[j] - through[j + 1])
+                if shade is not None:
+                    weight = weight * shade
+                colour = [total + weight * part for total, part in zip(colour, colours)]
         for c in range(3):
             result[c, here, cols] = colour[c]
-        result[3, here, cols] = 1.0 - jnp.exp2(-whole)
+        result[3, here, cols] = 1.0 - jnp.exp2(-jnp.abs(whole))
 
     quarter = tiles // COPIES
     for part in range(COPIES):
@@ -249,7 +260,7 @@
         store(c - 1, 0.3 * COLOUR_UNIT + (0.7 * COLOUR_UNIT) * facing * lax.rsqrt(square))
 
 
-def inner_kernel(count, depth, field, edges, beside, entries, *refs):
+def inner_kernel(count, depth, field, edges, beside, entries, flips, *refs):
     parts = len(refs) - (count - 1) - 7
     bricks = refs[: count - 1]
     own_bins = refs[count - 1 : count - 1 + parts]
@@ -263,6 +274,7 @@
     move = pltpu.make_async_copy(field.at[:, pl.ds(pl.multiple_of(rank * rows, ROWS), rows)], own_brick, sem)
     move.start()
     bricks = (own_brick, *bricks)
+    unit = jnp.where(flips[...] == 1, OPACITY_UNIT * LOG2_E, -OPACITY_UNIT * LOG2_E)
     zero_plane = jnp.zeros((rows, width), jnp.float32)
     zero_row = jnp.zeros((ROWS, width), jnp.float32)
     ext[0, inside, LANES : LANES + width] = zero_plane
@@ -273,7 +285,9 @@
         for j in range(depth):
             at = (rank ^ slot) * depth + j
             plane = bricks[slot][j]
-            scaled[slot * depth + j] = plane * (OPACITY_UNIT * LOG2_E)
+            for left in range(0, width, LANES):
+                cols = slice(left, left + LANES)
+                scaled[slot * depth + j, :, cols] = bricks[slot][j, :, cols] * unit
             ext[at + 1, inside, LANES : LANES + width] = plane
             ext[at + 1, :ROWS, LANES : LANES + width] = zero_row
             ext[at + 1, ROWS + rows :, LANES : LANES + width] = zero_row
@@ -355,21 +369,23 @@
     for top in range(0, early, ROWS):
         here = slice(top, top + ROWS)
 
-        def words(cell, cols, h, top=top):
+        shading, shaded = (outer, slice(0, ROWS)) if top == 0 else (inner, slice(top - ROWS, top))
+
+        def values(cell, cols, h, top=top, shading=shading, shaded=shaded):
             slot, j = divmod(cell, depth)
             if slot == 0:
-                return tuple(known[word, j, top : top + ROWS, cols] for word in range(2))
-            left = cols.start - h * half
-            left = pl.ds(left if isinstance(left, int) else pl.multiple_of(left, LANES), LANES)
-            row = 4 * depth + (2 * j + h) * early + top
-            labels = messages[slot - 1][row : row + ROWS, left].astype(jnp.int32)
-            return look(pair[0], labels), look(pair[1], labels)
+                words = tuple(known[word, j, top : top + ROWS, cols] for word in range(2))
+            else:
+                left = cols.start - h * half
+                left = pl.ds(left if isinstance(left, int) else pl.multiple_of(left, LANES), LANES)
+                row = 4 * depth + (2 * j + h) * early + top
+                labels = messages[slot - 1][row : row + ROWS, left].astype(jnp.int32)
+                words = look(pair[0], labels), look(pair[1], labels)
+            return cell_values(words, scaled[cell, top : top + ROWS, cols], shading[cell, shaded, cols])
 
         parts = copy_out(result, image, sems, top, 0)
-        shading, shaded = (outer, slice(0, ROWS)) if top == 0 else (inner, slice(top - ROWS, top))
         blend_rows(
-            count, depth, words, flips[here, :] == 1, scaled, here, shading, shaded, result, here,
-            lambda part, parts=parts: parts[part].start(),
+            count, depth, values, flips[here, :] == 1, result, here, lambda part, parts=parts: parts[part].start()
         )
         copies += parts
     if rows > ROWS:
@@ -378,18 +394,31 @@
         move.wait()
 
 
-def look_kernel(depth, entries, brick, found):
+def look_kernel(depth, late, lead, entries, scaled, inner, outer, known, brick, found):
     rows, width = found.shape[2:]
-    for j in range(depth):
+    pair = (entries[0], entries[1])
+    for index in range(2 * depth):
+        j = index % depth
+        cell = j if index < depth else lead * depth + j
         for top in range(0, rows, ROWS):
+            here = slice(top, top + ROWS)
+            span = slice(late + top, late + top + ROWS)
+            last = top + ROWS == rows
             for left in range(0, width, LANES):
-                at = (slice(top, top + ROWS), slice(left, left + LANES))
-                labels = brick[(j, *at)]
-                for word in range(2):
-                    found[(word, j, *at)] = look(entries[word], labels)
-
-
-def blend_kernel(count, depth, start, late, lead, entries, flips, scaled, shading, known, found, *refs):
+                cols = slice(left, left + LANES)
+                if index < depth:
+                    words = known[0, j, span, cols], known[1, j, span, cols]
+                else:
+                    labels = brick[j, here, cols]
+                    words = look(pair[0], labels), look(pair[1], labels)
+                shade = outer[cell, ROWS:, cols] if last else inner[cell, late + top - ROWS : late + top, cols]
+                tau, shade, colours = cell_values(words, scaled[cell, span, cols], shade)
+                found[0, index, here, cols] = tau
+                for c in range(3):
+                    found[1 + c, index, here, cols] = shade * colours[c]
+
+
+def blend_kernel(count, depth, start, late, lead, entries, flips, scaled, shading, found, *refs):
     bricks = refs[: count - 2]
     image, result, sems = refs[-3:]
     rows = result.shape[1]
@@ -399,23 +428,23 @@
     for top in range(0, rows, ROWS):
         here = slice(top, top + ROWS)
         span = slice(start + top, start + top + ROWS)
+        begin = start + top - late
         inner = start + top + ROWS < scaled.shape[1]
         shaded = slice(start + top - ROWS, start + top) if inner else slice(ROWS, 2 * ROWS)
 
-        def words(cell, cols, h, here=here, span=span, top=top):
+        def values(cell, cols, h, here=here, span=span, begin=begin, shaded=shaded):
             slot, j = divmod(cell, depth)
-            if slot == 0:
-                return tuple(known[word, j, span, cols] for word in range(2))
-            if slot == lead:
-                begin = start + top - late
-                return tuple(found[word, j, begin : begin + ROWS, cols] for word in range(2))
+            if slot in (0, lead):
+                index = j if slot == 0 else depth + j
+                ready = [found[part, index, begin : begin + ROWS, cols] for part in range(4)]
+                return ready[0], None, ready[1:]
             labels = bricks[unknown.index(slot)][j, here, cols]
-            return look(pair[0], labels), look(pair[1], labels)
+            words = look(pair[0], labels), look(pair[1], labels)
+            return cell_values(words, scaled[cell, span, cols], shading[cell, shaded, cols])
 
         parts = copy_out(result, image, sems, top, start)
         blend_rows(
-            count, depth, words, flips[span, :] == 1, scaled, span, shading, shaded, result, here,
-            lambda part, parts=parts: parts[part].start(),
+            count, depth, values, flips[span, :] == 1, result, here, lambda part, parts=parts: parts[part].start()
         )
         copies += parts
     for move in copies:
@@ -538,13 +567,13 @@
             pltpu.VMEM((2, depth, rows, width), jnp.int32),
             jax.ShapeDtypeStruct((ROWS, LANES), jnp.float32),
         ),
-        in_specs=[hbm] + [vmem] * (count + 3),
+        in_specs=[hbm] + [vmem] * (count + 4),
         out_specs=[vmem] * 5,
         scratch_shapes=[pltpu.VMEM((depth, rows, width), jnp.float32), pltpu.SemaphoreType.DMA],
         compiler_params=params,
         cost_estimate=cost(total * rows * width),
         name="inner",
-    )(in_hbm(field), edges, beside, entries, *[bricks[slot] for slot in slots[1:]], cuts[0])
+    )(in_hbm(field), edges, beside, entries, flips, *[bricks[slot] for slot in slots[1:]], cuts[0])
     done["inner"] = token
 
     image_shape = jax.ShapeDtypeStruct((4, rows, width), jnp.float32)
@@ -566,19 +595,19 @@
 
     arrived = [send("bins", cut, slot) for (slot, _, _), cut in zip(later[1:], cuts[1:])]
     found = pl.pallas_call(
-        functools.partial(look_kernel, depth),
-        out_shape=pltpu.VMEM((2, depth, late, width), jnp.int32),
-        in_specs=[vmem] * 2,
+        functools.partial(look_kernel, depth, early, lead),
+        out_shape=pltpu.VMEM((4, 2 * depth, late, width), jnp.float32),
+        in_specs=[vmem] * 6,
         out_specs=vmem,
         compiler_params=params,
         cost_estimate=cost(depth * late * width),
         name="look",
-    )(entries, arrived[0])
+    )(entries, scaled, inner, outer, known, arrived[0])
     for index, (top, size) in enumerate(pieces):
         labels = arrived[1 + index * len(others) : 1 + (index + 1) * len(others)]
         labels = [labels[others.index(slot)] for slot in sorted(others)]
         shading = outer if top + size == rows else inner
-        operands = [entries, flips, scaled, shading, known, found, *labels, image]
+        operands = [entries, flips, scaled, shading, found, *labels, image]
         image = pl.pallas_call(
             functools.partial(blend_kernel, count, depth, top, early, lead),
             out_shape=image_shape,

time: 54 us -> 53.8 us (level)
  no operation moved by 1% of the time
where the time goes in v7:
time: 53.8 us; the launch traced here: 53.5 us
  starting transfers between devices  20 us (37%)
  waiting for transfers between devices  18.4 us (34%)
  Pallas kernels  14.9 us (28%)
    ppermute x12, starting transfers between devices, partner(): lax.ppermute(x, axis, [(i, i ^ distance) for i in range(lax.axis_size(axi...  14.8 us
    ppermute x12, waiting for transfers between devices, partner(): lax.ppermute(x, axis, [(i, i ^ distance) for i in range(lax.axis_size(axi...  14.1 us
    ppermute x1, waiting for transfers between devices, shards(): below = lax.ppermute(first, 'sy', backward)  4.21 us
    pallas_call x1, Pallas kernels, shards(): pl.pallas_call(functools.partial(inner_kernel, count, depth), out_shape=(...  4.07 us
    ppermute x1, starting transfers between devices, shards(): above = lax.ppermute(last, 'sy', forward)  3.93 us
    pallas_call x1, Pallas kernels, shards(): pl.pallas_call(functools.partial(pack_kernel, count, depth, early, later)...  2.63 us
    pallas_call x1, Pallas kernels, shards(): pl.pallas_call(functools.partial(outer_kernel, count, depth), out_shape=(...  2.37 us
    pallas_call x2, Pallas kernels, shards(): pl.pallas_call(functools.partial(blend_kernel, count, depth, top, early,...  2.19 us
  transfers between devices with their start and end apart: 14, of which 8 were waited for; matrix products, arithmetic and copies ran while one was open for 0% of the time, Pallas kernels for 24%

profile of v7, /device:TPU:0, one launch (start us, length us, event | category | flops | bytes accessed | tf_op | source)
XLA Modules:
  0.0 53.5 jit_solution(1792140724689839326)
XLA Ops:
  0.0 1.1 %lead.1 = f32[2,32,2048]{2,1,0:T(8,128)S(1)} custom-call(f32[2,128,2048]{2,1,0:T(8,128)} %field.8), custom_call_target="tpu_custom_call" | custom-call | flops 2621440 | bytes 1048576 | tf_op jit(solution)/shard_map/lead/pallas_call | solution.py:479
  1.1 4.0 %collective-permute-start.4 = (f32[2,32,2048]{2,1,0:T(8,128)S(1)}, f32[2,32,2048]{2,1,0:T(8,128)S(1)}, u32[]{:S(2)}, u32[]{:S(2)}) collective-permute-start(f32[2,32,2048]{2,1,0:T(8,128)S(1)} %lead.1), channel_id=1, source_target_pairs={{0,3},{1,2},{2,1},{3,0},{4,7},{5,6},{6,5},{7,4},{8,11},{9,10},{10,... | collective-permute-start | bytes 1572872 | tf_op jit(solution)/shard_map/ppermute | solution.py:28
  5.0 1.4 %split.1 = (f32[2,32,2048]{2,1,0:T(8,128)S(1)}, f32[2,32,2048]{2,1,0:T(8,128)S(1)}, f32[2,2048]{1,0:T(2,128)S(1)}, f32[2,2048]{1,0:T(2,128)S(1)}) custom-call(f32[2,128,2048]{2,1,0:T(8,128)} %field.8), custom_call_target="tpu_custom_call" | custom-call | flops 10485760 | bytes 4194304 | tf_op jit(solution)/shard_map/split/pallas_call | solution.py:491
  6.4 0.6 %collective-permute-start.2 = (f32[2,32,2048]{2,1,0:T(8,128)S(1)}, f32[2,32,2048]{2,1,0:T(8,128)S(1)}, u32[]{:S(2)}, u32[]{:S(2)}) collective-permute-start(f32[2,32,2048]{2,1,0:T(8,128)S(1)} %get-tuple-element.43), channel_id=1, source_target_pairs={{0,1},{1,0},{2,3},{3,2},{4,5},{5,4},{6,7},{7,6},{8,9},{9,8},{10,11... | collective-permute-start | bytes 1572872 | tf_op jit(solution)/shard_map/ppermute | solution.py:28
  7.1 3.9 %collective-permute-start = (f32[2,2048]{1,0:T(2,128)S(1)}, f32[2,2048]{1,0:T(2,128)S(1)}, u32[]{:S(2)}, u32[]{:S(2)}) collective-permute-start(f32[2,2048]{1,0:T(2,128)S(1)} %get-tuple-element.38), channel_id=1, source_target_pairs={{0,4},{4,8},{8,12},{1,5},{5,9},{9,13},{2,6},{6,10},{10,14},{3,7},{... | collective-permute-start | bytes 49160 | tf_op jit(solution)/shard_map/ppermute | solution.py:507
  11.0 1.3 %collective-permute-start.1 = (f32[2,2048]{1,0:T(2,128)S(1)}, f32[2,2048]{1,0:T(2,128)S(1)}, u32[]{:S(2)}, u32[]{:S(2)}) collective-permute-start(f32[2,2048]{1,0:T(2,128)S(1)} %get-tuple-element.39), channel_id=1, source_target_pairs={{4,0},{8,4},{12,8},{5,1},{9,5},{13,9},{6,2},{10,6},{14,10},{7,3},{... | collective-permute-start | bytes 49160 | tf_op jit(solution)/shard_map/ppermute | solution.py:508
  12.4 4.2 %collective-permute-done.1.below = f32[2,2048]{1,0:T(2,128)S(1)} collective-permute-done((f32[2,2048]{1,0:T(2,128)S(1)}, f32[2,2048]{1,0:T(2,128)S(1)}, u32[]{:S(2)}, u32[]{:S(2)}) %collective-permute-start.1) | collective-permute-done | bytes 16416 | tf_op jit(solution)/shard_map/ppermute | solution.py:508
  16.7 2.6 %pack.1 = (f32[72,1024]{1,0:T(8,128)S(1)}, f32[72,1024]{1,0:T(8,128)S(1)}, f32[72,1024]{1,0:T(8,128)S(1)}, f32[8,1024]{1,0:T(8,128)S(1)}, s32[2,8,128]{2,1,0:T(8...) custom-call(f32[2,2048]{1,0:T(2,128)S(1)} %collective-permute-done.a, ...), custom_call_target="tpu_custom_call" | custom-call | flops 10485760 | bytes 4194304 | tf_op jit(solution)/shard_map/pack/pallas_call | solution.py:521
  19.3 2.5 %collective-permute-start.8 = (f32[72,1024]{1,0:T(8,128)S(1)}, f32[72,1024]{1,0:T(8,128)S(1)}, u32[]{:S(2)}, u32[]{:S(2)}) collective-permute-start(f32[72,1024]{1,0:T(8,128)S(1)} %get-tuple-element.55), channel_id=1, source_target_pairs={{0,3},{1,2},{2,1},{3,0},{4,7},{5,6},{6,5},{7,4},{8,11},{9,10},{10,... | collective-permute-start | bytes 884744 | tf_op jit(solution)/shard_map/ppermute | solution.py:28
  22.9 6.8 %collective-permute-done.2.refs_0_ = f32[2,32,2048]{2,1,0:T(8,128)S(1)} collective-permute-done((f32[2,32,2048]{2,1,0:T(8,128)S(1)}, f32[2,32,2048]{2,1,0:T(8,128)S(1)}, u32[]{:S(2)}, u32[]{:S(2)}) %collective-permute-start.2) | collective-permute-done | bytes 524320 | tf_op jit(solution)/shard_map/ppermute | solution.py:28
  29.7 0.8 %side.1 = f32[8,32,128]{2,1,0:T(8,128)S(1)} custom-call(f32[2,128,2048]{2,1,0:T(8,128)} %field.8, f32[2,32,2048]{2,1,0:T(8,128)S(1)} %collective-permute-done.2.refs_0_, f32[2,32,2048]{2,1,0:T(8,128)S(1)} %collective-permute-done.3.refs_1_, f32[2,32,2048]{2,1,0:T(8,128)S(1)} %collective-permute-done.4.refs_2_), custom_call_target="tpu_custom_call" | custom-call | flops 655360 | bytes 262144 | tf_op jit(solution)/shard_map/side/pallas_call | solution.py:549
  30.5 1.3 %collective-permute-done.5.beside = f32[8,32,128]{2,1,0:T(8,128)S(1)} collective-permute-done((f32[8,32,128]{2,1,0:T(8,128)S(1)}, f32[8,32,128]{2,1,0:T(8,128)S(1)}, u32[]{:S(2)}, u32[]{:S(2)}) %collective-permute-start.5) | collective-permute-done | bytes 131104 | tf_op jit(solution)/shard_map/ppermute | solution.py:28
  31.8 4.1 %inner.1 = (f32[10,48,2304]{2,1,0:T(8,128)S(1)}, f32[8,32,2048]{2,1,0:T(8,128)S(1)}, f32[8,16,2048]{2,1,0:T(8,128)S(1)}, s32[2,2,32,2048]{3,2,1,0:T(8,128)S(1)}, f32[8,128]{1,0:T(8,128)}) custom-call(f32[2,128,2048]{2,1,0:T(8,128)} %field.8, f32[8,1024]{1,0:T(8,128)S(1)} %get-tuple-element.42.edges, f32[8,32,128]{2,1,0:T(8,128)S(1)} %collective-permute-done.5.beside, ...), custom_call_target="tpu_custom_call" | custom-call | flops 10485760 | bytes 4194304 | tf_op jit(solution)/shard_map/inner/pallas_call | solution.py:561
  35.9 2.5 %collective-permute-start.9 = (s32[2,16,2048]{2,1,0:T(8,128)S(1)}, s32[2,16,2048]{2,1,0:T(8,128)S(1)}, u32[]{:S(2)}, u32[]{:S(2)}) collective-permute-start(s32[2,16,2048]{2,1,0:T(8,128)S(1)} %get-tuple-element.59), channel_id=1, source_target_pairs={{0,3},{1,2},{2,1},{3,0},{4,7},{5,6},{6,5},{7,4},{8,11},{9,10},{10,... | collective-permute-start | bytes 786440 | tf_op jit(solution)/shard_map/ppermute | solution.py:28
  38.4 3.1 %collective-permute-done.7.refs_1_ = f32[72,1024]{1,0:T(8,128)S(1)} collective-permute-done((f32[72,1024]{1,0:T(8,128)S(1)}, f32[72,1024]{1,0:T(8,128)S(1)}, u32[]{:S(2)}, u32[]{:S(2)}) %collective-permute-start.7) | collective-permute-done | bytes 294944 | tf_op jit(solution)/shard_map/ppermute | solution.py:28
  41.6 0.7 %collective-permute-done.6.refs_0_ = f32[72,1024]{1,0:T(8,128)S(1)} collective-permute-done((f32[72,1024]{1,0:T(8,128)S(1)}, f32[72,1024]{1,0:T(8,128)S(1)}, u32[]{:S(2)}, u32[]{:S(2)}) %collective-permute-start.6) | collective-permute-done | bytes 294944 | tf_op jit(solution)/shard_map/ppermute | solution.py:28
  42.3 1.5 %collective-permute-start.12 = (s32[2,8,2048]{2,1,0:T(8,128)S(1)}, s32[2,8,2048]{2,1,0:T(8,128)S(1)}, u32[]{:S(2)}, u32[]{:S(2)}) collective-permute-start(s32[2,8,2048]{2,1,0:T(8,128)S(1)} %get-tuple-element.65), channel_id=1, source_target_pairs={{0,1},{1,0},{2,3},{3,2},{4,5},{5,4},{6,7},{7,6},{8,9},{9,8},{10,11... | collective-permute-start | bytes 393224 | tf_op jit(solution)/shard_map/ppermute | solution.py:28
  43.8 1.3 %collective-permute-start.13 = (s32[2,8,2048]{2,1,0:T(8,128)S(1)}, s32[2,8,2048]{2,1,0:T(8,128)S(1)}, u32[]{:S(2)}, u32[]{:S(2)}) collective-permute-start(s32[2,8,2048]{2,1,0:T(8,128)S(1)} %get-tuple-element.67), channel_id=1, source_target_pairs={{0,2},{1,3},{2,0},{3,1},{4,6},{5,7},{6,4},{7,5},{8,10},{9,11},{10,... | collective-permute-start | bytes 393224 | tf_op jit(solution)/shard_map/ppermute | solution.py:28
  45.6 0.7 %collective-permute-start.11 = (s32[2,8,2048]{2,1,0:T(8,128)S(1)}, s32[2,8,2048]{2,1,0:T(8,128)S(1)}, u32[]{:S(2)}, u32[]{:S(2)}) collective-permute-start(s32[2,8,2048]{2,1,0:T(8,128)S(1)} %get-tuple-element.63), channel_id=1, source_target_pairs={{0,2},{1,3},{2,0},{3,1},{4,6},{5,7},{6,4},{7,5},{8,10},{9,11},{10,... | collective-permute-start | bytes 393224 | tf_op jit(solution)/shard_map/ppermute | solution.py:28
  46.4 2.4 %outer.1 = (f32[8,16,2048]{2,1,0:T(8,128)S(1)}, f32[4,32,2048]{2,1,0:T(8,128)}) custom-call(s32[2,8,128]{2,1,0:T(8,128)S(1)} %get-tuple-element.40.entries, s32[32,128]{1,0:T(8,128)S(1)} %get-tuple-element.41.flips, f32[10,48,2304]{2,1,0:T(8,128)S(1)} %get-tuple-element.47.ext, f32[8,32,2048]{2,1,0:T(8,128)S(1)} %get-tuple-element.46.scaled, ...), custom_call_target="tpu_custom_call" | custom-call | flops 10485760 | bytes 4194304 | tf_op jit(solution)/shard_map/outer/pallas_call | solution.py:580
  49.2 1.6 %collective-permute-done.12.refs_0_ = s32[2,8,2048]{2,1,0:T(8,128)S(1)} collective-permute-done((s32[2,8,2048]{2,1,0:T(8,128)S(1)}, s32[2,8,2048]{2,1,0:T(8,128)S(1)}, u32[]{:S(2)}, u32[]{:S(2)}) %collective-permute-start.12) | collective-permute-done | bytes 131104 | tf_op jit(solution)/shard_map/ppermute | solution.py:28
  50.8 1.1 %blend.2.refs_2_ = f32[4,32,2048]{2,1,0:T(8,128)} custom-call(s32[2,8,128]{2,1,0:T(8,128)S(1)} %get-tuple-element.40.entries, s32[32,128]{1,0:T(8,128)S(1)} %get-tuple-element.41.flips, f32[8,32,2048]{2,1,0:T(8,128)S(1)} %get-tuple-element.46.scaled, f32[8,16,2048]{2,1,0:T(8,128)S(1)} %get-tuple-element.48.inner.shading, ...), custom_call_target="tpu_custom_call", output_to_operand_aliasing={{}: (7, {})} | custom-call | flops 2621440 | bytes 1048576 | tf_op jit(solution)/shard_map/blend/pallas_call | solution.py:611
  51.9 0.6 %collective-permute-done.10.refs_0_ = s32[2,8,2048]{2,1,0:T(8,128)S(1)} collective-permute-done((s32[2,8,2048]{2,1,0:T(8,128)S(1)}, s32[2,8,2048]{2,1,0:T(8,128)S(1)}, u32[]{:S(2)}, u32[]{:S(2)}) %collective-permute-start.10) | collective-permute-done | bytes 131104 | tf_op jit(solution)/shard_map/ppermute | solution.py:28
  52.4 1.1 %blend.3 = f32[4,32,2048]{2,1,0:T(8,128)} custom-call(s32[2,8,128]{2,1,0:T(8,128)S(1)} %get-tuple-element.40.entries, s32[32,128]{1,0:T(8,128)S(1)} %get-tuple-element.41.flips, f32[8,32,2048]{2,1,0:T(8,128)S(1)} %get-tuple-element.46.scaled, f32[8,16,2048]{2,1,0:T(8,128)S(1)} %get-tuple-element.56.outer.shading, ...), custom_call_target="tpu_custom_call", output_to_operand_aliasing={{}: (7, {})} | custom-call | flops 2621440 | bytes 1048576 | tf_op jit(solution)/shard_map/blend/pallas_call | solution.py:611
  (18 shorter events, 2.3 us)
Async XLA Ops:
  0.0 12.3 %copy-start.1 = (bf16[4,128]{1,0:T(4,128)(2,1)S(1)}, bf16[4,128]{1,0:T(4,128)(2,1)}, u32[]{:S(2)}) copy-start(bf16[4,128]{1,0:T(4,128)(2,1)} %param.6) | copy-start | bytes 3076
  0.0 16.7 %copy-start = (s32[128]{0:T(128)S(1)}, s32[128]{0:T(128)}, u32[]{:S(2)}) copy-start(s32[128]{0:T(128)} %march.1) | copy-start | bytes 1540
  1.1 18.2 %collective-permute-start.4 = (f32[2,32,2048]{2,1,0:T(8,128)S(1)}, f32[2,32,2048]{2,1,0:T(8,128)S(1)}, u32[]{:S(2)}, u32[]{:S(2)}) collective-permute-start(f32[2,32,2048]{2,1,0:T(8,128)S(1)} %lead.1), channel_id=1, source_target_pairs={{0,3},{1,2},{2,1},{3,0},{4,7},{5,6},{6,5},{7,4},{8,11},{9,10},{10,... | collective-permute-start | bytes 1572872 | tf_op jit(solution)/shard_map/ppermute | solution.py:28
  6.4 23.2 %collective-permute-start.2 = (f32[2,32,2048]{2,1,0:T(8,128)S(1)}, f32[2,32,2048]{2,1,0:T(8,128)S(1)}, u32[]{:S(2)}, u32[]{:S(2)}) collective-permute-start(f32[2,32,2048]{2,1,0:T(8,128)S(1)} %get-tuple-element.43), channel_id=1, source_target_pairs={{0,1},{1,0},{2,3},{3,2},{4,5},{5,4},{6,7},{7,6},{8,9},{9,8},{10,11... | collective-permute-start | bytes 1572872 | tf_op jit(solution)/shard_map/ppermute | solution.py:28
  7.0 22.6 %collective-permute-start.3 = (f32[2,32,2048]{2,1,0:T(8,128)S(1)}, f32[2,32,2048]{2,1,0:T(8,128)S(1)}, u32[]{:S(2)}, u32[]{:S(2)}) collective-permute-start(f32[2,32,2048]{2,1,0:T(8,128)S(1)} %get-tuple-element.44), channel_id=1, source_target_pairs={{0,2},{1,3},{2,0},{3,1},{4,6},{5,7},{6,4},{7,5},{8,10},{9,11},{10,... | collective-permute-start | bytes 1572872 | tf_op jit(solution)/shard_map/ppermute | solution.py:28
  7.1 5.4 %collective-permute-start = (f32[2,2048]{1,0:T(2,128)S(1)}, f32[2,2048]{1,0:T(2,128)S(1)}, u32[]{:S(2)}, u32[]{:S(2)}) collective-permute-start(f32[2,2048]{1,0:T(2,128)S(1)} %get-tuple-element.38), channel_id=1, source_target_pairs={{0,4},{4,8},{8,12},{1,5},{5,9},{9,13},{2,6},{6,10},{10,14},{3,7},{... | collective-permute-start | bytes 49160 | tf_op jit(solution)/shard_map/ppermute | solution.py:507
  11.0 5.6 %collective-permute-start.1 = (f32[2,2048]{1,0:T(2,128)S(1)}, f32[2,2048]{1,0:T(2,128)S(1)}, u32[]{:S(2)}, u32[]{:S(2)}) collective-permute-start(f32[2,2048]{1,0:T(2,128)S(1)} %get-tuple-element.39), channel_id=1, source_target_pairs={{4,0},{8,4},{12,8},{5,1},{9,5},{13,9},{6,2},{10,6},{14,10},{7,3},{... | collective-permute-start | bytes 49160 | tf_op jit(solution)/shard_map/ppermute | solution.py:508
  19.3 16.6 %collective-permute-start.8 = (f32[72,1024]{1,0:T(8,128)S(1)}, f32[72,1024]{1,0:T(8,128)S(1)}, u32[]{:S(2)}, u32[]{:S(2)}) collective-permute-start(f32[72,1024]{1,0:T(8,128)S(1)} %get-tuple-element.55), channel_id=1, source_target_pairs={{0,3},{1,2},{2,1},{3,0},{4,7},{5,6},{6,5},{7,4},{8,11},{9,10},{10,... | collective-permute-start | bytes 884744 | tf_op jit(solution)/shard_map/ppermute | solution.py:28
  21.8 19.8 %collective-permute-start.7 = (f32[72,1024]{1,0:T(8,128)S(1)}, f32[72,1024]{1,0:T(8,128)S(1)}, u32[]{:S(2)}, u32[]{:S(2)}) collective-permute-start(f32[72,1024]{1,0:T(8,128)S(1)} %get-tuple-element.53), channel_id=1, source_target_pairs={{0,2},{1,3},{2,0},{3,1},{4,6},{5,7},{6,4},{7,5},{8,10},{9,11},{10,... | collective-permute-start | bytes 884744 | tf_op jit(solution)/shard_map/ppermute | solution.py:28
  22.3 20.0 %collective-permute-start.6 = (f32[72,1024]{1,0:T(8,128)S(1)}, f32[72,1024]{1,0:T(8,128)S(1)}, u32[]{:S(2)}, u32[]{:S(2)}) collective-permute-start(f32[72,1024]{1,0:T(8,128)S(1)} %get-tuple-element.51), channel_id=1, source_target_pairs={{0,1},{1,0},{2,3},{3,2},{4,5},{5,4},{6,7},{7,6},{8,9},{9,8},{10,11... | collective-permute-start | bytes 884744 | tf_op jit(solution)/shard_map/ppermute | solution.py:28
  30.4 1.4 %collective-permute-start.5 = (f32[8,32,128]{2,1,0:T(8,128)S(1)}, f32[8,32,128]{2,1,0:T(8,128)S(1)}, u32[]{:S(2)}, u32[]{:S(2)}) collective-permute-start(f32[8,32,128]{2,1,0:T(8,128)S(1)} %side.1), channel_id=1, source_target_pairs={{0,16},{16,0},{1,17},{17,1},{2,18},{18,2},{3,19},{19,3},{4,20},{20... | collective-permute-start | bytes 393224 | tf_op jit(solution)/shard_map/ppermute | solution.py:28
  35.9 12.8 %collective-permute-start.9 = (s32[2,16,2048]{2,1,0:T(8,128)S(1)}, s32[2,16,2048]{2,1,0:T(8,128)S(1)}, u32[]{:S(2)}, u32[]{:S(2)}) collective-permute-start(s32[2,16,2048]{2,1,0:T(8,128)S(1)} %get-tuple-element.59), channel_id=1, source_target_pairs={{0,3},{1,2},{2,1},{3,0},{4,7},{5,6},{6,5},{7,4},{8,11},{9,10},{10,... | collective-permute-start | bytes 786440 | tf_op jit(solution)/shard_map/ppermute | solution.py:28
  42.3 8.4 %collective-permute-start.12 = (s32[2,8,2048]{2,1,0:T(8,128)S(1)}, s32[2,8,2048]{2,1,0:T(8,128)S(1)}, u32[]{:S(2)}, u32[]{:S(2)}) collective-permute-start(s32[2,8,2048]{2,1,0:T(8,128)S(1)} %get-tuple-element.65), channel_id=1, source_target_pairs={{0,1},{1,0},{2,3},{3,2},{4,5},{5,4},{6,7},{7,6},{8,9},{9,8},{10,11... | collective-permute-start | bytes 393224 | tf_op jit(solution)/shard_map/ppermute | solution.py:28
  43.8 6.9 %collective-permute-start.13 = (s32[2,8,2048]{2,1,0:T(8,128)S(1)}, s32[2,8,2048]{2,1,0:T(8,128)S(1)}, u32[]{:S(2)}, u32[]{:S(2)}) collective-permute-start(s32[2,8,2048]{2,1,0:T(8,128)S(1)} %get-tuple-element.67), channel_id=1, source_target_pairs={{0,2},{1,3},{2,0},{3,1},{4,6},{5,7},{6,4},{7,5},{8,10},{9,11},{10,... | collective-permute-start | bytes 393224 | tf_op jit(solution)/shard_map/ppermute | solution.py:28
  45.1 7.3 %collective-permute-start.10 = (s32[2,8,2048]{2,1,0:T(8,128)S(1)}, s32[2,8,2048]{2,1,0:T(8,128)S(1)}, u32[]{:S(2)}, u32[]{:S(2)}) collective-permute-start(s32[2,8,2048]{2,1,0:T(8,128)S(1)} %get-tuple-element.61), channel_id=1, source_target_pairs={{0,1},{1,0},{2,3},{3,2},{4,5},{5,4},{6,7},{7,6},{8,9},{9,8},{10,11... | collective-permute-start | bytes 393224 | tf_op jit(solution)/shard_map/ppermute | solution.py:28
  45.6 6.8 %collective-permute-start.11 = (s32[2,8,2048]{2,1,0:T(8,128)S(1)}, s32[2,8,2048]{2,1,0:T(8,128)S(1)}, u32[]{:S(2)}, u32[]{:S(2)}) collective-permute-start(s32[2,8,2048]{2,1,0:T(8,128)S(1)} %get-tuple-element.63), channel_id=1, source_target_pairs={{0,2},{1,3},{2,0},{3,1},{4,6},{5,7},{6,4},{7,5},{8,10},{9,11},{10,... | collective-permute-start | bytes 393224 | tf_op jit(solution)/shard_map/ppermute | solution.py:28

commit v8 on v7

--- a/solution.py
+++ b/solution.py
@@ -467,7 +467,10 @@
         return pl.CostEstimate(flops=20 * cells, bytes_accessed=8 * cells, transcendentals=cells)
 
     done = {}
-    order = {"message": lambda index: [("field", 0)], "bins": lambda index: [("message", index), "inner"]}
+    order = {
+        "message": lambda index: [("field", 0)],
+        "bins": lambda index: [("message", index), "inner"] if index else [("message", 0), "beside"],
+    }
 
     def send(name, array, slot):
         index = partners.index(slot)
@@ -557,6 +560,7 @@
         name="side",
     )(in_hbm(field), *[bricks[slot] for slot in slots[1:]])
     beside = partner(slab, "sx", 1)
+    done["beside"] = beside
 
     ext, scaled, inner, known, token = pl.pallas_call(
         functools.partial(inner_kernel, count, depth),

time: 53.8 us -> 53.8 us (level)
  transfers between devices with their start and end apart: 14 -> 14, of which waited for: 8 -> 7; matrix products, arithmetic and copies ran while one was open for 0% -> 0% of each run, Pallas kernels for 24% -> 24%
where the time goes in v8:
time: 53.8 us; the launch traced here: 53.5 us
  starting transfers between devices  20.5 us (38%)
  waiting for transfers between devices  17.9 us (33%)
  Pallas kernels  14.9 us (28%)
    ppermute x12, starting transfers between devices, partner(): lax.ppermute(x, axis, [(i, i ^ distance) for i in range(lax.axis_size(axi...  15.3 us
    ppermute x12, waiting for transfers between devices, partner(): lax.ppermute(x, axis, [(i, i ^ distance) for i in range(lax.axis_size(axi...  13.6 us
    ppermute x1, waiting for transfers between devices, shards(): below = lax.ppermute(first, 'sy', backward)  4.21 us
    pallas_call x1, Pallas kernels, shards(): pl.pallas_call(functools.partial(inner_kernel, count, depth), out_shape=(...  4.07 us
    ppermute x1, starting transfers between devices, shards(): above = lax.ppermute(last, 'sy', forward)  3.93 us
    pallas_call x1, Pallas kernels, shards(): pl.pallas_call(functools.partial(pack_kernel, count, depth, early, later)...  2.63 us
    pallas_call x1, Pallas kernels, shards(): pl.pallas_call(functools.partial(outer_kernel, count, depth), out_shape=(...  2.37 us
    pallas_call x2, Pallas kernels, shards(): pl.pallas_call(functools.partial(blend_kernel, count, depth, top, early,...  2.2 us
  transfers between devices with their start and end apart: 14, of which 7 were waited for; matrix products, arithmetic and copies ran while one was open for 0% of the time, Pallas kernels for 24%

profile of v8, /device:TPU:0, one launch (start us, length us, event | category | flops | bytes accessed | tf_op | source)
XLA Modules:
  0.0 53.5 jit_solution(10883041400507704700)
XLA Ops:
  0.0 1.1 %lead.1 = f32[2,32,2048]{2,1,0:T(8,128)S(1)} custom-call(f32[2,128,2048]{2,1,0:T(8,128)} %field.8), custom_call_target="tpu_custom_call" | custom-call | flops 2621440 | bytes 1048576 | tf_op jit(solution)/shard_map/lead/pallas_call | solution.py:482
  1.1 4.0 %collective-permute-start.4 = (f32[2,32,2048]{2,1,0:T(8,128)S(1)}, f32[2,32,2048]{2,1,0:T(8,128)S(1)}, u32[]{:S(2)}, u32[]{:S(2)}) collective-permute-start(f32[2,32,2048]{2,1,0:T(8,128)S(1)} %lead.1), channel_id=1, source_target_pairs={{0,3},{1,2},{2,1},{3,0},{4,7},{5,6},{6,5},{7,4},{8,11},{9,10},{10,... | collective-permute-start | bytes 1572872 | tf_op jit(solution)/shard_map/ppermute | solution.py:28
  5.0 1.4 %split.1 = (f32[2,32,2048]{2,1,0:T(8,128)S(1)}, f32[2,32,2048]{2,1,0:T(8,128)S(1)}, f32[2,2048]{1,0:T(2,128)S(1)}, f32[2,2048]{1,0:T(2,128)S(1)}) custom-call(f32[2,128,2048]{2,1,0:T(8,128)} %field.8), custom_call_target="tpu_custom_call" | custom-call | flops 10485760 | bytes 4194304 | tf_op jit(solution)/shard_map/split/pallas_call | solution.py:494
  6.4 0.6 %collective-permute-start.2 = (f32[2,32,2048]{2,1,0:T(8,128)S(1)}, f32[2,32,2048]{2,1,0:T(8,128)S(1)}, u32[]{:S(2)}, u32[]{:S(2)}) collective-permute-start(f32[2,32,2048]{2,1,0:T(8,128)S(1)} %get-tuple-element.43), channel_id=1, source_target_pairs={{0,1},{1,0},{2,3},{3,2},{4,5},{5,4},{6,7},{7,6},{8,9},{9,8},{10,11... | collective-permute-start | bytes 1572872 | tf_op jit(solution)/shard_map/ppermute | solution.py:28
  7.1 3.9 %collective-permute-start = (f32[2,2048]{1,0:T(2,128)S(1)}, f32[2,2048]{1,0:T(2,128)S(1)}, u32[]{:S(2)}, u32[]{:S(2)}) collective-permute-start(f32[2,2048]{1,0:T(2,128)S(1)} %get-tuple-element.38), channel_id=1, source_target_pairs={{0,4},{4,8},{8,12},{1,5},{5,9},{9,13},{2,6},{6,10},{10,14},{3,7},{... | collective-permute-start | bytes 49160 | tf_op jit(solution)/shard_map/ppermute | solution.py:510
  11.0 1.3 %collective-permute-start.1 = (f32[2,2048]{1,0:T(2,128)S(1)}, f32[2,2048]{1,0:T(2,128)S(1)}, u32[]{:S(2)}, u32[]{:S(2)}) collective-permute-start(f32[2,2048]{1,0:T(2,128)S(1)} %get-tuple-element.39), channel_id=1, source_target_pairs={{4,0},{8,4},{12,8},{5,1},{9,5},{13,9},{6,2},{10,6},{14,10},{7,3},{... | collective-permute-start | bytes 49160 | tf_op jit(solution)/shard_map/ppermute | solution.py:511
  12.4 4.2 %collective-permute-done.1.below = f32[2,2048]{1,0:T(2,128)S(1)} collective-permute-done((f32[2,2048]{1,0:T(2,128)S(1)}, f32[2,2048]{1,0:T(2,128)S(1)}, u32[]{:S(2)}, u32[]{:S(2)}) %collective-permute-start.1) | collective-permute-done | bytes 16416 | tf_op jit(solution)/shard_map/ppermute | solution.py:511
  16.7 2.6 %pack.1 = (f32[72,1024]{1,0:T(8,128)S(1)}, f32[72,1024]{1,0:T(8,128)S(1)}, f32[72,1024]{1,0:T(8,128)S(1)}, f32[8,1024]{1,0:T(8,128)S(1)}, s32[2,8,128]{2,1,0:T(8...) custom-call(f32[2,2048]{1,0:T(2,128)S(1)} %collective-permute-done.a, ...), custom_call_target="tpu_custom_call" | custom-call | flops 10485760 | bytes 4194304 | tf_op jit(solution)/shard_map/pack/pallas_call | solution.py:524
  19.3 2.5 %collective-permute-start.8 = (f32[72,1024]{1,0:T(8,128)S(1)}, f32[72,1024]{1,0:T(8,128)S(1)}, u32[]{:S(2)}, u32[]{:S(2)}) collective-permute-start(f32[72,1024]{1,0:T(8,128)S(1)} %get-tuple-element.55), channel_id=1, source_target_pairs={{0,3},{1,2},{2,1},{3,0},{4,7},{5,6},{6,5},{7,4},{8,11},{9,10},{10,... | collective-permute-start | bytes 884744 | tf_op jit(solution)/shard_map/ppermute | solution.py:28
  22.3 0.5 %collective-permute-start.6 = (f32[72,1024]{1,0:T(8,128)S(1)}, f32[72,1024]{1,0:T(8,128)S(1)}, u32[]{:S(2)}, u32[]{:S(2)}) collective-permute-start(f32[72,1024]{1,0:T(8,128)S(1)} %get-tuple-element.51), channel_id=1, source_target_pairs={{0,1},{1,0},{2,3},{3,2},{4,5},{5,4},{6,7},{7,6},{8,9},{9,8},{10,11... | collective-permute-start | bytes 884744 | tf_op jit(solution)/shard_map/ppermute | solution.py:28
  22.9 6.8 %collective-permute-done.2.refs_0_ = f32[2,32,2048]{2,1,0:T(8,128)S(1)} collective-permute-done((f32[2,32,2048]{2,1,0:T(8,128)S(1)}, f32[2,32,2048]{2,1,0:T(8,128)S(1)}, u32[]{:S(2)}, u32[]{:S(2)}) %collective-permute-start.2) | collective-permute-done | bytes 524320 | tf_op jit(solution)/shard_map/ppermute | solution.py:28
  29.7 0.8 %side.1 = f32[8,32,128]{2,1,0:T(8,128)S(1)} custom-call(f32[2,128,2048]{2,1,0:T(8,128)} %field.8, f32[2,32,2048]{2,1,0:T(8,128)S(1)} %collective-permute-done.2.refs_0_, f32[2,32,2048]{2,1,0:T(8,128)S(1)} %collective-permute-done.3.refs_1_, f32[2,32,2048]{2,1,0:T(8,128)S(1)} %collective-permute-done.4.refs_2_), custom_call_target="tpu_custom_call" | custom-call | flops 655360 | bytes 262144 | tf_op jit(solution)/shard_map/side/pallas_call | solution.py:552
  30.5 1.3 %collective-permute-done.5.beside = f32[8,32,128]{2,1,0:T(8,128)S(1)} collective-permute-done((f32[8,32,128]{2,1,0:T(8,128)S(1)}, f32[8,32,128]{2,1,0:T(8,128)S(1)}, u32[]{:S(2)}, u32[]{:S(2)}) %collective-permute-start.5) | collective-permute-done | bytes 131104 | tf_op jit(solution)/shard_map/ppermute | solution.py:28
  31.8 3.6 %collective-permute-done.8.refs_2_ = f32[72,1024]{1,0:T(8,128)S(1)} collective-permute-done((f32[72,1024]{1,0:T(8,128)S(1)}, f32[72,1024]{1,0:T(8,128)S(1)}, u32[]{:S(2)}, u32[]{:S(2)}) %collective-permute-start.8) | collective-permute-done | bytes 294944 | tf_op jit(solution)/shard_map/ppermute | solution.py:28
  35.4 3.0 %collective-permute-start.9 = (s32[2,16,2048]{2,1,0:T(8,128)S(1)}, s32[2,16,2048]{2,1,0:T(8,128)S(1)}, u32[]{:S(2)}, u32[]{:S(2)}) collective-permute-start(s32[2,16,2048]{2,1,0:T(8,128)S(1)} %get-tuple-element.58), channel_id=1, source_target_pairs={{0,3},{1,2},{2,1},{3,0},{4,7},{5,6},{6,5},{7,4},{8,11},{9,10},{10,... | collective-permute-start | bytes 786440 | tf_op jit(solution)/shard_map/ppermute | solution.py:28
  38.4 4.1 %inner.1 = (f32[10,48,2304]{2,1,0:T(8,128)S(1)}, f32[8,32,2048]{2,1,0:T(8,128)S(1)}, f32[8,16,2048]{2,1,0:T(8,128)S(1)}, s32[2,2,32,2048]{3,2,1,0:T(8,128)S(1)}, f32[8,128]{1,0:T(8,128)}) custom-call(f32[2,128,2048]{2,1,0:T(8,128)} %field.8, f32[8,1024]{1,0:T(8,128)S(1)} %get-tuple-element.42.edges, f32[8,32,128]{2,1,0:T(8,128)S(1)} %collective-permute-done.5.beside, ...), custom_call_target="tpu_custom_call" | custom-call | flops 10485760 | bytes 4194304 | tf_op jit(solution)/shard_map/inner/pallas_call | solution.py:565
  42.5 1.3 %collective-permute-start.12 = (s32[2,8,2048]{2,1,0:T(8,128)S(1)}, s32[2,8,2048]{2,1,0:T(8,128)S(1)}, u32[]{:S(2)}, u32[]{:S(2)}) collective-permute-start(s32[2,8,2048]{2,1,0:T(8,128)S(1)} %get-tuple-element.65), channel_id=1, source_target_pairs={{0,1},{1,0},{2,3},{3,2},{4,5},{5,4},{6,7},{7,6},{8,9},{9,8},{10,11... | collective-permute-start | bytes 393224 | tf_op jit(solution)/shard_map/ppermute | solution.py:28
  43.8 1.3 %collective-permute-start.13 = (s32[2,8,2048]{2,1,0:T(8,128)S(1)}, s32[2,8,2048]{2,1,0:T(8,128)S(1)}, u32[]{:S(2)}, u32[]{:S(2)}) collective-permute-start(s32[2,8,2048]{2,1,0:T(8,128)S(1)} %get-tuple-element.67), channel_id=1, source_target_pairs={{0,2},{1,3},{2,0},{3,1},{4,6},{5,7},{6,4},{7,5},{8,10},{9,11},{10,... | collective-permute-start | bytes 393224 | tf_op jit(solution)/shard_map/ppermute | solution.py:28
  45.6 1.0 %collective-permute-start.11 = (s32[2,8,2048]{2,1,0:T(8,128)S(1)}, s32[2,8,2048]{2,1,0:T(8,128)S(1)}, u32[]{:S(2)}, u32[]{:S(2)}) collective-permute-start(s32[2,8,2048]{2,1,0:T(8,128)S(1)} %get-tuple-element.63), channel_id=1, source_target_pairs={{0,2},{1,3},{2,0},{3,1},{4,6},{5,7},{6,4},{7,5},{8,10},{9,11},{10,... | collective-permute-start | bytes 393224 | tf_op jit(solution)/shard_map/ppermute | solution.py:28
  46.6 2.4 %outer.1 = (f32[8,16,2048]{2,1,0:T(8,128)S(1)}, f32[4,32,2048]{2,1,0:T(8,128)}) custom-call(s32[2,8,128]{2,1,0:T(8,128)S(1)} %get-tuple-element.40.entries, s32[32,128]{1,0:T(8,128)S(1)} %get-tuple-element.41.flips, f32[10,48,2304]{2,1,0:T(8,128)S(1)} %get-tuple-element.47.ext, f32[8,32,2048]{2,1,0:T(8,128)S(1)} %get-tuple-element.46.scaled, ...), custom_call_target="tpu_custom_call" | custom-call | flops 10485760 | bytes 4194304 | tf_op jit(solution)/shard_map/outer/pallas_call | solution.py:584
  49.4 1.3 %collective-permute-done.12.refs_0_ = s32[2,8,2048]{2,1,0:T(8,128)S(1)} collective-permute-done((s32[2,8,2048]{2,1,0:T(8,128)S(1)}, s32[2,8,2048]{2,1,0:T(8,128)S(1)}, u32[]{:S(2)}, u32[]{:S(2)}) %collective-permute-start.12) | collective-permute-done | bytes 131104 | tf_op jit(solution)/shard_map/ppermute | solution.py:28
  50.8 1.1 %blend.2.refs_2_ = f32[4,32,2048]{2,1,0:T(8,128)} custom-call(s32[2,8,128]{2,1,0:T(8,128)S(1)} %get-tuple-element.40.entries, s32[32,128]{1,0:T(8,128)S(1)} %get-tuple-element.41.flips, f32[8,32,2048]{2,1,0:T(8,128)S(1)} %get-tuple-element.46.scaled, f32[8,16,2048]{2,1,0:T(8,128)S(1)} %get-tuple-element.48.inner.shading, ...), custom_call_target="tpu_custom_call", output_to_operand_aliasing={{}: (7, {})} | custom-call | flops 2621440 | bytes 1048576 | tf_op jit(solution)/shard_map/blend/pallas_call | solution.py:615
  51.9 0.6 %collective-permute-done.10.refs_0_ = s32[2,8,2048]{2,1,0:T(8,128)S(1)} collective-permute-done((s32[2,8,2048]{2,1,0:T(8,128)S(1)}, s32[2,8,2048]{2,1,0:T(8,128)S(1)}, u32[]{:S(2)}, u32[]{:S(2)}) %collective-permute-start.10) | collective-permute-done | bytes 131104 | tf_op jit(solution)/shard_map/ppermute | solution.py:28
  52.4 1.1 %blend.3 = f32[4,32,2048]{2,1,0:T(8,128)} custom-call(s32[2,8,128]{2,1,0:T(8,128)S(1)} %get-tuple-element.40.entries, s32[32,128]{1,0:T(8,128)S(1)} %get-tuple-element.41.flips, f32[8,32,2048]{2,1,0:T(8,128)S(1)} %get-tuple-element.46.scaled, f32[8,16,2048]{2,1,0:T(8,128)S(1)} %get-tuple-element.56.outer.shading, ...), custom_call_target="tpu_custom_call", output_to_operand_aliasing={{}: (7, {})} | custom-call | flops 2621440 | bytes 1048576 | tf_op jit(solution)/shard_map/blend/pallas_call | solution.py:615
  (18 shorter events, 1.7 us)
Async XLA Ops:
  0.0 12.3 %copy-start.1 = (bf16[4,128]{1,0:T(4,128)(2,1)S(1)}, bf16[4,128]{1,0:T(4,128)(2,1)}, u32[]{:S(2)}) copy-start(bf16[4,128]{1,0:T(4,128)(2,1)} %param.6) | copy-start | bytes 3076
  0.0 16.7 %copy-start = (s32[128]{0:T(128)S(1)}, s32[128]{0:T(128)}, u32[]{:S(2)}) copy-start(s32[128]{0:T(128)} %march.1) | copy-start | bytes 1540
  1.1 18.2 %collective-permute-start.4 = (f32[2,32,2048]{2,1,0:T(8,128)S(1)}, f32[2,32,2048]{2,1,0:T(8,128)S(1)}, u32[]{:S(2)}, u32[]{:S(2)}) collective-permute-start(f32[2,32,2048]{2,1,0:T(8,128)S(1)} %lead.1), channel_id=1, source_target_pairs={{0,3},{1,2},{2,1},{3,0},{4,7},{5,6},{6,5},{7,4},{8,11},{9,10},{10,... | collective-permute-start | bytes 1572872 | tf_op jit(solution)/shard_map/ppermute | solution.py:28
  6.4 23.2 %collective-permute-start.2 = (f32[2,32,2048]{2,1,0:T(8,128)S(1)}, f32[2,32,2048]{2,1,0:T(8,128)S(1)}, u32[]{:S(2)}, u32[]{:S(2)}) collective-permute-start(f32[2,32,2048]{2,1,0:T(8,128)S(1)} %get-tuple-element.43), channel_id=1, source_target_pairs={{0,1},{1,0},{2,3},{3,2},{4,5},{5,4},{6,7},{7,6},{8,9},{9,8},{10,11... | collective-permute-start | bytes 1572872 | tf_op jit(solution)/shard_map/ppermute | solution.py:28
  7.0 22.6 %collective-permute-start.3 = (f32[2,32,2048]{2,1,0:T(8,128)S(1)}, f32[2,32,2048]{2,1,0:T(8,128)S(1)}, u32[]{:S(2)}, u32[]{:S(2)}) collective-permute-start(f32[2,32,2048]{2,1,0:T(8,128)S(1)} %get-tuple-element.44), channel_id=1, source_target_pairs={{0,2},{1,3},{2,0},{3,1},{4,6},{5,7},{6,4},{7,5},{8,10},{9,11},{10,... | collective-permute-start | bytes 1572872 | tf_op jit(solution)/shard_map/ppermute | solution.py:28
  7.1 5.4 %collective-permute-start = (f32[2,2048]{1,0:T(2,128)S(1)}, f32[2,2048]{1,0:T(2,128)S(1)}, u32[]{:S(2)}, u32[]{:S(2)}) collective-permute-start(f32[2,2048]{1,0:T(2,128)S(1)} %get-tuple-element.38), channel_id=1, source_target_pairs={{0,4},{4,8},{8,12},{1,5},{5,9},{9,13},{2,6},{6,10},{10,14},{3,7},{... | collective-permute-start | bytes 49160 | tf_op jit(solution)/shard_map/ppermute | solution.py:510
  11.0 5.6 %collective-permute-start.1 = (f32[2,2048]{1,0:T(2,128)S(1)}, f32[2,2048]{1,0:T(2,128)S(1)}, u32[]{:S(2)}, u32[]{:S(2)}) collective-permute-start(f32[2,2048]{1,0:T(2,128)S(1)} %get-tuple-element.39), channel_id=1, source_target_pairs={{4,0},{8,4},{12,8},{5,1},{9,5},{13,9},{6,2},{10,6},{14,10},{7,3},{... | collective-permute-start | bytes 49160 | tf_op jit(solution)/shard_map/ppermute | solution.py:511
  19.3 16.1 %collective-permute-start.8 = (f32[72,1024]{1,0:T(8,128)S(1)}, f32[72,1024]{1,0:T(8,128)S(1)}, u32[]{:S(2)}, u32[]{:S(2)}) collective-permute-start(f32[72,1024]{1,0:T(8,128)S(1)} %get-tuple-element.55), channel_id=1, source_target_pairs={{0,3},{1,2},{2,1},{3,0},{4,7},{5,6},{6,5},{7,4},{8,11},{9,10},{10,... | collective-permute-start | bytes 884744 | tf_op jit(solution)/shard_map/ppermute | solution.py:28
  21.8 20.7 %collective-permute-start.7 = (f32[72,1024]{1,0:T(8,128)S(1)}, f32[72,1024]{1,0:T(8,128)S(1)}, u32[]{:S(2)}, u32[]{:S(2)}) collective-permute-start(f32[72,1024]{1,0:T(8,128)S(1)} %get-tuple-element.53), channel_id=1, source_target_pairs={{0,2},{1,3},{2,0},{3,1},{4,6},{5,7},{6,4},{7,5},{8,10},{9,11},{10,... | collective-permute-start | bytes 884744 | tf_op jit(solution)/shard_map/ppermute | solution.py:28
  22.3 20.2 %collective-permute-start.6 = (f32[72,1024]{1,0:T(8,128)S(1)}, f32[72,1024]{1,0:T(8,128)S(1)}, u32[]{:S(2)}, u32[]{:S(2)}) collective-permute-start(f32[72,1024]{1,0:T(8,128)S(1)} %get-tuple-element.51), channel_id=1, source_target_pairs={{0,1},{1,0},{2,3},{3,2},{4,5},{5,4},{6,7},{7,6},{8,9},{9,8},{10,11... | collective-permute-start | bytes 884744 | tf_op jit(solution)/shard_map/ppermute | solution.py:28
  30.4 1.4 %collective-permute-start.5 = (f32[8,32,128]{2,1,0:T(8,128)S(1)}, f32[8,32,128]{2,1,0:T(8,128)S(1)}, u32[]{:S(2)}, u32[]{:S(2)}) collective-permute-start(f32[8,32,128]{2,1,0:T(8,128)S(1)} %side.1), channel_id=1, source_target_pairs={{0,16},{16,0},{1,17},{17,1},{2,18},{18,2},{3,19},{19,3},{4,20},{20... | collective-permute-start | bytes 393224 | tf_op jit(solution)/shard_map/ppermute | solution.py:28
  35.4 13.5 %collective-permute-start.9 = (s32[2,16,2048]{2,1,0:T(8,128)S(1)}, s32[2,16,2048]{2,1,0:T(8,128)S(1)}, u32[]{:S(2)}, u32[]{:S(2)}) collective-permute-start(s32[2,16,2048]{2,1,0:T(8,128)S(1)} %get-tuple-element.58), channel_id=1, source_target_pairs={{0,3},{1,2},{2,1},{3,0},{4,7},{5,6},{6,5},{7,4},{8,11},{9,10},{10,... | collective-permute-start | bytes 786440 | tf_op jit(solution)/shard_map/ppermute | solution.py:28
  42.5 8.3 %collective-permute-start.12 = (s32[2,8,2048]{2,1,0:T(8,128)S(1)}, s32[2,8,2048]{2,1,0:T(8,128)S(1)}, u32[]{:S(2)}, u32[]{:S(2)}) collective-permute-start(s32[2,8,2048]{2,1,0:T(8,128)S(1)} %get-tuple-element.65), channel_id=1, source_target_pairs={{0,1},{1,0},{2,3},{3,2},{4,5},{5,4},{6,7},{7,6},{8,9},{9,8},{10,11... | collective-permute-start | bytes 393224 | tf_op jit(solution)/shard_map/ppermute | solution.py:28
  43.8 6.9 %collective-permute-start.13 = (s32[2,8,2048]{2,1,0:T(8,128)S(1)}, s32[2,8,2048]{2,1,0:T(8,128)S(1)}, u32[]{:S(2)}, u32[]{:S(2)}) collective-permute-start(s32[2,8,2048]{2,1,0:T(8,128)S(1)} %get-tuple-element.67), channel_id=1, source_target_pairs={{0,2},{1,3},{2,0},{3,1},{4,6},{5,7},{6,4},{7,5},{8,10},{9,11},{10,... | collective-permute-start | bytes 393224 | tf_op jit(solution)/shard_map/ppermute | solution.py:28
  45.1 7.3 %collective-permute-start.10 = (s32[2,8,2048]{2,1,0:T(8,128)S(1)}, s32[2,8,2048]{2,1,0:T(8,128)S(1)}, u32[]{:S(2)}, u32[]{:S(2)}) collective-permute-start(s32[2,8,2048]{2,1,0:T(8,128)S(1)} %get-tuple-element.61), channel_id=1, source_target_pairs={{0,1},{1,0},{2,3},{3,2},{4,5},{5,4},{6,7},{7,6},{8,9},{9,8},{10,11... | collective-permute-start | bytes 393224 | tf_op jit(solution)/shard_map/ppermute | solution.py:28
  45.6 6.8 %collective-permute-start.11 = (s32[2,8,2048]{2,1,0:T(8,128)S(1)}, s32[2,8,2048]{2,1,0:T(8,128)S(1)}, u32[]{:S(2)}, u32[]{:S(2)}) collective-permute-start(s32[2,8,2048]{2,1,0:T(8,128)S(1)} %get-tuple-element.63), channel_id=1, source_target_pairs={{0,2},{1,3},{2,0},{3,1},{4,6},{5,7},{6,4},{7,5},{8,10},{9,11},{10,... | collective-permute-start | bytes 393224 | tf_op jit(solution)/shard_map/ppermute | solution.py:28
